TPU v7x, 32 devices: a whole 2x2x4 slice. The times are simulated.
32 devices in a mesh: grp: 8 (over y, x, core), chan: 4 (over z).
Axes of the slice: x: 2, y: 2, z: 4, core: 2. Of those that a mesh axis runs over, the one named last changes fastest.
Arguments:
- spectra: bfloat16 [512, 2, 2, 8192], P(('grp', 'chan')), may hold values from -45 to 45
- pair_blocks: int32 [8, 4, 18, 2], P('grp', 'chan'), may hold values from 0 to 31
- owners: int32 [8, 4, 18, 1], P('grp', 'chan'), may hold values from 0 to 7; in each aligned block of 18 rows (0 to 17, 18 to 35, ..., all dimensions but the last counted through in order) at most 3 rows name the same one
Outputs:
- stacks: float32 [8, 4, 24, 4, 1024], P('grp', 'chan')
Inputs may be any that keep to these rules, and one draw needn't show every extreme that they name: `owners`: at most 3 of one device's 18 pair blocks name the same owner.
All inputs are finite; a program needn't handle non-finite values.
Results may differ from a plain program's by a relative error of at most 0.011.
Values may be sent and summed in bfloat16 or wider, within the bound.
No kernel may reach another device: no remote copies, remote signals or barrier semaphores. Data moves between devices by JAX's collectives and lax.ppermute only.
A program may use at most 128 MiB of HBM per device.

v0:
```python
import functools

import jax
import jax.numpy as jnp
import numpy as np
from jax import lax
from jax.experimental import pallas as pl
from jax.experimental.pallas import tpu as pltpu
from jax.sharding import PartitionSpec as P

F = 8192
LAGS = 1024
BLK = 2
NB_SRC = 18
MOST = 3
WINDOWS = 2
LANES = 128
PAIRS = BLK * BLK
VMEM_LIMIT = 24 * 1024 * 1024
HALF = LAGS // 2
ROOM = 4
HALVES = 2
JOINT = 1


def whiten_kernel(parts, second, place_ref, spec_ref, *refs):
    blocks = F // LANES
    each = blocks // parts
    place = place_ref[0]
    out_refs = list(refs[-parts:])

    def values(start):
        span = pl.ds(start, LANES)
        re = spec_ref[0, :, span].astype(jnp.float32)
        im = spec_ref[1, :, span].astype(jnp.float32)
        return re, im, re * re + im * im

    if second:
        deep = spec_ref.shape[1]
        joint = out_refs[JOINT]
        joint[:deep] = refs[0][...]
        joint[deep:, each * 2 * LANES :] = jnp.zeros((deep, LANES), jnp.bfloat16)
        out_refs[JOINT] = joint.at[deep:]
    else:
        pairs_ref = refs[0]
        shape = (spec_ref.shape[1], LANES)
        line = lax.broadcasted_iota(jnp.int32, shape, 0)
        spare = jnp.zeros((1, LANES - NB_SRC), jnp.int32)
        wide = lambda row: jnp.broadcast_to(jnp.concatenate([row, spare], axis=1), shape)
        notes = jnp.where(line == 0, wide(pairs_ref[0:1]), wide(pairs_ref[1:2]))
        notes = notes.astype(jnp.float32).astype(jnp.bfloat16)
        for out_ref in out_refs:
            out_ref[:, each * 2 * LANES :] = notes
    sums = [None] * 4
    for k in range(blocks):
        power = values(k * LANES)[2]
        sums[k % 4] = power if k < 4 else sums[k % 4] + power
    total = jnp.sum((sums[0] + sums[1]) + (sums[2] + sums[3]), axis=1, keepdims=True)
    level = 0.1 * (total * (1.0 / F) + 1e-05)
    for d, out_ref in enumerate(out_refs):
        first = jnp.bitwise_xor(place, d) * each
        for k in range(each):
            re, im, power = values(pl.multiple_of((first + k) * LANES, LANES))
            scale = lax.rsqrt(power + level)
            at = k * 2 * LANES
            out_ref[:, at : at + LANES] = (re * scale).astype(jnp.bfloat16)
            out_ref[:, at + LANES : at + 2 * LANES] = (im * scale).astype(jnp.bfloat16)


def whiten(spectra, others, place, parts, second):
    rows = spectra.shape[0] * WINDOWS
    planes = jnp.transpose(spectra.reshape(rows, 2, F), (1, 0, 2))
    width = 2 * F // parts
    shapes = [(rows, width if second else width + LANES)] * parts
    if second:
        shapes[JOINT] = (HALVES * rows, width + LANES)
    whole = lambda array: pl.BlockSpec(array.shape, lambda i, place: (0,) * array.ndim)
    return list(pl.pallas_call(
        functools.partial(whiten_kernel, parts, second),
        grid_spec=pltpu.PrefetchScalarGridSpec(
            num_scalar_prefetch=1,
            grid=(1,),
            in_specs=[whole(array) for array in [planes, *others]],
            out_specs=[pl.BlockSpec(shape, lambda i, place: (0, 0)) for shape in shapes],
        ),
        out_shape=[jax.ShapeDtypeStruct(shape, jnp.bfloat16) for shape in shapes],
        compiler_params=pltpu.CompilerParams(vmem_limit_bytes=VMEM_LIMIT),
        name="whiten",
    )(place[None], planes, *others))


def table_kernel(first_ref, hi_cos_ref, hi_sin_ref, mid_cos_ref, mid_sin_ref, lo_cos_ref, lo_sin_ref, out_ref, cos, sin):
    s = pl.program_id(0)
    few = lo_cos_ref.shape[0]

    @pl.when(s == 0)
    def combine():
        lo_cos = lo_cos_ref[...]
        lo_sin = lo_sin_ref[...]
        for i in range(LANES // few):
            mid_cos = mid_cos_ref[i : i + 1]
            mid_sin = mid_sin_ref[i : i + 1]
            cos[i * few : (i + 1) * few] = mid_cos * lo_cos - mid_sin * lo_sin
            sin[i * few : (i + 1) * few] = mid_sin * lo_cos + mid_cos * lo_sin

    hi_cos = hi_cos_ref[pl.ds(s, 1), :]
    hi_sin = hi_sin_ref[pl.ds(s, 1), :]
    minus_cos = -hi_cos
    for i in range(0, LANES, 16):
        lo_cos = cos[i : i + 16]
        lo_sin = sin[i : i + 16]
        out_ref[i : i + 16, :HALF] = (hi_cos * lo_cos - hi_sin * lo_sin).astype(jnp.bfloat16)
        out_ref[i : i + 16, HALF:] = (minus_cos * lo_sin - hi_sin * lo_cos).astype(jnp.bfloat16)

    @pl.when(jnp.logical_and(first_ref[0] == 0, s == 0))
    def zero_bin():
        row = lax.broadcasted_iota(jnp.int32, (16, HALF), 0)
        weight = jnp.where(row == 0, 0.5, 1.0)
        out_ref[0:16, :HALF] = ((hi_cos * cos[0:16] - hi_sin * sin[0:16]) * weight).astype(jnp.bfloat16)


def tables(place, chunks):
    lag = jnp.arange(HALF, dtype=jnp.int32)
    few = 8
    middle = LANES // few
    bins = jnp.concatenate([
        (place * chunks + jnp.arange(chunks, dtype=jnp.int32)) * LANES,
        jnp.arange(middle, dtype=jnp.int32) * few,
        jnp.arange(few, dtype=jnp.int32),
    ])
    phase = bins[:, None] * lag[None, :] % (2 * F)
    angle = phase.astype(jnp.float32) * (jnp.pi / F)
    cos = jnp.cos(angle)
    sin = jnp.sin(angle)
    unit = 2.0 / jnp.sqrt(jnp.float32(F))
    cuts = [slice(0, chunks), slice(chunks, chunks + middle), slice(chunks + middle, None)]
    operands = [cos[cuts[0]] * unit, sin[cuts[0]] * unit, cos[cuts[1]], sin[cuts[1]], cos[cuts[2]], sin[cuts[2]]]
    return pl.pallas_call(
        table_kernel,
        grid_spec=pltpu.PrefetchScalarGridSpec(
            num_scalar_prefetch=1,
            grid=(chunks,),
            in_specs=[pl.BlockSpec(array.shape, lambda s, first: (0, 0)) for array in operands],
            out_specs=pl.BlockSpec((LANES, LAGS), lambda s, first: (s, 0)),
            scratch_shapes=[pltpu.VMEM((LANES, HALF), jnp.float32)] * 2,
        ),
        out_shape=jax.ShapeDtypeStruct((chunks * LANES, LAGS), jnp.bfloat16),
        cost_estimate=pl.CostEstimate(
            flops=chunks * LANES * LAGS * 4, bytes_accessed=chunks * LANES * LAGS * 2, transcendentals=0
        ),
        compiler_params=pltpu.CompilerParams(vmem_limit_bytes=VMEM_LIMIT),
        name="tables",
    )(place[None], *operands)


def iota(shape, axis):
    return lax.broadcasted_iota(jnp.int32, shape, axis)


def ones(hit):
    return hit.astype(jnp.float32).astype(jnp.bfloat16)


def choose_rows(parts, lists, place, packed, rows_ref):
    height = rows_ref.shape[1]
    count = rows_ref.shape[0] // (2 * BLK * WINDOWS)
    deep = packed.shape[0] // lists
    blocks = deep // (BLK * WINDOWS)
    line = iota((count, 1), 0)
    group = jnp.zeros_like(line)
    for z in range(1, lists):
        group = group + jnp.where(line >= z * NB_SRC, 1, 0)
    here = iota((count, LANES), 1) == line - group * NB_SRC

    def column(kind):
        row = ones(iota((count, packed.shape[0]), 1) == group * deep + kind)
        found = jnp.dot(row, packed, preferred_element_type=jnp.float32)
        return jnp.sum(jnp.where(here, found, 0.0), axis=1, keepdims=True).astype(jnp.int32)

    across = iota((count, height), 1)
    picks = []
    for block in (column(0), column(1)):
        source = jnp.bitwise_xor(lax.shift_right_logical(block, (HALVES * blocks).bit_length() - 1), place)
        half = jnp.bitwise_and(lax.shift_right_logical(block, blocks.bit_length() - 1), HALVES - 1)
        inner = jnp.bitwise_and(block, blocks - 1)
        first = (half * parts + source) * deep + inner * (BLK * WINDOWS)
        for offset in range(BLK * WINDOWS):
            picks.append((across == first + offset).astype(jnp.float32))
    rows_ref[...] = jnp.concatenate(picks, axis=0).astype(jnp.bfloat16)


def corr_kernel(per_step, parts, lists, place, *refs):
    refs = list(refs)
    note_refs, panel_refs, refs = refs[:lists], refs[lists : lists + 2 * parts - 1], refs[lists + 2 * parts - 1 :]
    (table_ref, ends_ref), out_refs, (total, edge, rows_ref) = refs[:2], refs[2:-3], refs[-3:]
    deep = panel_refs[0].shape[0]
    panel_refs.insert(parts + JOINT, panel_refs[JOINT].at[deep:])
    panel_refs[JOINT] = panel_refs[JOINT].at[:deep]
    step = pl.program_id(0)
    count = total.shape[0] // PAIRS

    @pl.when(step == 0)
    def prepare():
        packed = jnp.concatenate([ref[:deep] for ref in note_refs])
        choose_rows(parts, lists, place[0], packed, rows_ref)

    panel = jnp.concatenate([ref[...] for ref in panel_refs])
    chosen = jnp.dot(rows_ref[...], panel, preferred_element_type=jnp.float32)

    def row(side, channel, window, start):
        first = ((side * BLK + channel) * WINDOWS + window) * count
        return chosen[first : first + count, start : start + LANES]

    reals = []
    imags = []
    lane = iota((1, LANES), 1)
    first_bin = jnp.logical_and(jnp.logical_and(place[0] == 0, step == 0), lane == 0)
    edge_part = 0.0
    for i in range(per_step):
        at = i * 2 * LANES
        real = []
        imag = []
        for p in range(BLK):
            for q in range(BLK):
                re = 0.0
                im = 0.0
                for w in range(WINDOWS):
                    ra, ia = row(0, p, w, at), row(0, p, w, at + LANES)
                    rb, ib = row(1, q, w, at), row(1, q, w, at + LANES)
                    re = re + (ra * rb + ia * ib)
                    im = im + (ia * rb - ra * ib)
                real.append(re * (1.0 / WINDOWS))
                imag.append(im * (1.0 / WINDOWS))
        real = jnp.concatenate(real, axis=0)
        imag = jnp.concatenate(imag, axis=0)
        ends = ends_ref[0:1]
        if i == 0:
            ends = jnp.where(first_bin, 0.5 * ends, ends)
        edge_part = edge_part + (real * ends + imag * ends_ref[1:2])
        reals.append(real.astype(jnp.bfloat16))
        imags.append(imag.astype(jnp.bfloat16))

    def transform(pieces, columns):
        rows = jnp.concatenate(pieces, axis=1)
        return jnp.dot(rows, table_ref[:, columns], preferred_element_type=jnp.float32)

    even = transform(reals, slice(0, HALF))
    odd = transform(imags, slice(HALF, LAGS))

    @pl.when(step == 0)
    def start():
        total[:, :HALF] = even
        total[:, HALF:] = odd
        edge[...] = edge_part

    @pl.when(step > 0)
    def add():
        total[:, :HALF] += even
        total[:, HALF:] += odd
        edge[...] += edge_part

    @pl.when(step == pl.num_programs(0) - 1)
    def finish():
        even = total[:, :HALF]
        odd = total[:, HALF:]
        later = (even + odd).astype(jnp.bfloat16)
        mirror = ones(iota((HALF, HALF), 0) + iota((HALF, HALF), 1) == HALF)
        sooner = jnp.dot((even - odd).astype(jnp.bfloat16), mirror, preferred_element_type=jnp.float32)
        least = jnp.sum(edge[...], axis=1, keepdims=True)
        sooner = jnp.where(iota(sooner.shape, 1) == 0, least, sooner).astype(jnp.bfloat16)
        each = NB_SRC * PAIRS
        shape = (each * len(out_refs), PAIRS * count)
        column = iota(shape, 1)
        number = column * PAIRS
        for n in range(1, PAIRS):
            number = number - jnp.where(column >= n * count, count * PAIRS - 1, 0)
        order = ones(iota(shape, 0) == number)
        both = jnp.concatenate([sooner, later], axis=1)
        rows = jnp.dot(order, both, preferred_element_type=jnp.float32)
        for i, out_ref in enumerate(out_refs):
            out_ref[...] = rows[i * each : (i + 1) * each].astype(jnp.bfloat16)


def correlate(panels, table, place, parts, wanted):
    per_step = 4
    span = per_step * 2 * LANES
    deep = panels[0].shape[0]
    steps = 2 * table.shape[0] // span
    lists = len(wanted)
    count = -(-lists * NB_SRC // 8) * 8
    each = NB_SRC * PAIRS
    turn = np.arange(LANES) * (np.pi / 16)
    ends = np.stack([np.cos(turn), np.sin(turn)]) * (2.0 / np.sqrt(F))
    return pl.pallas_call(
        functools.partial(corr_kernel, per_step, parts, lists),
        grid_spec=pltpu.PrefetchScalarGridSpec(
            num_scalar_prefetch=1,
            grid=(steps,),
            in_specs=[
                pl.BlockSpec((panels[d].shape[0], LANES), lambda i, place: (0, steps * span // LANES))
                for d in wanted
            ]
            + [pl.BlockSpec((array.shape[0], span), lambda i, place: (0, i)) for array in panels]
            + [
                pl.BlockSpec((span // 2, LAGS), lambda i, place: (i, 0)),
                pl.BlockSpec((2, LANES), lambda i, place: (0, 0)),
            ],
            out_specs=[pl.BlockSpec((each, LAGS), lambda i, place: (0, 0))] * lists,
            scratch_shapes=[
                pltpu.VMEM((count * PAIRS, LAGS), jnp.float32),
                pltpu.VMEM((count * PAIRS, LANES), jnp.float32),
                pltpu.VMEM((2 * BLK * WINDOWS * count, deep * parts * HALVES), jnp.bfloat16),
            ],
        ),
        out_shape=[jax.ShapeDtypeStruct((each, LAGS), jnp.bfloat16)] * lists,
        compiler_params=pltpu.CompilerParams(vmem_limit_bytes=VMEM_LIMIT),
        cost_estimate=pl.CostEstimate(
            flops=count * PAIRS * steps * span * LAGS,
            bytes_accessed=steps * span * LAGS,
            transcendentals=0,
        ),
        name="correlate",
    )(place[None], *[panels[d] for d in wanted], *panels, table, jnp.asarray(ends, jnp.float32))


def settle_kernel(owners_ref, *refs):
    part_refs, out_ref = refs[:-1], refs[-1]
    rows = out_ref.shape[0]
    slots = rows // PAIRS
    each = NB_SRC * PAIRS
    tall = 24
    spare = jnp.full((1, LANES - NB_SRC), rows, jnp.int32)
    owner = jnp.concatenate([owners_ref[...], spare], axis=1)
    wide = jnp.broadcast_to(owner, (tall, LANES)).astype(jnp.float32)
    line, lane = iota((tall, LANES), 0), iota((tall, LANES), 1)
    other = jnp.sum(jnp.where(line == lane, wide, 0.0), axis=1, keepdims=True)
    earlier = jnp.logical_and(other == wide, line < lane).astype(jnp.float32)
    rank = jnp.sum(earlier, axis=0, keepdims=True)
    slot = owner.astype(jnp.float32) * ROOM + rank
    held = ones(iota((slots, LANES), 0).astype(jnp.float32) == slot)
    down = ones(lax.shift_right_logical(iota((rows, slots), 0), 2) == iota((rows, slots), 1))
    over = ones(lax.shift_right_logical(iota((LANES, each), 1), 2) == iota((LANES, each), 0))
    block = jnp.dot(down, held, preferred_element_type=jnp.float32).astype(jnp.bfloat16)
    block = jnp.dot(block, over, preferred_element_type=jnp.float32)
    same = jnp.bitwise_and(iota((rows, each), 0), PAIRS - 1) == jnp.bitwise_and(iota((rows, each), 1), PAIRS - 1)
    chosen = jnp.where(same, block, 0.0).astype(jnp.bfloat16)
    total = sum(ref[...].astype(jnp.float32) for ref in part_refs)
    out_ref[...] = jnp.dot(chosen, total.astype(jnp.bfloat16), preferred_element_type=jnp.float32).astype(jnp.bfloat16)


def settle(owners, partials, groups):
    rows = groups * ROOM * PAIRS
    return pl.pallas_call(
        settle_kernel,
        out_shape=jax.ShapeDtypeStruct((rows, LAGS), jnp.bfloat16),
        compiler_params=pltpu.CompilerParams(vmem_limit_bytes=VMEM_LIMIT),
        name="settle",
    )(owners, *partials)


def local(spectra, pair_blocks, owners):
    groups = lax.axis_size("grp")
    parts = lax.axis_size("chan")
    place = lax.axis_index("chan")
    chunks = F // LANES // parts
    each = spectra.shape[0] // HALVES

    def swap(array, d):
        return lax.ppermute(array, "chan", [(i, i ^ d) for i in range(parts)])

    first = whiten(spectra[:each], [pair_blocks[0, 0].T], place, parts, False)
    apart = [d for d in reversed(range(1, parts)) if d != JOINT]
    spectra, ready = lax.optimization_barrier((spectra, first[JOINT]))
    for d in apart:
        first[d] = swap(first[d], d)
    second = whiten(spectra[each:], [ready], place, parts, True)
    for d in apart:
        second[d] = swap(second[d], d)
    first[JOINT] = swap(second.pop(JOINT), JOINT)
    panels = first + second

    table = tables(place, chunks)
    order = list(reversed(range(parts)))
    partials = []
    for wanted in (order[: parts // 2], order[parts // 2 :]):
        for d, rows in zip(wanted, correlate(panels, table, place, parts, wanted)):
            partials.append(swap(rows, d) if d else rows)
    corr = settle(owners[0, 0].T, partials, groups)
    corr = corr.reshape(groups, ROOM * PAIRS, LAGS)
    got = lax.all_to_all(corr, "grp", split_axis=0, concat_axis=0, tiled=True)
    got = got[:, : MOST * PAIRS].reshape(groups * MOST, PAIRS, LAGS)
    return got.astype(jnp.float32).reshape(1, 1, groups * MOST, PAIRS, LAGS)


def solution(mesh):
    return jax.shard_map(
        local,
        mesh=mesh,
        in_specs=(
            P(("grp", "chan"), None, None, None),
            P("grp", "chan", None, None),
            P("grp", "chan", None, None),
        ),
        out_specs=P("grp", "chan", None, None, None),
        check_vma=False,
    )
```

profile of v0, /device:TPU:0, one launch (start us, length us, event | category | flops | bytes accessed | tf_op | source)
XLA Modules:
  0.0 61.5 jit_solution(17497809939914798341)
XLA Ops:
  0.0 1.4 %slice.27 = bf16[8,2,2,8192]{3,2,1,0:T(2,128)(2,1)S(1)} slice(bf16[16,2,2,8192]{3,2,1,0:T(2,128)(2,1)} %param.5), slice={[0:8], [0:2], [0:2], [0:8192]} | slice | bytes 1048576 | tf_op jit(solution)/shard_map/slice | solution.py:371
  1.4 0.3 copy.15
  1.8 0.7 %copy-done.1 = s32[1,1,18,2]{2,3,1,0:T(2,128)S(1)} copy-done((s32[1,1,18,2]{2,3,1,0:T(2,128)S(1)}, s32[1,1,18,2]{2,3,1,0:T(2,128)}, u32[]{:S(2)}) %copy-start.1) | copy-done | bytes 168
  2.4 0.3 whiten.2
  2.8 5.1 %collective-permute-start = (bf16[16,4224]{1,0:T(8,128)(2,1)S(1)}, bf16[16,4224]{1,0:T(8,128)(2,1)S(1)}, u32[]{:S(2)}, u32[]{:S(2)}) collective-permute-start(bf16[16,4224]{1,0:T(8,128)(2,1)S(1)} %get-tuple-element.19), channel_id=1, source_target_pairs={{0,3},{1,2},{2,1},{3,0},{4,7},{5,6},{6,5},{7,4},{8,11},{9,10},{10,... | collective-permute-start | bytes 405512 | tf_op jit(solution)/shard_map/ppermute | solution.py:369
  7.9 1.4 %slice.28 = bf16[8,2,2,8192]{3,2,1,0:T(2,128)(2,1)S(1)} slice(bf16[16,2,2,8192]{3,2,1,0:T(2,128)(2,1)} %param.5), slice={[8:16], [0:2], [0:2], [0:8192]} | slice | bytes 1048576 | tf_op jit(solution)/shard_map/slice | solution.py:376
  9.3 0.3 copy.14
  9.6 0.3 whiten.3
  9.9 0.7 %collective-permute-start.2 = (bf16[32,4224]{1,0:T(8,128)(2,1)S(1)}, bf16[32,4224]{1,0:T(8,128)(2,1)S(1)}, u32[]{:S(2)}, u32[]{:S(2)}) collective-permute-start(bf16[32,4224]{1,0:T(8,128)(2,1)S(1)} %get-tuple-element.25), channel_id=1, source_target_pairs={{0,1},{1,0},{2,3},{3,2},{4,5},{5,4},{6,7},{7,6},{8,9},{9,8},{10,11... | collective-permute-start | bytes 811016 | tf_op jit(solution)/shard_map/ppermute | solution.py:369
  10.6 2.4 %collective-permute-start.3 = (bf16[16,4096]{1,0:T(8,128)(2,1)S(1)}, bf16[16,4096]{1,0:T(8,128)(2,1)S(1)}, u32[]{:S(2)}, u32[]{:S(2)}) collective-permute-start(bf16[16,4096]{1,0:T(8,128)(2,1)S(1)} %get-tuple-element.27), channel_id=1, source_target_pairs={{0,2},{1,3},{2,0},{3,1},{4,6},{5,7},{6,4},{7,5},{8,10},{9,11},{10,... | collective-permute-start | bytes 393224 | tf_op jit(solution)/shard_map/ppermute | solution.py:369
  13.0 1.4 %collective-permute-start.4 = (bf16[16,4096]{1,0:T(8,128)(2,1)S(1)}, bf16[16,4096]{1,0:T(8,128)(2,1)S(1)}, u32[]{:S(2)}, u32[]{:S(2)}) collective-permute-start(bf16[16,4096]{1,0:T(8,128)(2,1)S(1)} %get-tuple-element.28), channel_id=1, source_target_pairs={{0,3},{1,2},{2,1},{3,0},{4,7},{5,6},{6,5},{7,4},{8,11},{9,10},{10,... | collective-permute-start | bytes 393224 | tf_op jit(solution)/shard_map/ppermute | solution.py:369
  14.5 0.4 fusion.6
  14.9 1.3 %tables.1.refs_9_ = bf16[2048,1024]{1,0:T(8,128)(2,1)S(1)} custom-call(s32[1]{0:T(128)} %bitcast.1.place_ref.first_ref.place, f32[16,512]{1,0:T(8,128)S(1)} %get-tuple-element.39.hi_cos_ref, f32[16,512]{1,0:T(8,128)S(1)} %get-tuple-element.34.hi_sin_ref, f32[16,512]{1,0:T(8,128)S(1)} %get-tuple-element.40.mid_cos_ref, ...), custom_call_target="tpu_custom_call" | custom-call | flops 8388608 | bytes 4194304 | tf_op jit(solution)/shard_map/tables/pallas_call | solution.py:138
  16.3 12.5 %collective-permute-done.3.refs_7_ = bf16[16,4096]{1,0:T(8,128)(2,1)S(1)} collective-permute-done((bf16[16,4096]{1,0:T(8,128)(2,1)S(1)}, bf16[16,4096]{1,0:T(8,128)(2,1)S(1)}, u32[]{:S(2)}, u32[]{:S(2)}) %collective-permute-start.3) | collective-permute-done | bytes 131104 | tf_op jit(solution)/shard_map/ppermute | solution.py:369
  28.8 4.6 %correlate.2 = (bf16[72,1024]{1,0:T(8,128)(2,1)S(1)}, bf16[72,1024]{1,0:T(8,128)(2,1)S(1)}) custom-call(s32[1]{0:T(128)} %bitcast.1.place_ref.first_ref.place, bf16[16,4224]{1,0:T(8,128)(2,1)S(1)} %collective-permute-done.refs_0_.refs_5_, bf16[16,4224]{1,0:T(8,128)(2,1)S(1)} %collective-permute-done.1.refs_1_.refs_4_, ...), custom_call_target="tpu_custom_call" | custom-call | flops 671088640 | bytes 4194304 | tf_op jit(solution)/shard_map/correlate/pallas_call | solution.py:294
  33.4 2.7 %collective-permute-start.5 = (bf16[72,1024]{1,0:T(8,128)(2,1)S(1)}, bf16[72,1024]{1,0:T(8,128)(2,1)S(1)}, u32[]{:S(2)}, u32[]{:S(2)}) collective-permute-start(bf16[72,1024]{1,0:T(8,128)(2,1)S(1)} %get-tuple-element.29), channel_id=1, source_target_pairs={{0,3},{1,2},{2,1},{3,0},{4,7},{5,6},{6,5},{7,4},{8,11},{9,10},{10,... | collective-permute-start | bytes 442376 | tf_op jit(solution)/shard_map/ppermute | solution.py:369
  36.1 1.2 %collective-permute-start.6 = (bf16[72,1024]{1,0:T(8,128)(2,1)S(1)}, bf16[72,1024]{1,0:T(8,128)(2,1)S(1)}, u32[]{:S(2)}, u32[]{:S(2)}) collective-permute-start(bf16[72,1024]{1,0:T(8,128)(2,1)S(1)} %get-tuple-element.30), channel_id=1, source_target_pairs={{0,2},{1,3},{2,0},{3,1},{4,6},{5,7},{6,4},{7,5},{8,10},{9,11},{10,... | collective-permute-start | bytes 442376 | tf_op jit(solution)/shard_map/ppermute | solution.py:369
  37.3 4.5 %correlate.3 = (bf16[72,1024]{1,0:T(8,128)(2,1)S(1)}, bf16[72,1024]{1,0:T(8,128)(2,1)S(1)}) custom-call(s32[1]{0:T(128)} %bitcast.1.place_ref.first_ref.place, bf16[32,4224]{1,0:T(8,128)(2,1)S(1)} %collective-permute-done.2.refs_3_.refs_0_, bf16[16,4224]{1,0:T(8,128)(2,1)S(1)} %get-tuple-element.21.refs_2_.refs_1_, ...), custom_call_target="tpu_custom_call" | custom-call | flops 671088640 | bytes 4194304 | tf_op jit(solution)/shard_map/correlate/pallas_call | solution.py:294
  41.9 0.6 collective-permute-start.7
  42.5 6.3 %collective-permute-done.6.refs_1_ = bf16[72,1024]{1,0:T(8,128)(2,1)S(1)} collective-permute-done((bf16[72,1024]{1,0:T(8,128)(2,1)S(1)}, bf16[72,1024]{1,0:T(8,128)(2,1)S(1)}, u32[]{:S(2)}, u32[]{:S(2)}) %collective-permute-start.6) | collective-permute-done | bytes 147488 | tf_op jit(solution)/shard_map/ppermute | solution.py:369
  48.8 0.8 %collective-permute-done.7.refs_2_ = bf16[72,1024]{1,0:T(8,128)(2,1)S(1)} collective-permute-done((bf16[72,1024]{1,0:T(8,128)(2,1)S(1)}, bf16[72,1024]{1,0:T(8,128)(2,1)S(1)}, u32[]{:S(2)}, u32[]{:S(2)}) %collective-permute-start.7) | collective-permute-done | bytes 147488 | tf_op jit(solution)/shard_map/ppermute | solution.py:369
  49.6 0.5 settle.1
  50.1 10.5 %all_to_all.5 = bf16[8,16,1024]{2,1,0:T(8,128)(2,1)S(1)} all-to-all(bf16[8,16,1024]{2,1,0:T(8,128)(2,1)S(1)} %bitcast.16), channel_id=1, replica_groups=mesh['grp'=8,'chan'=4] {'grp'}, dimensions={0} | all-to-all | bytes 524288 | tf_op jit(solution)/shard_map/all_to_all | solution.py:390
  60.7 0.9 %reshape.27 = f32[1,1,24,4,1024]{4,3,2,1,0:T(4,128)} reshape(f32[8,12,1024]{2,1,0:T(8,128)S(1)} %slice_convert_fusion) | data formatting | bytes 786432 | tf_op jit(solution)/shard_map/convert_element_type | solution.py:392
  (19 shorter events, 0.2 us)
Async XLA Ops:
  1.7 27.0 %copy-start = (f32[2,128]{1,0:T(2,128)S(1)}, f32[2,128]{1,0:T(2,128)}, u32[]{:S(2)}) copy-start(f32[2,128]{1,0:T(2,128)} %constant.31.clone.refs_10_) | copy-start | bytes 3076
  1.7 0.7 %copy-start.1 = (s32[1,1,18,2]{2,3,1,0:T(2,128)S(1)}, s32[1,1,18,2]{2,3,1,0:T(2,128)}, u32[]{:S(2)}) copy-start(s32[1,1,18,2]{2,3,1,0:T(2,128)} %param.6) | copy-start | bytes 436
  2.8 26.0 %collective-permute-start = (bf16[16,4224]{1,0:T(8,128)(2,1)S(1)}, bf16[16,4224]{1,0:T(8,128)(2,1)S(1)}, u32[]{:S(2)}, u32[]{:S(2)}) collective-permute-start(bf16[16,4224]{1,0:T(8,128)(2,1)S(1)} %get-tuple-element.19), channel_id=1, source_target_pairs={{0,3},{1,2},{2,1},{3,0},{4,7},{5,6},{6,5},{7,4},{8,11},{9,10},{10,... | collective-permute-start | bytes 405512 | tf_op jit(solution)/shard_map/ppermute | solution.py:369
  7.9 20.9 %collective-permute-start.1 = (bf16[16,4224]{1,0:T(8,128)(2,1)S(1)}, bf16[16,4224]{1,0:T(8,128)(2,1)S(1)}, u32[]{:S(2)}, u32[]{:S(2)}) collective-permute-start(bf16[16,4224]{1,0:T(8,128)(2,1)S(1)} %get-tuple-element.20), channel_id=1, source_target_pairs={{0,2},{1,3},{2,0},{3,1},{4,6},{5,7},{6,4},{7,5},{8,10},{9,11},{10,... | collective-permute-start | bytes 405512 | tf_op jit(solution)/shard_map/ppermute | solution.py:369
  9.9 18.8 %collective-permute-start.2 = (bf16[32,4224]{1,0:T(8,128)(2,1)S(1)}, bf16[32,4224]{1,0:T(8,128)(2,1)S(1)}, u32[]{:S(2)}, u32[]{:S(2)}) collective-permute-start(bf16[32,4224]{1,0:T(8,128)(2,1)S(1)} %get-tuple-element.25), channel_id=1, source_target_pairs={{0,1},{1,0},{2,3},{3,2},{4,5},{5,4},{6,7},{7,6},{8,9},{9,8},{10,11... | collective-permute-start | bytes 811016 | tf_op jit(solution)/shard_map/ppermute | solution.py:369
  10.6 18.1 %collective-permute-start.3 = (bf16[16,4096]{1,0:T(8,128)(2,1)S(1)}, bf16[16,4096]{1,0:T(8,128)(2,1)S(1)}, u32[]{:S(2)}, u32[]{:S(2)}) collective-permute-start(bf16[16,4096]{1,0:T(8,128)(2,1)S(1)} %get-tuple-element.27), channel_id=1, source_target_pairs={{0,2},{1,3},{2,0},{3,1},{4,6},{5,7},{6,4},{7,5},{8,10},{9,11},{10,... | collective-permute-start | bytes 393224 | tf_op jit(solution)/shard_map/ppermute | solution.py:369
  13.0 15.7 %collective-permute-start.4 = (bf16[16,4096]{1,0:T(8,128)(2,1)S(1)}, bf16[16,4096]{1,0:T(8,128)(2,1)S(1)}, u32[]{:S(2)}, u32[]{:S(2)}) collective-permute-start(bf16[16,4096]{1,0:T(8,128)(2,1)S(1)} %get-tuple-element.28), channel_id=1, source_target_pairs={{0,3},{1,2},{2,1},{3,0},{4,7},{5,6},{6,5},{7,4},{8,11},{9,10},{10,... | collective-permute-start | bytes 393224 | tf_op jit(solution)/shard_map/ppermute | solution.py:369
  33.4 16.2 %copy-start.2 = (s32[1,1,18,1]{2,3,1,0:T(1,128)S(1)}, s32[1,1,18,1]{2,3,1,0:T(1,128)}, u32[]{:S(2)}) copy-start(s32[1,1,18,1]{2,3,1,0:T(1,128)} %param.7) | copy-start | bytes 220
  33.4 9.1 %collective-permute-start.5 = (bf16[72,1024]{1,0:T(8,128)(2,1)S(1)}, bf16[72,1024]{1,0:T(8,128)(2,1)S(1)}, u32[]{:S(2)}, u32[]{:S(2)}) collective-permute-start(bf16[72,1024]{1,0:T(8,128)(2,1)S(1)} %get-tuple-element.29), channel_id=1, source_target_pairs={{0,3},{1,2},{2,1},{3,0},{4,7},{5,6},{6,5},{7,4},{8,11},{9,10},{10,... | collective-permute-start | bytes 442376 | tf_op jit(solution)/shard_map/ppermute | solution.py:369
  36.1 12.7 %collective-permute-start.6 = (bf16[72,1024]{1,0:T(8,128)(2,1)S(1)}, bf16[72,1024]{1,0:T(8,128)(2,1)S(1)}, u32[]{:S(2)}, u32[]{:S(2)}) collective-permute-start(bf16[72,1024]{1,0:T(8,128)(2,1)S(1)} %get-tuple-element.30), channel_id=1, source_target_pairs={{0,2},{1,3},{2,0},{3,1},{4,6},{5,7},{6,4},{7,5},{8,10},{9,11},{10,... | collective-permute-start | bytes 442376 | tf_op jit(solution)/shard_map/ppermute | solution.py:369
  41.9 7.7 %collective-permute-start.7 = (bf16[72,1024]{1,0:T(8,128)(2,1)S(1)}, bf16[72,1024]{1,0:T(8,128)(2,1)S(1)}, u32[]{:S(2)}, u32[]{:S(2)}) collective-permute-start(bf16[72,1024]{1,0:T(8,128)(2,1)S(1)} %get-tuple-element.31), channel_id=1, source_target_pairs={{0,1},{1,0},{2,3},{3,2},{4,5},{5,4},{6,7},{7,6},{8,9},{9,8},{10,11... | collective-permute-start | bytes 442376 | tf_op jit(solution)/shard_map/ppermute | solution.py:369
where the time goes:
time: 61.8 us; the launch traced here: 61.5 us
  waiting for transfers between devices  19.6 us (32%)
  starting transfers between devices  14.1 us (23%)
  Pallas kernels  11.7 us (19%)
  blocking collectives  10.5 us (17%)
  local copies, waits for them, and re-layouts  5 us (8%)
    ppermute x8, waiting for transfers between devices, swap(): return lax.ppermute(array, 'chan', [(i, i ^ d) for i in range(parts)])  19.6 us
    ppermute x8, starting transfers between devices, swap(): return lax.ppermute(array, 'chan', [(i, i ^ d) for i in range(parts)])  14.1 us
    all_to_all x1, blocking collectives, local(): got = lax.all_to_all(corr, 'grp', split_axis=0, concat_axis=0, tiled=True)  10.5 us
    pallas_call x2, Pallas kernels, correlate(): pl.pallas_call(functools.partial(corr_kernel, per_step, parts, lists), gr...  9.18 us
    slice x1, local copies, waits for them, and re-layouts, local(): second = whiten(spectra[each:], [ready], place, parts, True)  1.43 us
    slice x1, local copies, waits for them, and re-layouts, local(): first = whiten(spectra[:each], [pair_blocks[0, 0].T], place, parts, False)  1.43 us
    pallas_call x1, Pallas kernels, tables(): pl.pallas_call(table_kernel, grid_spec=pltpu.PrefetchScalarGridSpec(num_s...  1.33 us
  transfers between devices with their start and end apart: 8, of which 3 were waited for; matrix products, arithmetic and copies ran while one was open for 4% of the time, Pallas kernels for 10%

commit v1 on v0

--- a/solution.py
+++ b/solution.py
@@ -38,11 +38,10 @@
     if second:
         deep = spec_ref.shape[1]
         joint = out_refs[JOINT]
-        joint[:deep] = refs[0][...]
-        joint[deep:, each * 2 * LANES :] = jnp.zeros((deep, LANES), jnp.bfloat16)
+        joint[:deep, : each * 2 * LANES] = refs[0][...]
+        joint[:deep, each * 2 * LANES :] = jnp.zeros((deep, LANES), jnp.bfloat16)
         out_refs[JOINT] = joint.at[deep:]
-    else:
-        pairs_ref = refs[0]
+        pairs_ref = refs[1]
         shape = (spec_ref.shape[1], LANES)
         line = lax.broadcasted_iota(jnp.int32, shape, 0)
         spare = jnp.zeros((1, LANES - NB_SRC), jnp.int32)
@@ -71,7 +70,7 @@
     rows = spectra.shape[0] * WINDOWS
     planes = jnp.transpose(spectra.reshape(rows, 2, F), (1, 0, 2))
     width = 2 * F // parts
-    shapes = [(rows, width if second else width + LANES)] * parts
+    shapes = [(rows, width + LANES if second else width)] * parts
     if second:
         shapes[JOINT] = (HALVES * rows, width + LANES)
     whole = lambda array: pl.BlockSpec(array.shape, lambda i, place: (0,) * array.ndim)
@@ -201,7 +200,7 @@
 
     @pl.when(step == 0)
     def prepare():
-        packed = jnp.concatenate([ref[:deep] for ref in note_refs])
+        packed = jnp.concatenate([ref[ref.shape[0] - deep :] for ref in note_refs])
         choose_rows(parts, lists, place[0], packed, rows_ref)
 
     panel = jnp.concatenate([ref[...] for ref in panel_refs])
@@ -289,6 +288,8 @@
     lists = len(wanted)
     count = -(-lists * NB_SRC // 8) * 8
     each = NB_SRC * PAIRS
+    noted = panels[parts:]
+    noted.insert(JOINT, panels[JOINT])
     turn = np.arange(LANES) * (np.pi / 16)
     ends = np.stack([np.cos(turn), np.sin(turn)]) * (2.0 / np.sqrt(F))
     return pl.pallas_call(
@@ -297,7 +298,7 @@
             num_scalar_prefetch=1,
             grid=(steps,),
             in_specs=[
-                pl.BlockSpec((panels[d].shape[0], LANES), lambda i, place: (0, steps * span // LANES))
+                pl.BlockSpec((noted[d].shape[0], LANES), lambda i, place: (0, steps * span // LANES))
                 for d in wanted
             ]
             + [pl.BlockSpec((array.shape[0], span), lambda i, place: (0, i)) for array in panels]
@@ -320,12 +321,12 @@
             transcendentals=0,
         ),
         name="correlate",
-    )(place[None], *[panels[d] for d in wanted], *panels, table, jnp.asarray(ends, jnp.float32))
-
-
-def settle_kernel(owners_ref, *refs):
-    part_refs, out_ref = refs[:-1], refs[-1]
-    rows = out_ref.shape[0]
+    )(place[None], *[noted[d] for d in wanted], *panels, table, jnp.asarray(ends, jnp.float32))
+
+
+def settle_kernel(groups, mine_ref, owners_ref, *refs):
+    part_refs, out_refs = refs[:-groups], refs[-groups:]
+    rows = groups * ROOM * PAIRS
     slots = rows // PAIRS
     each = NB_SRC * PAIRS
     tall = 24
@@ -336,7 +337,7 @@
     other = jnp.sum(jnp.where(line == lane, wide, 0.0), axis=1, keepdims=True)
     earlier = jnp.logical_and(other == wide, line < lane).astype(jnp.float32)
     rank = jnp.sum(earlier, axis=0, keepdims=True)
-    slot = owner.astype(jnp.float32) * ROOM + rank
+    slot = jnp.bitwise_xor(owner, mine_ref[0]).astype(jnp.float32) * ROOM + rank
     held = ones(iota((slots, LANES), 0).astype(jnp.float32) == slot)
     down = ones(lax.shift_right_logical(iota((rows, slots), 0), 2) == iota((rows, slots), 1))
     over = ones(lax.shift_right_logical(iota((LANES, each), 1), 2) == iota((LANES, each), 0))
@@ -345,17 +346,52 @@
     same = jnp.bitwise_and(iota((rows, each), 0), PAIRS - 1) == jnp.bitwise_and(iota((rows, each), 1), PAIRS - 1)
     chosen = jnp.where(same, block, 0.0).astype(jnp.bfloat16)
     total = sum(ref[...].astype(jnp.float32) for ref in part_refs)
-    out_ref[...] = jnp.dot(chosen, total.astype(jnp.bfloat16), preferred_element_type=jnp.float32).astype(jnp.bfloat16)
-
-
-def settle(owners, partials, groups):
-    rows = groups * ROOM * PAIRS
-    return pl.pallas_call(
-        settle_kernel,
-        out_shape=jax.ShapeDtypeStruct((rows, LAGS), jnp.bfloat16),
+    placed = jnp.dot(chosen, total.astype(jnp.bfloat16), preferred_element_type=jnp.float32)
+    deep = ROOM * PAIRS
+    for m, out_ref in enumerate(out_refs):
+        out_ref[...] = placed[m * deep : (m + 1) * deep].astype(jnp.bfloat16)
+
+
+def settle(owners, partials, mine, groups):
+    whole = lambda array: pl.BlockSpec(array.shape, lambda i, mine: (0, 0))
+    outs = [jax.ShapeDtypeStruct((ROOM * PAIRS, LAGS), jnp.bfloat16)] * groups
+    return list(pl.pallas_call(
+        functools.partial(settle_kernel, groups),
+        grid_spec=pltpu.PrefetchScalarGridSpec(
+            num_scalar_prefetch=1,
+            grid=(1,),
+            in_specs=[whole(array) for array in [owners, *partials]],
+            out_specs=[whole(array) for array in outs],
+        ),
+        out_shape=outs,
         compiler_params=pltpu.CompilerParams(vmem_limit_bytes=VMEM_LIMIT),
         name="settle",
-    )(owners, *partials)
+    )(mine[None], owners, *partials))
+
+
+def widen_kernel(mine_ref, *refs):
+    part_refs, out_ref = refs[:-1], refs[-1]
+    for m, part_ref in enumerate(part_refs):
+        values = part_ref[...].astype(jnp.float32)
+        first = jnp.bitwise_xor(mine_ref[0], m) * MOST
+        for r in range(MOST):
+            out_ref[first + r] = values[r * PAIRS : (r + 1) * PAIRS]
+
+
+def widen(pieces, mine):
+    shape = (len(pieces) * MOST, PAIRS, LAGS)
+    return pl.pallas_call(
+        widen_kernel,
+        grid_spec=pltpu.PrefetchScalarGridSpec(
+            num_scalar_prefetch=1,
+            grid=(1,),
+            in_specs=[pl.BlockSpec(array.shape, lambda i, mine: (0, 0)) for array in pieces],
+            out_specs=pl.BlockSpec(shape, lambda i, mine: (0, 0, 0)),
+        ),
+        out_shape=jax.ShapeDtypeStruct(shape, jnp.float32),
+        compiler_params=pltpu.CompilerParams(vmem_limit_bytes=VMEM_LIMIT),
+        name="widen",
+    )(mine[None], *pieces)
 
 
 def local(spectra, pair_blocks, owners):
@@ -368,12 +404,12 @@
     def swap(array, d):
         return lax.ppermute(array, "chan", [(i, i ^ d) for i in range(parts)])
 
-    first = whiten(spectra[:each], [pair_blocks[0, 0].T], place, parts, False)
+    first = whiten(spectra[:each], [], place, parts, False)
     apart = [d for d in reversed(range(1, parts)) if d != JOINT]
     spectra, ready = lax.optimization_barrier((spectra, first[JOINT]))
     for d in apart:
         first[d] = swap(first[d], d)
-    second = whiten(spectra[each:], [ready], place, parts, True)
+    second = whiten(spectra[each:], [ready, pair_blocks[0, 0].T], place, parts, True)
     for d in apart:
         second[d] = swap(second[d], d)
     first[JOINT] = swap(second.pop(JOINT), JOINT)
@@ -385,11 +421,11 @@
     for wanted in (order[: parts // 2], order[parts // 2 :]):
         for d, rows in zip(wanted, correlate(panels, table, place, parts, wanted)):
             partials.append(swap(rows, d) if d else rows)
-    corr = settle(owners[0, 0].T, partials, groups)
-    corr = corr.reshape(groups, ROOM * PAIRS, LAGS)
-    got = lax.all_to_all(corr, "grp", split_axis=0, concat_axis=0, tiled=True)
-    got = got[:, : MOST * PAIRS].reshape(groups * MOST, PAIRS, LAGS)
-    return got.astype(jnp.float32).reshape(1, 1, groups * MOST, PAIRS, LAGS)
+    mine = lax.axis_index("grp")
+    pieces = settle(owners[0, 0].T, partials, mine, groups)
+    for m in reversed(range(1, groups)):
+        pieces[m] = lax.ppermute(pieces[m], "grp", [(i, i ^ m) for i in range(groups)])
+    return widen(pieces, mine)[None, None]
 
 
 def solution(mesh):

time: 61.8 us -> 62.9 us (1.018)
  blocking collectives: 10.5 us -> 0 us
  starting transfers between devices: 14.1 us -> 20.4 us
  waiting for transfers between devices: 19.6 us -> 25.7 us
  local copies, waits for them, and re-layouts: 5 us -> 3.48 us
  Pallas kernels: 11.7 us -> 12.5 us
    all_to_all x1 -> x0, blocking collectives: 10.5 us -> none  [local(): got = lax.all_to_all(corr, 'grp', split_axis=0, concat_axis=0, tiled=True)]
    ppermute x0 -> x7, starting transfers between devices: none -> 6.32 us  [local(): lax.ppermute(pieces[m], 'grp', [(i, i ^ m) for i in range(groups)])]
    ppermute x0 -> x7, waiting for transfers between devices: none -> 4 us  [local(): lax.ppermute(pieces[m], 'grp', [(i, i ^ m) for i in range(groups)])]
    ppermute x8, waiting for transfers between devices: 19.6 us -> 21.7 us  [swap(): return lax.ppermute(array, 'chan', [(i, i ^ d) for i in range(parts)])]
    convert_element_type x1 -> x0, local copies, waits for them, and re-layouts: 0.87 us -> none  [local(): return got.astype(jnp.float32).reshape(1, 1, groups * MOST, PAIRS, LAGS)]
    pallas_call x1 -> x2, Pallas kernels: 0.52 us -> 1.3 us  [the longest x1 0.78 us: widen(): pl.pallas_call(widen_kernel, grid_spec=pltpu.PrefetchScalarGridSpec(num_s...]
    unnamed x6, local copies, waits for them, and re-layouts: 0.69 us -> 0.02 us
  transfers between devices with their start and end apart: 8 -> 15, of which waited for: 3 -> 6; matrix products, arithmetic and copies ran while one was open for 4% -> 1% of each run, Pallas kernels for 10% -> 9%
where the time goes in v1:
time: 62.9 us; the launch traced here: 62.7 us
  waiting for transfers between devices  25.7 us (41%)
  starting transfers between devices  20.4 us (32%)
  Pallas kernels  12.5 us (20%)
  local copies, waits for them, and re-layouts  3.48 us (6%)
    ppermute x8, waiting for transfers between devices, swap(): return lax.ppermute(array, 'chan', [(i, i ^ d) for i in range(parts)])  21.7 us
    ppermute x8, starting transfers between devices, swap(): return lax.ppermute(array, 'chan', [(i, i ^ d) for i in range(parts)])  14 us
    pallas_call x2, Pallas kernels, correlate(): pl.pallas_call(functools.partial(corr_kernel, per_step, parts, lists), gr...  9.23 us
    ppermute x7, starting transfers between devices, local(): lax.ppermute(pieces[m], 'grp', [(i, i ^ m) for i in range(groups)])  6.32 us
    ppermute x7, waiting for transfers between devices, local(): lax.ppermute(pieces[m], 'grp', [(i, i ^ m) for i in range(groups)])  4 us
    slice x1, local copies, waits for them, and re-layouts, local(): first = whiten(spectra[:each], [], place, parts, False)  1.44 us
    slice x1, local copies, waits for them, and re-layouts, local(): spectra[each:]  1.43 us
    pallas_call x1, Pallas kernels, tables(): pl.pallas_call(table_kernel, grid_spec=pltpu.PrefetchScalarGridSpec(num_s...  1.33 us
  transfers between devices with their start and end apart: 15, of which 6 were waited for; matrix products, arithmetic and copies ran while one was open for 1% of the time, Pallas kernels for 9%

profile of v1, /device:TPU:0, one launch (start us, length us, event | category | flops | bytes accessed | tf_op | source)
XLA Modules:
  0.0 62.7 jit_solution(12304962670723547876)
XLA Ops:
  0.0 1.4 %slice.24 = bf16[8,2,2,8192]{3,2,1,0:T(2,128)(2,1)S(1)} slice(bf16[16,2,2,8192]{3,2,1,0:T(2,128)(2,1)} %param.5), slice={[0:8], [0:2], [0:2], [0:8192]} | slice | bytes 1048576 | tf_op jit(solution)/shard_map/slice | solution.py:407
  2.1 1.4 %slice.25 = bf16[8,2,2,8192]{3,2,1,0:T(2,128)(2,1)S(1)} slice(bf16[16,2,2,8192]{3,2,1,0:T(2,128)(2,1)} %param.5), slice={[8:16], [0:2], [0:2], [0:8192]} | slice | bytes 1048576 | tf_op jit(solution)/shard_map/slice | solution.py:412
  4.2 5.1 %collective-permute-start = (bf16[16,4224]{1,0:T(8,128)(2,1)S(1)}, bf16[16,4224]{1,0:T(8,128)(2,1)S(1)}, u32[]{:S(2)}, u32[]{:S(2)}) collective-permute-start(bf16[16,4224]{1,0:T(8,128)(2,1)S(1)} %get-tuple-element.30), channel_id=1, source_target_pairs={{0,3},{1,2},{2,1},{3,0},{4,7},{5,6},{6,5},{7,4},{8,11},{9,10},{10,... | collective-permute-start | bytes 405512 | tf_op jit(solution)/shard_map/ppermute | solution.py:405
  9.3 0.6 %collective-permute-start.2 = (bf16[32,4224]{1,0:T(8,128)(2,1)S(1)}, bf16[32,4224]{1,0:T(8,128)(2,1)S(1)}, u32[]{:S(2)}, u32[]{:S(2)}) collective-permute-start(bf16[32,4224]{1,0:T(8,128)(2,1)S(1)} %get-tuple-element.33), channel_id=1, source_target_pairs={{0,1},{1,0},{2,3},{3,2},{4,5},{5,4},{6,7},{7,6},{8,9},{9,8},{10,11... | collective-permute-start | bytes 811016 | tf_op jit(solution)/shard_map/ppermute | solution.py:405
  9.9 2.3 %collective-permute-start.3 = (bf16[16,4096]{1,0:T(8,128)(2,1)S(1)}, bf16[16,4096]{1,0:T(8,128)(2,1)S(1)}, u32[]{:S(2)}, u32[]{:S(2)}) collective-permute-start(bf16[16,4096]{1,0:T(8,128)(2,1)S(1)} %get-tuple-element.34), channel_id=1, source_target_pairs={{0,2},{1,3},{2,0},{3,1},{4,6},{5,7},{6,4},{7,5},{8,10},{9,11},{10,... | collective-permute-start | bytes 393224 | tf_op jit(solution)/shard_map/ppermute | solution.py:405
  12.2 1.5 %collective-permute-start.4 = (bf16[16,4096]{1,0:T(8,128)(2,1)S(1)}, bf16[16,4096]{1,0:T(8,128)(2,1)S(1)}, u32[]{:S(2)}, u32[]{:S(2)}) collective-permute-start(bf16[16,4096]{1,0:T(8,128)(2,1)S(1)} %get-tuple-element.35), channel_id=1, source_target_pairs={{0,3},{1,2},{2,1},{3,0},{4,7},{5,6},{6,5},{7,4},{8,11},{9,10},{10,... | collective-permute-start | bytes 393224 | tf_op jit(solution)/shard_map/ppermute | solution.py:405
  13.8 0.4 fusion.6
  14.2 1.3 %tables.1.refs_9_ = bf16[2048,1024]{1,0:T(8,128)(2,1)S(1)} custom-call(s32[1]{0:T(128)} %bitcast.2.place_ref.first_ref.place, f32[16,512]{1,0:T(8,128)S(1)} %get-tuple-element.55.hi_cos_ref, f32[16,512]{1,0:T(8,128)S(1)} %get-tuple-element.50.hi_sin_ref, f32[16,512]{1,0:T(8,128)S(1)} %get-tuple-element.56.mid_cos_ref, ...), custom_call_target="tpu_custom_call" | custom-call | flops 8388608 | bytes 4194304 | tf_op jit(solution)/shard_map/tables/pallas_call | solution.py:137
  15.5 14.6 %collective-permute-done.3.refs_4_ = bf16[16,4096]{1,0:T(8,128)(2,1)S(1)} collective-permute-done((bf16[16,4096]{1,0:T(8,128)(2,1)S(1)}, bf16[16,4096]{1,0:T(8,128)(2,1)S(1)}, u32[]{:S(2)}, u32[]{:S(2)}) %collective-permute-start.3) | collective-permute-done | bytes 131104 | tf_op jit(solution)/shard_map/ppermute | solution.py:405
  30.2 4.6 %correlate.2 = (bf16[72,1024]{1,0:T(8,128)(2,1)S(1)}, bf16[72,1024]{1,0:T(8,128)(2,1)S(1)}) custom-call(s32[1]{0:T(128)} %bitcast.2.place_ref.first_ref.place, bf16[16,4224]{1,0:T(8,128)(2,1)S(1)} %collective-permute-done.refs_0_.refs_8_, bf16[16,4224]{1,0:T(8,128)(2,1)S(1)} %collective-permute-done.1.refs_1_.refs_7_, ...), custom_call_target="tpu_custom_call" | custom-call | flops 671088640 | bytes 4194304 | tf_op jit(solution)/shard_map/correlate/pallas_call | solution.py:295
  34.8 2.7 %collective-permute-start.5 = (bf16[72,1024]{1,0:T(8,128)(2,1)S(1)}, bf16[72,1024]{1,0:T(8,128)(2,1)S(1)}, u32[]{:S(2)}, u32[]{:S(2)}) collective-permute-start(bf16[72,1024]{1,0:T(8,128)(2,1)S(1)} %get-tuple-element.37), channel_id=1, source_target_pairs={{0,3},{1,2},{2,1},{3,0},{4,7},{5,6},{6,5},{7,4},{8,11},{9,10},{10,... | collective-permute-start | bytes 442376 | tf_op jit(solution)/shard_map/ppermute | solution.py:405
  37.6 1.2 %collective-permute-start.6 = (bf16[72,1024]{1,0:T(8,128)(2,1)S(1)}, bf16[72,1024]{1,0:T(8,128)(2,1)S(1)}, u32[]{:S(2)}, u32[]{:S(2)}) collective-permute-start(bf16[72,1024]{1,0:T(8,128)(2,1)S(1)} %get-tuple-element.38), channel_id=1, source_target_pairs={{0,2},{1,3},{2,0},{3,1},{4,6},{5,7},{6,4},{7,5},{8,10},{9,11},{10,... | collective-permute-start | bytes 442376 | tf_op jit(solution)/shard_map/ppermute | solution.py:405
  38.8 4.6 %correlate.3 = (bf16[72,1024]{1,0:T(8,128)(2,1)S(1)}, bf16[72,1024]{1,0:T(8,128)(2,1)S(1)}) custom-call(s32[1]{0:T(128)} %bitcast.2.place_ref.first_ref.place, bf16[32,4224]{1,0:T(8,128)(2,1)S(1)} %collective-permute-done.2.refs_3_.refs_0_, bf16[16,4224]{1,0:T(8,128)(2,1)S(1)} %get-tuple-element.36.refs_6_.refs_1_, ...), custom_call_target="tpu_custom_call" | custom-call | flops 671088640 | bytes 4194304 | tf_op jit(solution)/shard_map/correlate/pallas_call | solution.py:295
  43.4 0.6 collective-permute-start.7
  43.9 6.3 %collective-permute-done.6.refs_1_ = bf16[72,1024]{1,0:T(8,128)(2,1)S(1)} collective-permute-done((bf16[72,1024]{1,0:T(8,128)(2,1)S(1)}, bf16[72,1024]{1,0:T(8,128)(2,1)S(1)}, u32[]{:S(2)}, u32[]{:S(2)}) %collective-permute-start.6) | collective-permute-done | bytes 147488 | tf_op jit(solution)/shard_map/ppermute | solution.py:405
  50.2 0.8 %collective-permute-done.7.refs_2_ = bf16[72,1024]{1,0:T(8,128)(2,1)S(1)} collective-permute-done((bf16[72,1024]{1,0:T(8,128)(2,1)S(1)}, bf16[72,1024]{1,0:T(8,128)(2,1)S(1)}, u32[]{:S(2)}, u32[]{:S(2)}) %collective-permute-start.7) | collective-permute-done | bytes 147488 | tf_op jit(solution)/shard_map/ppermute | solution.py:405
  51.1 0.5 settle.1
  51.7 1.6 %collective-permute-start.9 = (bf16[16,1024]{1,0:T(8,128)(2,1)S(1)}, bf16[16,1024]{1,0:T(8,128)(2,1)S(1)}, u32[]{:S(2)}, u32[]{:S(2)}) collective-permute-start(bf16[16,1024]{1,0:T(8,128)(2,1)S(1)} %get-tuple-element.43), channel_id=1, source_target_pairs={{0,8},{4,12},{8,0},{12,4},{16,24},{20,28},{24,16},{28,20},{1,9},{5... | collective-permute-start | bytes 98312 | tf_op jit(solution)/shard_map/ppermute | solution.py:427
  53.5 1.5 %collective-permute-start.11 = (bf16[16,1024]{1,0:T(8,128)(2,1)S(1)}, bf16[16,1024]{1,0:T(8,128)(2,1)S(1)}, u32[]{:S(2)}, u32[]{:S(2)}) collective-permute-start(bf16[16,1024]{1,0:T(8,128)(2,1)S(1)} %get-tuple-element.45), channel_id=1, source_target_pairs={{0,16},{4,20},{8,24},{12,28},{16,0},{20,4},{24,8},{28,12},{1,17},{... | collective-permute-start | bytes 98312 | tf_op jit(solution)/shard_map/ppermute | solution.py:427
  55.2 2.5 %collective-permute-start.13 = (bf16[16,1024]{1,0:T(8,128)(2,1)S(1)}, bf16[16,1024]{1,0:T(8,128)(2,1)S(1)}, u32[]{:S(2)}, u32[]{:S(2)}) collective-permute-start(bf16[16,1024]{1,0:T(8,128)(2,1)S(1)} %get-tuple-element.47), channel_id=1, source_target_pairs={{0,24},{4,28},{8,16},{12,20},{16,8},{20,12},{24,0},{28,4},{1,25},{... | collective-permute-start | bytes 98312 | tf_op jit(solution)/shard_map/ppermute | solution.py:427
  57.9 0.6 collective-permute-done.12.refs_5_
  58.5 1.6 %collective-permute-done.13.refs_6_ = bf16[16,1024]{1,0:T(8,128)(2,1)S(1)} collective-permute-done((bf16[16,1024]{1,0:T(8,128)(2,1)S(1)}, bf16[16,1024]{1,0:T(8,128)(2,1)S(1)}, u32[]{:S(2)}, u32[]{:S(2)}) %collective-permute-start.13) | collective-permute-done | bytes 32800 | tf_op jit(solution)/shard_map/ppermute | solution.py:427
  60.0 1.9 %collective-permute-done.14.refs_7_ = bf16[16,1024]{1,0:T(8,128)(2,1)S(1)} collective-permute-done((bf16[16,1024]{1,0:T(8,128)(2,1)S(1)}, bf16[16,1024]{1,0:T(8,128)(2,1)S(1)}, u32[]{:S(2)}, u32[]{:S(2)}) %collective-permute-start.14) | collective-permute-done | bytes 32800 | tf_op jit(solution)/shard_map/ppermute | solution.py:427
  61.9 0.8 %widen.1 = f32[24,4,1024]{2,1,0:T(4,128)} custom-call(s32[1]{0:T(128)} %bitcast.mine_ref, bf16[16,1024]{1,0:T(8,128)(2,1)S(1)} %get-tuple-element.41.refs_0_, bf16[16,1024]{1,0:T(8,128)(2,1)S(1)} %collective-permute-done.8.refs_1_, bf16[16,1024]{1,0:T(8,128)(2,1)S(1)} %collective-permute-done.9.refs_2_, ...), custom_call_target="tpu_custom_call" | custom-call | tf_op jit(solution)/shard_map/widen/pallas_call | solution.py:383
  (31 shorter events, 2.2 us)
Async XLA Ops:
  0.0 3.8 %copy-start.1 = (s32[1,1,18,2]{2,3,1,0:T(2,128)S(1)}, s32[1,1,18,2]{2,3,1,0:T(2,128)}, u32[]{:S(2)}) copy-start(s32[1,1,18,2]{2,3,1,0:T(2,128)} %param.6) | copy-start | bytes 436
  1.7 28.4 %copy-start = (f32[2,128]{1,0:T(2,128)S(1)}, f32[2,128]{1,0:T(2,128)}, u32[]{:S(2)}) copy-start(f32[2,128]{1,0:T(2,128)} %constant.36.clone.refs_10_) | copy-start | bytes 3076
  4.2 26.0 %collective-permute-start = (bf16[16,4224]{1,0:T(8,128)(2,1)S(1)}, bf16[16,4224]{1,0:T(8,128)(2,1)S(1)}, u32[]{:S(2)}, u32[]{:S(2)}) collective-permute-start(bf16[16,4224]{1,0:T(8,128)(2,1)S(1)} %get-tuple-element.30), channel_id=1, source_target_pairs={{0,3},{1,2},{2,1},{3,0},{4,7},{5,6},{6,5},{7,4},{8,11},{9,10},{10,... | collective-permute-start | bytes 405512 | tf_op jit(solution)/shard_map/ppermute | solution.py:405
  9.3 20.9 %collective-permute-start.1 = (bf16[16,4224]{1,0:T(8,128)(2,1)S(1)}, bf16[16,4224]{1,0:T(8,128)(2,1)S(1)}, u32[]{:S(2)}, u32[]{:S(2)}) collective-permute-start(bf16[16,4224]{1,0:T(8,128)(2,1)S(1)} %get-tuple-element.31), channel_id=1, source_target_pairs={{0,2},{1,3},{2,0},{3,1},{4,6},{5,7},{6,4},{7,5},{8,10},{9,11},{10,... | collective-permute-start | bytes 405512 | tf_op jit(solution)/shard_map/ppermute | solution.py:405
  9.3 20.9 %collective-permute-start.2 = (bf16[32,4224]{1,0:T(8,128)(2,1)S(1)}, bf16[32,4224]{1,0:T(8,128)(2,1)S(1)}, u32[]{:S(2)}, u32[]{:S(2)}) collective-permute-start(bf16[32,4224]{1,0:T(8,128)(2,1)S(1)} %get-tuple-element.33), channel_id=1, source_target_pairs={{0,1},{1,0},{2,3},{3,2},{4,5},{5,4},{6,7},{7,6},{8,9},{9,8},{10,11... | collective-permute-start | bytes 811016 | tf_op jit(solution)/shard_map/ppermute | solution.py:405
  9.9 20.2 %collective-permute-start.3 = (bf16[16,4096]{1,0:T(8,128)(2,1)S(1)}, bf16[16,4096]{1,0:T(8,128)(2,1)S(1)}, u32[]{:S(2)}, u32[]{:S(2)}) collective-permute-start(bf16[16,4096]{1,0:T(8,128)(2,1)S(1)} %get-tuple-element.34), channel_id=1, source_target_pairs={{0,2},{1,3},{2,0},{3,1},{4,6},{5,7},{6,4},{7,5},{8,10},{9,11},{10,... | collective-permute-start | bytes 393224 | tf_op jit(solution)/shard_map/ppermute | solution.py:405
  12.2 17.9 %collective-permute-start.4 = (bf16[16,4096]{1,0:T(8,128)(2,1)S(1)}, bf16[16,4096]{1,0:T(8,128)(2,1)S(1)}, u32[]{:S(2)}, u32[]{:S(2)}) collective-permute-start(bf16[16,4096]{1,0:T(8,128)(2,1)S(1)} %get-tuple-element.35), channel_id=1, source_target_pairs={{0,3},{1,2},{2,1},{3,0},{4,7},{5,6},{6,5},{7,4},{8,11},{9,10},{10,... | collective-permute-start | bytes 393224 | tf_op jit(solution)/shard_map/ppermute | solution.py:405
  34.8 16.2 %copy-start.2 = (s32[1,1,18,1]{2,3,1,0:T(1,128)S(1)}, s32[1,1,18,1]{2,3,1,0:T(1,128)}, u32[]{:S(2)}) copy-start(s32[1,1,18,1]{2,3,1,0:T(1,128)} %param.7) | copy-start | bytes 220
  34.8 9.1 %collective-permute-start.5 = (bf16[72,1024]{1,0:T(8,128)(2,1)S(1)}, bf16[72,1024]{1,0:T(8,128)(2,1)S(1)}, u32[]{:S(2)}, u32[]{:S(2)}) collective-permute-start(bf16[72,1024]{1,0:T(8,128)(2,1)S(1)} %get-tuple-element.37), channel_id=1, source_target_pairs={{0,3},{1,2},{2,1},{3,0},{4,7},{5,6},{6,5},{7,4},{8,11},{9,10},{10,... | collective-permute-start | bytes 442376 | tf_op jit(solution)/shard_map/ppermute | solution.py:405
  37.6 12.6 %collective-permute-start.6 = (bf16[72,1024]{1,0:T(8,128)(2,1)S(1)}, bf16[72,1024]{1,0:T(8,128)(2,1)S(1)}, u32[]{:S(2)}, u32[]{:S(2)}) collective-permute-start(bf16[72,1024]{1,0:T(8,128)(2,1)S(1)} %get-tuple-element.38), channel_id=1, source_target_pairs={{0,2},{1,3},{2,0},{3,1},{4,6},{5,7},{6,4},{7,5},{8,10},{9,11},{10,... | collective-permute-start | bytes 442376 | tf_op jit(solution)/shard_map/ppermute | solution.py:405
  43.4 7.7 %collective-permute-start.7 = (bf16[72,1024]{1,0:T(8,128)(2,1)S(1)}, bf16[72,1024]{1,0:T(8,128)(2,1)S(1)}, u32[]{:S(2)}, u32[]{:S(2)}) collective-permute-start(bf16[72,1024]{1,0:T(8,128)(2,1)S(1)} %get-tuple-element.39), channel_id=1, source_target_pairs={{0,1},{1,0},{2,3},{3,2},{4,5},{5,4},{6,7},{7,6},{8,9},{9,8},{10,11... | collective-permute-start | bytes 442376 | tf_op jit(solution)/shard_map/ppermute | solution.py:405
  51.6 3.6 %collective-permute-start.8 = (bf16[16,1024]{1,0:T(8,128)(2,1)S(1)}, bf16[16,1024]{1,0:T(8,128)(2,1)S(1)}, u32[]{:S(2)}, u32[]{:S(2)}) collective-permute-start(bf16[16,1024]{1,0:T(8,128)(2,1)S(1)} %get-tuple-element.42), channel_id=1, source_target_pairs={{0,4},{4,0},{8,12},{12,8},{16,20},{20,16},{24,28},{28,24},{1,5},{5... | collective-permute-start | bytes 98312 | tf_op jit(solution)/shard_map/ppermute | solution.py:427
  51.7 6.0 %collective-permute-start.9 = (bf16[16,1024]{1,0:T(8,128)(2,1)S(1)}, bf16[16,1024]{1,0:T(8,128)(2,1)S(1)}, u32[]{:S(2)}, u32[]{:S(2)}) collective-permute-start(bf16[16,1024]{1,0:T(8,128)(2,1)S(1)} %get-tuple-element.43), channel_id=1, source_target_pairs={{0,8},{4,12},{8,0},{12,4},{16,24},{20,28},{24,16},{28,20},{1,9},{5... | collective-permute-start | bytes 98312 | tf_op jit(solution)/shard_map/ppermute | solution.py:427
  53.2 4.7 %collective-permute-start.10 = (bf16[16,1024]{1,0:T(8,128)(2,1)S(1)}, bf16[16,1024]{1,0:T(8,128)(2,1)S(1)}, u32[]{:S(2)}, u32[]{:S(2)}) collective-permute-start(bf16[16,1024]{1,0:T(8,128)(2,1)S(1)} %get-tuple-element.44), channel_id=1, source_target_pairs={{0,12},{4,8},{8,4},{12,0},{16,28},{20,24},{24,20},{28,16},{1,13},{... | collective-permute-start | bytes 98312 | tf_op jit(solution)/shard_map/ppermute | solution.py:427
  53.5 4.4 %collective-permute-start.11 = (bf16[16,1024]{1,0:T(8,128)(2,1)S(1)}, bf16[16,1024]{1,0:T(8,128)(2,1)S(1)}, u32[]{:S(2)}, u32[]{:S(2)}) collective-permute-start(bf16[16,1024]{1,0:T(8,128)(2,1)S(1)} %get-tuple-element.45), channel_id=1, source_target_pairs={{0,16},{4,20},{8,24},{12,28},{16,0},{20,4},{24,8},{28,12},{1,17},{... | collective-permute-start | bytes 98312 | tf_op jit(solution)/shard_map/ppermute | solution.py:427
  55.1 3.4 %collective-permute-start.12 = (bf16[16,1024]{1,0:T(8,128)(2,1)S(1)}, bf16[16,1024]{1,0:T(8,128)(2,1)S(1)}, u32[]{:S(2)}, u32[]{:S(2)}) collective-permute-start(bf16[16,1024]{1,0:T(8,128)(2,1)S(1)} %get-tuple-element.46), channel_id=1, source_target_pairs={{0,20},{4,16},{8,28},{12,24},{16,4},{20,0},{24,12},{28,8},{1,21},{... | collective-permute-start | bytes 98312 | tf_op jit(solution)/shard_map/ppermute | solution.py:427
  55.2 4.8 %collective-permute-start.13 = (bf16[16,1024]{1,0:T(8,128)(2,1)S(1)}, bf16[16,1024]{1,0:T(8,128)(2,1)S(1)}, u32[]{:S(2)}, u32[]{:S(2)}) collective-permute-start(bf16[16,1024]{1,0:T(8,128)(2,1)S(1)} %get-tuple-element.47), channel_id=1, source_target_pairs={{0,24},{4,28},{8,16},{12,20},{16,8},{20,12},{24,0},{28,4},{1,25},{... | collective-permute-start | bytes 98312 | tf_op jit(solution)/shard_map/ppermute | solution.py:427
  57.7 4.2 %collective-permute-start.14 = (bf16[16,1024]{1,0:T(8,128)(2,1)S(1)}, bf16[16,1024]{1,0:T(8,128)(2,1)S(1)}, u32[]{:S(2)}, u32[]{:S(2)}) collective-permute-start(bf16[16,1024]{1,0:T(8,128)(2,1)S(1)} %get-tuple-element.48), channel_id=1, source_target_pairs={{0,28},{4,24},{8,20},{12,16},{16,12},{20,8},{24,4},{28,0},{1,29},{... | collective-permute-start | bytes 98312 | tf_op jit(solution)/shard_map/ppermute | solution.py:427

commit v2 on v1

--- a/solution.py
+++ b/solution.py
@@ -19,15 +19,14 @@
 VMEM_LIMIT = 24 * 1024 * 1024
 HALF = LAGS // 2
 ROOM = 4
-HALVES = 2
-JOINT = 1
-
-
-def whiten_kernel(parts, second, place_ref, spec_ref, *refs):
+WAVES = 2
+
+
+def whiten_kernel(parts, place_ref, spec_ref, pairs_ref, *out_refs):
     blocks = F // LANES
     each = blocks // parts
+    share = each // WAVES
     place = place_ref[0]
-    out_refs = list(refs[-parts:])
 
     def values(start):
         span = pl.ds(start, LANES)
@@ -35,30 +34,23 @@
         im = spec_ref[1, :, span].astype(jnp.float32)
         return re, im, re * re + im * im
 
-    if second:
-        deep = spec_ref.shape[1]
-        joint = out_refs[JOINT]
-        joint[:deep, : each * 2 * LANES] = refs[0][...]
-        joint[:deep, each * 2 * LANES :] = jnp.zeros((deep, LANES), jnp.bfloat16)
-        out_refs[JOINT] = joint.at[deep:]
-        pairs_ref = refs[1]
-        shape = (spec_ref.shape[1], LANES)
-        line = lax.broadcasted_iota(jnp.int32, shape, 0)
-        spare = jnp.zeros((1, LANES - NB_SRC), jnp.int32)
-        wide = lambda row: jnp.broadcast_to(jnp.concatenate([row, spare], axis=1), shape)
-        notes = jnp.where(line == 0, wide(pairs_ref[0:1]), wide(pairs_ref[1:2]))
-        notes = notes.astype(jnp.float32).astype(jnp.bfloat16)
-        for out_ref in out_refs:
-            out_ref[:, each * 2 * LANES :] = notes
+    shape = (spec_ref.shape[1], LANES)
+    line = lax.broadcasted_iota(jnp.int32, shape, 0)
+    spare = jnp.zeros((1, LANES - NB_SRC), jnp.int32)
+    wide = lambda row: jnp.broadcast_to(jnp.concatenate([row, spare], axis=1), shape)
+    notes = jnp.where(line == 0, wide(pairs_ref[0:1]), wide(pairs_ref[1:2]))
+    notes = notes.astype(jnp.float32).astype(jnp.bfloat16)
+    for out_ref in out_refs[:parts]:
+        out_ref[:, share * 2 * LANES :] = notes
     sums = [None] * 4
     for k in range(blocks):
         power = values(k * LANES)[2]
         sums[k % 4] = power if k < 4 else sums[k % 4] + power
     total = jnp.sum((sums[0] + sums[1]) + (sums[2] + sums[3]), axis=1, keepdims=True)
     level = 0.1 * (total * (1.0 / F) + 1e-05)
-    for d, out_ref in enumerate(out_refs):
-        first = jnp.bitwise_xor(place, d) * each
-        for k in range(each):
+    for index, out_ref in enumerate(out_refs):
+        first = jnp.bitwise_xor(place, index % parts) * each + index // parts * share
+        for k in range(share):
             re, im, power = values(pl.multiple_of((first + k) * LANES, LANES))
             scale = lax.rsqrt(power + level)
             at = k * 2 * LANES
@@ -66,26 +58,25 @@
             out_ref[:, at + LANES : at + 2 * LANES] = (im * scale).astype(jnp.bfloat16)
 
 
-def whiten(spectra, others, place, parts, second):
+def whiten(spectra, pairs, place, parts):
     rows = spectra.shape[0] * WINDOWS
     planes = jnp.transpose(spectra.reshape(rows, 2, F), (1, 0, 2))
-    width = 2 * F // parts
-    shapes = [(rows, width + LANES if second else width)] * parts
-    if second:
-        shapes[JOINT] = (HALVES * rows, width + LANES)
+    width = 2 * F // parts // WAVES
+    shapes = [(rows, width + LANES)] * parts + [(rows, width)] * parts * (WAVES - 1)
     whole = lambda array: pl.BlockSpec(array.shape, lambda i, place: (0,) * array.ndim)
-    return list(pl.pallas_call(
-        functools.partial(whiten_kernel, parts, second),
+    outs = pl.pallas_call(
+        functools.partial(whiten_kernel, parts),
         grid_spec=pltpu.PrefetchScalarGridSpec(
             num_scalar_prefetch=1,
             grid=(1,),
-            in_specs=[whole(array) for array in [planes, *others]],
+            in_specs=[whole(array) for array in [planes, pairs]],
             out_specs=[pl.BlockSpec(shape, lambda i, place: (0, 0)) for shape in shapes],
         ),
         out_shape=[jax.ShapeDtypeStruct(shape, jnp.bfloat16) for shape in shapes],
         compiler_params=pltpu.CompilerParams(vmem_limit_bytes=VMEM_LIMIT),
         name="whiten",
-    )(place[None], planes, *others))
+    )(place[None], planes, pairs)
+    return list(outs[:parts]), list(outs[parts:])
 
 
 def table_kernel(first_ref, hi_cos_ref, hi_sin_ref, mid_cos_ref, mid_sin_ref, lo_cos_ref, lo_sin_ref, out_ref, cos, sin):
@@ -160,7 +151,7 @@
     return hit.astype(jnp.float32).astype(jnp.bfloat16)
 
 
-def choose_rows(parts, lists, place, packed, rows_ref):
+def choose_rows(lists, place, packed, rows_ref):
     height = rows_ref.shape[1]
     count = rows_ref.shape[0] // (2 * BLK * WINDOWS)
     deep = packed.shape[0] // lists
@@ -179,30 +170,25 @@
     across = iota((count, height), 1)
     picks = []
     for block in (column(0), column(1)):
-        source = jnp.bitwise_xor(lax.shift_right_logical(block, (HALVES * blocks).bit_length() - 1), place)
-        half = jnp.bitwise_and(lax.shift_right_logical(block, blocks.bit_length() - 1), HALVES - 1)
-        inner = jnp.bitwise_and(block, blocks - 1)
-        first = (half * parts + source) * deep + inner * (BLK * WINDOWS)
+        first = jnp.bitwise_xor(block, place * blocks) * (BLK * WINDOWS)
         for offset in range(BLK * WINDOWS):
             picks.append((across == first + offset).astype(jnp.float32))
     rows_ref[...] = jnp.concatenate(picks, axis=0).astype(jnp.bfloat16)
 
 
-def corr_kernel(per_step, parts, lists, place, *refs):
-    refs = list(refs)
-    note_refs, panel_refs, refs = refs[:lists], refs[lists : lists + 2 * parts - 1], refs[lists + 2 * parts - 1 :]
-    (table_ref, ends_ref), out_refs, (total, edge, rows_ref) = refs[:2], refs[2:-3], refs[-3:]
-    deep = panel_refs[0].shape[0]
-    panel_refs.insert(parts + JOINT, panel_refs[JOINT].at[deep:])
-    panel_refs[JOINT] = panel_refs[JOINT].at[:deep]
+def corr_kernel(per_step, parts, lists, wave, place, *refs):
+    panel_refs, (table_ref, ends_ref), refs = refs[:parts], refs[parts : parts + 2], refs[parts + 2 :]
     step = pl.program_id(0)
+    if wave:
+        (total_in, edge_in, rows_ref), out_refs, (total, edge) = refs[:3], refs[3:-2], refs[-2:]
+    else:
+        note_refs, (total, edge, rows_ref) = refs[:lists], refs[lists:]
+
+        @pl.when(step == 0)
+        def prepare():
+            choose_rows(lists, place[0], jnp.concatenate([ref[...] for ref in note_refs]), rows_ref)
+
     count = total.shape[0] // PAIRS
-
-    @pl.when(step == 0)
-    def prepare():
-        packed = jnp.concatenate([ref[ref.shape[0] - deep :] for ref in note_refs])
-        choose_rows(parts, lists, place[0], packed, rows_ref)
-
     panel = jnp.concatenate([ref[...] for ref in panel_refs])
     chosen = jnp.dot(rows_ref[...], panel, preferred_element_type=jnp.float32)
 
@@ -233,7 +219,7 @@
         real = jnp.concatenate(real, axis=0)
         imag = jnp.concatenate(imag, axis=0)
         ends = ends_ref[0:1]
-        if i == 0:
+        if i == 0 and wave == 0:
             ends = jnp.where(first_bin, 0.5 * ends, ends)
         edge_part = edge_part + (real * ends + imag * ends_ref[1:2])
         reals.append(real.astype(jnp.bfloat16))
@@ -248,15 +234,18 @@
 
     @pl.when(step == 0)
     def start():
-        total[:, :HALF] = even
-        total[:, HALF:] = odd
-        edge[...] = edge_part
+        total[:, :HALF] = total_in[:, :HALF] + even if wave else even
+        total[:, HALF:] = total_in[:, HALF:] + odd if wave else odd
+        edge[...] = edge_in[...] + edge_part if wave else edge_part
 
     @pl.when(step > 0)
     def add():
         total[:, :HALF] += even
         total[:, HALF:] += odd
         edge[...] += edge_part
+
+    if wave < WAVES - 1:
+        return
 
     @pl.when(step == pl.num_programs(0) - 1)
     def finish():
@@ -280,40 +269,47 @@
             out_ref[...] = rows[i * each : (i + 1) * each].astype(jnp.bfloat16)
 
 
-def correlate(panels, table, place, parts, wanted):
+def correlate(panels, table, place, parts, wanted, wave, before):
     per_step = 4
     span = per_step * 2 * LANES
-    deep = panels[0].shape[0]
-    steps = 2 * table.shape[0] // span
+    rows = panels[0].shape[0]
+    steps = 2 * table.shape[0] // span // WAVES
     lists = len(wanted)
     count = -(-lists * NB_SRC // 8) * 8
     each = NB_SRC * PAIRS
-    noted = panels[parts:]
-    noted.insert(JOINT, panels[JOINT])
     turn = np.arange(LANES) * (np.pi / 16)
     ends = np.stack([np.cos(turn), np.sin(turn)]) * (2.0 / np.sqrt(F))
+    sums = [
+        jax.ShapeDtypeStruct((count * PAIRS, LAGS), jnp.float32),
+        jax.ShapeDtypeStruct((count * PAIRS, LANES), jnp.float32),
+    ]
+    chosen = jax.ShapeDtypeStruct((2 * BLK * WINDOWS * count, rows * parts), jnp.bfloat16)
+    whole = lambda array: pl.BlockSpec(array.shape, lambda i, place: (0, 0))
+    if wave:
+        extra = before
+        extra_specs = [whole(array) for array in before]
+        outs = [jax.ShapeDtypeStruct((each, LAGS), jnp.bfloat16)] * lists
+        scratch = [pltpu.VMEM(array.shape, array.dtype) for array in sums]
+    else:
+        extra = [panels[d] for d in wanted]
+        extra_specs = [pl.BlockSpec((rows, LANES), lambda i, place: (0, steps * span // LANES))] * lists
+        outs = [*sums, chosen]
+        scratch = []
     return pl.pallas_call(
-        functools.partial(corr_kernel, per_step, parts, lists),
+        functools.partial(corr_kernel, per_step, parts, lists, wave),
         grid_spec=pltpu.PrefetchScalarGridSpec(
             num_scalar_prefetch=1,
             grid=(steps,),
             in_specs=[
-                pl.BlockSpec((noted[d].shape[0], LANES), lambda i, place: (0, steps * span // LANES))
-                for d in wanted
-            ]
-            + [pl.BlockSpec((array.shape[0], span), lambda i, place: (0, i)) for array in panels]
-            + [
-                pl.BlockSpec((span // 2, LAGS), lambda i, place: (i, 0)),
+                *[pl.BlockSpec((rows, span), lambda i, place: (0, i))] * parts,
+                pl.BlockSpec((span // 2, LAGS), lambda i, place: (i + wave * steps, 0)),
                 pl.BlockSpec((2, LANES), lambda i, place: (0, 0)),
+                *extra_specs,
             ],
-            out_specs=[pl.BlockSpec((each, LAGS), lambda i, place: (0, 0))] * lists,
-            scratch_shapes=[
-                pltpu.VMEM((count * PAIRS, LAGS), jnp.float32),
-                pltpu.VMEM((count * PAIRS, LANES), jnp.float32),
-                pltpu.VMEM((2 * BLK * WINDOWS * count, deep * parts * HALVES), jnp.bfloat16),
-            ],
-        ),
-        out_shape=[jax.ShapeDtypeStruct((each, LAGS), jnp.bfloat16)] * lists,
+            out_specs=[whole(array) for array in outs],
+            scratch_shapes=scratch,
+        ),
+        out_shape=outs,
         compiler_params=pltpu.CompilerParams(vmem_limit_bytes=VMEM_LIMIT),
         cost_estimate=pl.CostEstimate(
             flops=count * PAIRS * steps * span * LAGS,
@@ -321,7 +317,7 @@
             transcendentals=0,
         ),
         name="correlate",
-    )(place[None], *[noted[d] for d in wanted], *panels, table, jnp.asarray(ends, jnp.float32))
+    )(place[None], *panels, table, jnp.asarray(ends, jnp.float32), *extra)
 
 
 def settle_kernel(groups, mine_ref, owners_ref, *refs):
@@ -399,27 +395,27 @@
     parts = lax.axis_size("chan")
     place = lax.axis_index("chan")
     chunks = F // LANES // parts
-    each = spectra.shape[0] // HALVES
 
     def swap(array, d):
         return lax.ppermute(array, "chan", [(i, i ^ d) for i in range(parts)])
 
-    first = whiten(spectra[:each], [], place, parts, False)
-    apart = [d for d in reversed(range(1, parts)) if d != JOINT]
-    spectra, ready = lax.optimization_barrier((spectra, first[JOINT]))
-    for d in apart:
-        first[d] = swap(first[d], d)
-    second = whiten(spectra[each:], [ready, pair_blocks[0, 0].T], place, parts, True)
-    for d in apart:
-        second[d] = swap(second[d], d)
-    first[JOINT] = swap(second.pop(JOINT), JOINT)
-    panels = first + second
-
+    def exchange(panels):
+        moved = {d: swap(panels[d], d) for d in reversed(range(1, parts))}
+        return panels[:1] + [moved[d] for d in range(1, parts)]
+
+    first, second = whiten(spectra, pair_blocks[0, 0].T, place, parts)
+    first = exchange(first)
     table = tables(place, chunks)
+    table, second = lax.optimization_barrier((table, second))
+    second = exchange(second)
+
     order = list(reversed(range(parts)))
+    halves = (order[: parts // 2], order[parts // 2 :])
+    sums = [correlate(first, table, place, parts, wanted, 0, None) for wanted in halves]
+    second, sums = lax.optimization_barrier((second, sums))
     partials = []
-    for wanted in (order[: parts // 2], order[parts // 2 :]):
-        for d, rows in zip(wanted, correlate(panels, table, place, parts, wanted)):
+    for wanted, before in zip(halves, sums):
+        for d, rows in zip(wanted, correlate(second, table, place, parts, wanted, 1, before)):
             partials.append(swap(rows, d) if d else rows)
     mine = lax.axis_index("grp")
     pieces = settle(owners[0, 0].T, partials, mine, groups)

time: 62.9 us -> 59.1 us (0.940)
  waiting for transfers between devices: 25.7 us -> 22.8 us
  local copies, waits for them, and re-layouts: 3.48 us -> 2.51 us
  Pallas kernels: 12.5 us -> 11.7 us
  starting transfers between devices: 20.4 us -> 21.2 us
    ppermute x8 -> x9, waiting for transfers between devices: 21.7 us -> 18.8 us  [swap(): return lax.ppermute(array, 'chan', [(i, i ^ d) for i in range(parts)])]
    slice x2 -> x0, local copies, waits for them, and re-layouts: 2.87 us -> none  [the longest x1 1.44 us: local(): first = whiten(spectra[:each], [], place, parts, False)]
    reshape x2 -> x1, local copies, waits for them, and re-layouts: 0.59 us -> 1.82 us  [whiten(): planes = jnp.transpose(spectra.reshape(rows, 2, F), (1, 0, 2))]
    ppermute x8 -> x9, starting transfers between devices: 14 us -> 14.9 us  [swap(): return lax.ppermute(array, 'chan', [(i, i ^ d) for i in range(parts)])]
    pallas_call x4 -> x5, Pallas kernels: 9.87 us -> 9.1 us  [the longest x4 8.48 us: correlate(): pl.pallas_call(functools.partial(corr_kernel, per_step, parts, lists, wav...]
    unnamed x6, local copies, waits for them, and re-layouts: 0.02 us -> 0.68 us
  transfers between devices with their start and end apart: 15 -> 16, of which waited for: 6 -> 7; matrix products, arithmetic and copies ran while one was open for 1% -> 1% of each run, Pallas kernels for 9% -> 13%
where the time goes in v2:
time: 59.1 us; the launch traced here: 58.9 us
  waiting for transfers between devices  22.8 us (39%)
  starting transfers between devices  21.2 us (36%)
  Pallas kernels  11.7 us (20%)
  local copies, waits for them, and re-layouts  2.51 us (4%)
    ppermute x9, waiting for transfers between devices, swap(): return lax.ppermute(array, 'chan', [(i, i ^ d) for i in range(parts)])  18.8 us
    ppermute x9, starting transfers between devices, swap(): return lax.ppermute(array, 'chan', [(i, i ^ d) for i in range(parts)])  14.9 us
    pallas_call x4, Pallas kernels, correlate(): pl.pallas_call(functools.partial(corr_kernel, per_step, parts, lists, wav...  8.48 us
    ppermute x7, starting transfers between devices, local(): lax.ppermute(pieces[m], 'grp', [(i, i ^ m) for i in range(groups)])  6.32 us
    ppermute x7, waiting for transfers between devices, local(): lax.ppermute(pieces[m], 'grp', [(i, i ^ m) for i in range(groups)])  4 us
    reshape x1, local copies, waits for them, and re-layouts, whiten(): planes = jnp.transpose(spectra.reshape(rows, 2, F), (1, 0, 2))  1.82 us
    pallas_call x1, Pallas kernels, tables(): pl.pallas_call(table_kernel, grid_spec=pltpu.PrefetchScalarGridSpec(num_s...  1.33 us
  transfers between devices with their start and end apart: 16, of which 7 were waited for; matrix products, arithmetic and copies ran while one was open for 1% of the time, Pallas kernels for 13%

profile of v2, /device:TPU:0, one launch (start us, length us, event | category | flops | bytes accessed | tf_op | source)
XLA Modules:
  0.0 58.9 jit_solution(16704366840226099528)
XLA Ops:
  0.0 1.8 %copy.11 = bf16[32,2,8192]{2,0,1:T(8,128)(2,1)S(1)} copy(bf16[32,2,8192]{2,1,0:T(2,128)(2,1)} %bitcast.14) | data formatting | bytes 2097152 | tf_op jit(solution)/shard_map/reshape | solution.py:63
  1.8 0.7 %copy-done.1 = s32[1,1,18,2]{2,3,1,0:T(2,128)S(1)} copy-done((s32[1,1,18,2]{2,3,1,0:T(2,128)S(1)}, s32[1,1,18,2]{2,3,1,0:T(2,128)}, u32[]{:S(2)}) %copy-start.1) | copy-done | bytes 168
  3.1 3.1 %collective-permute-start.3 = (bf16[32,2176]{1,0:T(8,128)(2,1)S(1)}, bf16[32,2176]{1,0:T(8,128)(2,1)S(1)}, u32[]{:S(2)}, u32[]{:S(2)}) collective-permute-start(bf16[32,2176]{1,0:T(8,128)(2,1)S(1)} %get-tuple-element.55), channel_id=1, source_target_pairs={{0,1},{1,0},{2,3},{3,2},{4,5},{5,4},{6,7},{7,6},{8,9},{9,8},{10,11... | collective-permute-start | bytes 417800 | tf_op jit(solution)/shard_map/ppermute | solution.py:400
  6.2 2.6 %collective-permute-start.4 = (bf16[32,2176]{1,0:T(8,128)(2,1)S(1)}, bf16[32,2176]{1,0:T(8,128)(2,1)S(1)}, u32[]{:S(2)}, u32[]{:S(2)}) collective-permute-start(bf16[32,2176]{1,0:T(8,128)(2,1)S(1)} %get-tuple-element.56), channel_id=1, source_target_pairs={{0,2},{1,3},{2,0},{3,1},{4,6},{5,7},{6,4},{7,5},{8,10},{9,11},{10,... | collective-permute-start | bytes 417800 | tf_op jit(solution)/shard_map/ppermute | solution.py:400
  9.4 1.3 %tables.1.refs_4_ = bf16[2048,1024]{1,0:T(8,128)(2,1)S(1)} custom-call(s32[1]{0:T(128)} %bitcast.2.first_ref.place_ref.place, f32[16,512]{1,0:T(8,128)S(1)} %get-tuple-element.93.hi_cos_ref, f32[16,512]{1,0:T(8,128)S(1)} %get-tuple-element.88.hi_sin_ref, f32[16,512]{1,0:T(8,128)S(1)} %get-tuple-element.94.mid_cos_ref, ...), custom_call_target="tpu_custom_call" | custom-call | flops 8388608 | bytes 4194304 | tf_op jit(solution)/shard_map/tables/pallas_call | solution.py:128
  10.7 1.0 %collective-permute-start = (bf16[32,2048]{1,0:T(8,128)(2,1)S(1)}, bf16[32,2048]{1,0:T(8,128)(2,1)S(1)}, u32[]{:S(2)}, u32[]{:S(2)}) collective-permute-start(bf16[32,2048]{1,0:T(8,128)(2,1)S(1)} %get-tuple-element.51), channel_id=1, source_target_pairs={{0,1},{1,0},{2,3},{3,2},{4,5},{5,4},{6,7},{7,6},{8,9},{9,8},{10,11... | collective-permute-start | bytes 393224 | tf_op jit(solution)/shard_map/ppermute | solution.py:400
  11.6 3.5 %collective-permute-start.1 = (bf16[32,2048]{1,0:T(8,128)(2,1)S(1)}, bf16[32,2048]{1,0:T(8,128)(2,1)S(1)}, u32[]{:S(2)}, u32[]{:S(2)}) collective-permute-start(bf16[32,2048]{1,0:T(8,128)(2,1)S(1)} %get-tuple-element.52), channel_id=1, source_target_pairs={{0,2},{1,3},{2,0},{3,1},{4,6},{5,7},{6,4},{7,5},{8,10},{9,11},{10,... | collective-permute-start | bytes 393224 | tf_op jit(solution)/shard_map/ppermute | solution.py:400
  15.4 4.3 %collective-permute-done.4.refs_2_.refs_7_ = bf16[32,2176]{1,0:T(8,128)(2,1)S(1)} collective-permute-done((bf16[32,2176]{1,0:T(8,128)(2,1)S(1)}, bf16[32,2176]{1,0:T(8,128)(2,1)S(1)}, u32[]{:S(2)}, u32[]{:S(2)}) %collective-permute-start.4) | collective-permute-done | bytes 139296 | tf_op jit(solution)/shard_map/ppermute | solution.py:400
  19.7 2.2 %correlate.5 = (f32[160,1024]{1,0:T(8,128)S(1)}, f32[160,128]{1,0:T(8,128)S(1)}, bf16[320,128]{1,0:T(8,128)(2,1)S(1)}) custom-call(s32[1]{0:T(128)} %bitcast.2.first_ref.place_ref.place, bf16[32,2176]{1,0:T(8,128)(2,1)S(1)} %get-tuple-element.54.refs_0_.refs_7_, bf16[32,2176]{1,0:T(8,128)(2,1)S(1)} %collective-permute-done.3.refs_1_.refs_6_, ...), custom_call_target="tpu_custom_call" | custom-call | flops 335544320 | bytes 2097152 | tf_op jit(solution)/shard_map/correlate/pallas_call | solution.py:298
  21.9 2.2 %correlate.4 = (f32[160,1024]{1,0:T(8,128)S(1)}, f32[160,128]{1,0:T(8,128)S(1)}, bf16[320,128]{1,0:T(8,128)(2,1)S(1)}) custom-call(s32[1]{0:T(128)} %bitcast.2.first_ref.place_ref.place, bf16[32,2176]{1,0:T(8,128)(2,1)S(1)} %get-tuple-element.54.refs_0_.refs_7_, bf16[32,2176]{1,0:T(8,128)(2,1)S(1)} %collective-permute-done.3.refs_1_.refs_6_, ...), custom_call_target="tpu_custom_call" | custom-call | flops 335544320 | bytes 2097152 | tf_op jit(solution)/shard_map/correlate/pallas_call | solution.py:298
  24.1 7.0 %collective-permute-done.1.refs_2_ = bf16[32,2048]{1,0:T(8,128)(2,1)S(1)} collective-permute-done((bf16[32,2048]{1,0:T(8,128)(2,1)S(1)}, bf16[32,2048]{1,0:T(8,128)(2,1)S(1)}, u32[]{:S(2)}, u32[]{:S(2)}) %collective-permute-start.1) | collective-permute-done | bytes 131104 | tf_op jit(solution)/shard_map/ppermute | solution.py:400
  31.1 2.1 %correlate.6 = (bf16[72,1024]{1,0:T(8,128)(2,1)S(1)}, bf16[72,1024]{1,0:T(8,128)(2,1)S(1)}) custom-call(s32[1]{0:T(128)} %bitcast.2.first_ref.place_ref.place, bf16[32,2048]{1,0:T(8,128)(2,1)S(1)} %get-tuple-element.65.refs_0_, bf16[32,2048]{1,0:T(8,128)(2,1)S(1)} %collective-permute-done.refs_1_, bf16[32,2048]{1,0:T(8,128)(2,1)S(1)} %collective-permute-done.1.refs_2_, ...), custom_call_target="tpu_custom_call" | custom-call | flops 335544320 | bytes 2097152 | tf_op jit(solution)/shard_map/correlate/pallas_call | solution.py:298
  33.2 2.4 %collective-permute-start.6 = (bf16[72,1024]{1,0:T(8,128)(2,1)S(1)}, bf16[72,1024]{1,0:T(8,128)(2,1)S(1)}, u32[]{:S(2)}, u32[]{:S(2)}) collective-permute-start(bf16[72,1024]{1,0:T(8,128)(2,1)S(1)} %get-tuple-element.72), channel_id=1, source_target_pairs={{0,3},{1,2},{2,1},{3,0},{4,7},{5,6},{6,5},{7,4},{8,11},{9,10},{10,... | collective-permute-start | bytes 442376 | tf_op jit(solution)/shard_map/ppermute | solution.py:400
  35.6 1.3 %collective-permute-start.7 = (bf16[72,1024]{1,0:T(8,128)(2,1)S(1)}, bf16[72,1024]{1,0:T(8,128)(2,1)S(1)}, u32[]{:S(2)}, u32[]{:S(2)}) collective-permute-start(bf16[72,1024]{1,0:T(8,128)(2,1)S(1)} %get-tuple-element.73), channel_id=1, source_target_pairs={{0,2},{1,3},{2,0},{3,1},{4,6},{5,7},{6,4},{7,5},{8,10},{9,11},{10,... | collective-permute-start | bytes 442376 | tf_op jit(solution)/shard_map/ppermute | solution.py:400
  36.9 2.1 %correlate.7 = (bf16[72,1024]{1,0:T(8,128)(2,1)S(1)}, bf16[72,1024]{1,0:T(8,128)(2,1)S(1)}) custom-call(s32[1]{0:T(128)} %bitcast.2.first_ref.place_ref.place, bf16[32,2048]{1,0:T(8,128)(2,1)S(1)} %get-tuple-element.65.refs_0_, bf16[32,2048]{1,0:T(8,128)(2,1)S(1)} %collective-permute-done.refs_1_, bf16[32,2048]{1,0:T(8,128)(2,1)S(1)} %collective-permute-done.1.refs_2_, ...), custom_call_target="tpu_custom_call" | custom-call | flops 335544320 | bytes 2097152 | tf_op jit(solution)/shard_map/correlate/pallas_call | solution.py:298
  38.9 0.8 %collective-permute-start.8 = (bf16[72,1024]{1,0:T(8,128)(2,1)S(1)}, bf16[72,1024]{1,0:T(8,128)(2,1)S(1)}, u32[]{:S(2)}, u32[]{:S(2)}) collective-permute-start(bf16[72,1024]{1,0:T(8,128)(2,1)S(1)} %get-tuple-element.77), channel_id=1, source_target_pairs={{0,1},{1,0},{2,3},{3,2},{4,5},{5,4},{6,7},{7,6},{8,9},{9,8},{10,11... | collective-permute-start | bytes 442376 | tf_op jit(solution)/shard_map/ppermute | solution.py:400
  39.8 2.1 %collective-permute-done.6.refs_0_ = bf16[72,1024]{1,0:T(8,128)(2,1)S(1)} collective-permute-done((bf16[72,1024]{1,0:T(8,128)(2,1)S(1)}, bf16[72,1024]{1,0:T(8,128)(2,1)S(1)}, u32[]{:S(2)}, u32[]{:S(2)}) %collective-permute-start.6) | collective-permute-done | bytes 147488 | tf_op jit(solution)/shard_map/ppermute | solution.py:400
  41.8 5.4 %collective-permute-done.7.refs_1_ = bf16[72,1024]{1,0:T(8,128)(2,1)S(1)} collective-permute-done((bf16[72,1024]{1,0:T(8,128)(2,1)S(1)}, bf16[72,1024]{1,0:T(8,128)(2,1)S(1)}, u32[]{:S(2)}, u32[]{:S(2)}) %collective-permute-start.7) | collective-permute-done | bytes 147488 | tf_op jit(solution)/shard_map/ppermute | solution.py:400
  47.9 1.6 %collective-permute-start.10 = (bf16[16,1024]{1,0:T(8,128)(2,1)S(1)}, bf16[16,1024]{1,0:T(8,128)(2,1)S(1)}, u32[]{:S(2)}, u32[]{:S(2)}) collective-permute-start(bf16[16,1024]{1,0:T(8,128)(2,1)S(1)} %get-tuple-element.81), channel_id=1, source_target_pairs={{0,8},{4,12},{8,0},{12,4},{16,24},{20,28},{24,16},{28,20},{1,9},{5... | collective-permute-start | bytes 98312 | tf_op jit(solution)/shard_map/ppermute | solution.py:423
  49.7 1.5 %collective-permute-start.12 = (bf16[16,1024]{1,0:T(8,128)(2,1)S(1)}, bf16[16,1024]{1,0:T(8,128)(2,1)S(1)}, u32[]{:S(2)}, u32[]{:S(2)}) collective-permute-start(bf16[16,1024]{1,0:T(8,128)(2,1)S(1)} %get-tuple-element.83), channel_id=1, source_target_pairs={{0,16},{4,20},{8,24},{12,28},{16,0},{20,4},{24,8},{28,12},{1,17},{... | collective-permute-start | bytes 98312 | tf_op jit(solution)/shard_map/ppermute | solution.py:423
  51.4 2.4 %collective-permute-start.14 = (bf16[16,1024]{1,0:T(8,128)(2,1)S(1)}, bf16[16,1024]{1,0:T(8,128)(2,1)S(1)}, u32[]{:S(2)}, u32[]{:S(2)}) collective-permute-start(bf16[16,1024]{1,0:T(8,128)(2,1)S(1)} %get-tuple-element.85), channel_id=1, source_target_pairs={{0,24},{4,28},{8,16},{12,20},{16,8},{20,12},{24,0},{28,4},{1,25},{... | collective-permute-start | bytes 98312 | tf_op jit(solution)/shard_map/ppermute | solution.py:423
  54.7 1.6 %collective-permute-done.14.refs_6_ = bf16[16,1024]{1,0:T(8,128)(2,1)S(1)} collective-permute-done((bf16[16,1024]{1,0:T(8,128)(2,1)S(1)}, bf16[16,1024]{1,0:T(8,128)(2,1)S(1)}, u32[]{:S(2)}, u32[]{:S(2)}) %collective-permute-start.14) | collective-permute-done | bytes 32800 | tf_op jit(solution)/shard_map/ppermute | solution.py:423
  56.2 1.9 %collective-permute-done.15.refs_7_ = bf16[16,1024]{1,0:T(8,128)(2,1)S(1)} collective-permute-done((bf16[16,1024]{1,0:T(8,128)(2,1)S(1)}, bf16[16,1024]{1,0:T(8,128)(2,1)S(1)}, u32[]{:S(2)}, u32[]{:S(2)}) %collective-permute-start.15) | collective-permute-done | bytes 32800 | tf_op jit(solution)/shard_map/ppermute | solution.py:423
  58.1 0.8 %widen.1 = f32[24,4,1024]{2,1,0:T(4,128)} custom-call(s32[1]{0:T(128)} %bitcast.mine_ref, bf16[16,1024]{1,0:T(8,128)(2,1)S(1)} %get-tuple-element.79.refs_0_, bf16[16,1024]{1,0:T(8,128)(2,1)S(1)} %collective-permute-done.9.refs_1_, bf16[16,1024]{1,0:T(8,128)(2,1)S(1)} %collective-permute-done.10.refs_2_, ...), custom_call_target="tpu_custom_call" | custom-call | tf_op jit(solution)/shard_map/widen/pallas_call | solution.py:379
  (31 shorter events, 3.3 us)
Async XLA Ops:
  0.0 19.7 %copy-start = (f32[2,128]{1,0:T(2,128)S(1)}, f32[2,128]{1,0:T(2,128)}, u32[]{:S(2)}) copy-start(f32[2,128]{1,0:T(2,128)} %constant.36.clone.refs_5_) | copy-start | bytes 3076
  1.8 0.7 %copy-start.1 = (s32[1,1,18,2]{2,3,1,0:T(2,128)S(1)}, s32[1,1,18,2]{2,3,1,0:T(2,128)}, u32[]{:S(2)}) copy-start(s32[1,1,18,2]{2,3,1,0:T(2,128)} %param.8) | copy-start | bytes 436
  3.1 12.0 %collective-permute-start.3 = (bf16[32,2176]{1,0:T(8,128)(2,1)S(1)}, bf16[32,2176]{1,0:T(8,128)(2,1)S(1)}, u32[]{:S(2)}, u32[]{:S(2)}) collective-permute-start(bf16[32,2176]{1,0:T(8,128)(2,1)S(1)} %get-tuple-element.55), channel_id=1, source_target_pairs={{0,1},{1,0},{2,3},{3,2},{4,5},{5,4},{6,7},{7,6},{8,9},{9,8},{10,11... | collective-permute-start | bytes 417800 | tf_op jit(solution)/shard_map/ppermute | solution.py:400
  6.2 13.5 %collective-permute-start.4 = (bf16[32,2176]{1,0:T(8,128)(2,1)S(1)}, bf16[32,2176]{1,0:T(8,128)(2,1)S(1)}, u32[]{:S(2)}, u32[]{:S(2)}) collective-permute-start(bf16[32,2176]{1,0:T(8,128)(2,1)S(1)} %get-tuple-element.56), channel_id=1, source_target_pairs={{0,2},{1,3},{2,0},{3,1},{4,6},{5,7},{6,4},{7,5},{8,10},{9,11},{10,... | collective-permute-start | bytes 417800 | tf_op jit(solution)/shard_map/ppermute | solution.py:400
  8.8 10.9 %collective-permute-start.5 = (bf16[32,2176]{1,0:T(8,128)(2,1)S(1)}, bf16[32,2176]{1,0:T(8,128)(2,1)S(1)}, u32[]{:S(2)}, u32[]{:S(2)}) collective-permute-start(bf16[32,2176]{1,0:T(8,128)(2,1)S(1)} %get-tuple-element.57), channel_id=1, source_target_pairs={{0,3},{1,2},{2,1},{3,0},{4,7},{5,6},{6,5},{7,4},{8,11},{9,10},{10,... | collective-permute-start | bytes 417800 | tf_op jit(solution)/shard_map/ppermute | solution.py:400
  10.7 13.4 %collective-permute-start = (bf16[32,2048]{1,0:T(8,128)(2,1)S(1)}, bf16[32,2048]{1,0:T(8,128)(2,1)S(1)}, u32[]{:S(2)}, u32[]{:S(2)}) collective-permute-start(bf16[32,2048]{1,0:T(8,128)(2,1)S(1)} %get-tuple-element.51), channel_id=1, source_target_pairs={{0,1},{1,0},{2,3},{3,2},{4,5},{5,4},{6,7},{7,6},{8,9},{9,8},{10,11... | collective-permute-start | bytes 393224 | tf_op jit(solution)/shard_map/ppermute | solution.py:400
  11.6 19.4 %collective-permute-start.1 = (bf16[32,2048]{1,0:T(8,128)(2,1)S(1)}, bf16[32,2048]{1,0:T(8,128)(2,1)S(1)}, u32[]{:S(2)}, u32[]{:S(2)}) collective-permute-start(bf16[32,2048]{1,0:T(8,128)(2,1)S(1)} %get-tuple-element.52), channel_id=1, source_target_pairs={{0,2},{1,3},{2,0},{3,1},{4,6},{5,7},{6,4},{7,5},{8,10},{9,11},{10,... | collective-permute-start | bytes 393224 | tf_op jit(solution)/shard_map/ppermute | solution.py:400
  15.1 15.9 %collective-permute-start.2 = (bf16[32,2048]{1,0:T(8,128)(2,1)S(1)}, bf16[32,2048]{1,0:T(8,128)(2,1)S(1)}, u32[]{:S(2)}, u32[]{:S(2)}) collective-permute-start(bf16[32,2048]{1,0:T(8,128)(2,1)S(1)} %get-tuple-element.53), channel_id=1, source_target_pairs={{0,3},{1,2},{2,1},{3,0},{4,7},{5,6},{6,5},{7,4},{8,11},{9,10},{10,... | collective-permute-start | bytes 393224 | tf_op jit(solution)/shard_map/ppermute | solution.py:400
  31.1 16.2 %copy-start.2 = (s32[1,1,18,1]{2,3,1,0:T(1,128)S(1)}, s32[1,1,18,1]{2,3,1,0:T(1,128)}, u32[]{:S(2)}) copy-start(s32[1,1,18,1]{2,3,1,0:T(1,128)} %param.9) | copy-start | bytes 220
  33.2 8.7 %collective-permute-start.6 = (bf16[72,1024]{1,0:T(8,128)(2,1)S(1)}, bf16[72,1024]{1,0:T(8,128)(2,1)S(1)}, u32[]{:S(2)}, u32[]{:S(2)}) collective-permute-start(bf16[72,1024]{1,0:T(8,128)(2,1)S(1)} %get-tuple-element.72), channel_id=1, source_target_pairs={{0,3},{1,2},{2,1},{3,0},{4,7},{5,6},{6,5},{7,4},{8,11},{9,10},{10,... | collective-permute-start | bytes 442376 | tf_op jit(solution)/shard_map/ppermute | solution.py:400
  35.6 11.7 %collective-permute-start.7 = (bf16[72,1024]{1,0:T(8,128)(2,1)S(1)}, bf16[72,1024]{1,0:T(8,128)(2,1)S(1)}, u32[]{:S(2)}, u32[]{:S(2)}) collective-permute-start(bf16[72,1024]{1,0:T(8,128)(2,1)S(1)} %get-tuple-element.73), channel_id=1, source_target_pairs={{0,2},{1,3},{2,0},{3,1},{4,6},{5,7},{6,4},{7,5},{8,10},{9,11},{10,... | collective-permute-start | bytes 442376 | tf_op jit(solution)/shard_map/ppermute | solution.py:400
  38.9 8.3 %collective-permute-start.8 = (bf16[72,1024]{1,0:T(8,128)(2,1)S(1)}, bf16[72,1024]{1,0:T(8,128)(2,1)S(1)}, u32[]{:S(2)}, u32[]{:S(2)}) collective-permute-start(bf16[72,1024]{1,0:T(8,128)(2,1)S(1)} %get-tuple-element.77), channel_id=1, source_target_pairs={{0,1},{1,0},{2,3},{3,2},{4,5},{5,4},{6,7},{7,6},{8,9},{9,8},{10,11... | collective-permute-start | bytes 442376 | tf_op jit(solution)/shard_map/ppermute | solution.py:400
  47.8 3.6 %collective-permute-start.9 = (bf16[16,1024]{1,0:T(8,128)(2,1)S(1)}, bf16[16,1024]{1,0:T(8,128)(2,1)S(1)}, u32[]{:S(2)}, u32[]{:S(2)}) collective-permute-start(bf16[16,1024]{1,0:T(8,128)(2,1)S(1)} %get-tuple-element.80), channel_id=1, source_target_pairs={{0,4},{4,0},{8,12},{12,8},{16,20},{20,16},{24,28},{28,24},{1,5},{5... | collective-permute-start | bytes 98312 | tf_op jit(solution)/shard_map/ppermute | solution.py:423
  47.9 6.0 %collective-permute-start.10 = (bf16[16,1024]{1,0:T(8,128)(2,1)S(1)}, bf16[16,1024]{1,0:T(8,128)(2,1)S(1)}, u32[]{:S(2)}, u32[]{:S(2)}) collective-permute-start(bf16[16,1024]{1,0:T(8,128)(2,1)S(1)} %get-tuple-element.81), channel_id=1, source_target_pairs={{0,8},{4,12},{8,0},{12,4},{16,24},{20,28},{24,16},{28,20},{1,9},{5... | collective-permute-start | bytes 98312 | tf_op jit(solution)/shard_map/ppermute | solution.py:423
  49.4 4.7 %collective-permute-start.11 = (bf16[16,1024]{1,0:T(8,128)(2,1)S(1)}, bf16[16,1024]{1,0:T(8,128)(2,1)S(1)}, u32[]{:S(2)}, u32[]{:S(2)}) collective-permute-start(bf16[16,1024]{1,0:T(8,128)(2,1)S(1)} %get-tuple-element.82), channel_id=1, source_target_pairs={{0,12},{4,8},{8,4},{12,0},{16,28},{20,24},{24,20},{28,16},{1,13},{... | collective-permute-start | bytes 98312 | tf_op jit(solution)/shard_map/ppermute | solution.py:423
  49.7 4.4 %collective-permute-start.12 = (bf16[16,1024]{1,0:T(8,128)(2,1)S(1)}, bf16[16,1024]{1,0:T(8,128)(2,1)S(1)}, u32[]{:S(2)}, u32[]{:S(2)}) collective-permute-start(bf16[16,1024]{1,0:T(8,128)(2,1)S(1)} %get-tuple-element.83), channel_id=1, source_target_pairs={{0,16},{4,20},{8,24},{12,28},{16,0},{20,4},{24,8},{28,12},{1,17},{... | collective-permute-start | bytes 98312 | tf_op jit(solution)/shard_map/ppermute | solution.py:423
  51.2 3.4 %collective-permute-start.13 = (bf16[16,1024]{1,0:T(8,128)(2,1)S(1)}, bf16[16,1024]{1,0:T(8,128)(2,1)S(1)}, u32[]{:S(2)}, u32[]{:S(2)}) collective-permute-start(bf16[16,1024]{1,0:T(8,128)(2,1)S(1)} %get-tuple-element.84), channel_id=1, source_target_pairs={{0,20},{4,16},{8,28},{12,24},{16,4},{20,0},{24,12},{28,8},{1,21},{... | collective-permute-start | bytes 98312 | tf_op jit(solution)/shard_map/ppermute | solution.py:423
  51.4 4.8 %collective-permute-start.14 = (bf16[16,1024]{1,0:T(8,128)(2,1)S(1)}, bf16[16,1024]{1,0:T(8,128)(2,1)S(1)}, u32[]{:S(2)}, u32[]{:S(2)}) collective-permute-start(bf16[16,1024]{1,0:T(8,128)(2,1)S(1)} %get-tuple-element.85), channel_id=1, source_target_pairs={{0,24},{4,28},{8,16},{12,20},{16,8},{20,12},{24,0},{28,4},{1,25},{... | collective-permute-start | bytes 98312 | tf_op jit(solution)/shard_map/ppermute | solution.py:423
  53.9 4.2 %collective-permute-start.15 = (bf16[16,1024]{1,0:T(8,128)(2,1)S(1)}, bf16[16,1024]{1,0:T(8,128)(2,1)S(1)}, u32[]{:S(2)}, u32[]{:S(2)}) collective-permute-start(bf16[16,1024]{1,0:T(8,128)(2,1)S(1)} %get-tuple-element.86), channel_id=1, source_target_pairs={{0,28},{4,24},{8,20},{12,16},{16,12},{20,8},{24,4},{28,0},{1,29},{... | collective-permute-start | bytes 98312 | tf_op jit(solution)/shard_map/ppermute | solution.py:423

commit v3 on v2

--- a/solution.py
+++ b/solution.py
@@ -321,7 +321,7 @@
 
 
 def settle_kernel(groups, mine_ref, owners_ref, *refs):
-    part_refs, out_refs = refs[:-groups], refs[-groups:]
+    part_refs, out_refs = refs[:-2], refs[-2:]
     rows = groups * ROOM * PAIRS
     slots = rows // PAIRS
     each = NB_SRC * PAIRS
@@ -333,7 +333,9 @@
     other = jnp.sum(jnp.where(line == lane, wide, 0.0), axis=1, keepdims=True)
     earlier = jnp.logical_and(other == wide, line < lane).astype(jnp.float32)
     rank = jnp.sum(earlier, axis=0, keepdims=True)
-    slot = jnp.bitwise_xor(owner, mine_ref[0]).astype(jnp.float32) * ROOM + rank
+    turn = jnp.bitwise_xor(owner, mine_ref[0])
+    block = lax.shift_right_logical(turn, 1) + jnp.bitwise_and(turn, 1) * (groups // 2)
+    slot = jnp.where(owner < groups, block, rows).astype(jnp.float32) * ROOM + rank
     held = ones(iota((slots, LANES), 0).astype(jnp.float32) == slot)
     down = ones(lax.shift_right_logical(iota((rows, slots), 0), 2) == iota((rows, slots), 1))
     over = ones(lax.shift_right_logical(iota((LANES, each), 1), 2) == iota((LANES, each), 0))
@@ -343,14 +345,13 @@
     chosen = jnp.where(same, block, 0.0).astype(jnp.bfloat16)
     total = sum(ref[...].astype(jnp.float32) for ref in part_refs)
     placed = jnp.dot(chosen, total.astype(jnp.bfloat16), preferred_element_type=jnp.float32)
-    deep = ROOM * PAIRS
-    for m, out_ref in enumerate(out_refs):
-        out_ref[...] = placed[m * deep : (m + 1) * deep].astype(jnp.bfloat16)
+    for i, out_ref in enumerate(out_refs):
+        out_ref[...] = placed[i * rows // 2 : (i + 1) * rows // 2].astype(jnp.bfloat16)
 
 
 def settle(owners, partials, mine, groups):
     whole = lambda array: pl.BlockSpec(array.shape, lambda i, mine: (0, 0))
-    outs = [jax.ShapeDtypeStruct((ROOM * PAIRS, LAGS), jnp.bfloat16)] * groups
+    outs = [jax.ShapeDtypeStruct((groups * ROOM * PAIRS // 2, LAGS), jnp.bfloat16)] * 2
     return list(pl.pallas_call(
         functools.partial(settle_kernel, groups),
         grid_spec=pltpu.PrefetchScalarGridSpec(
@@ -365,17 +366,36 @@
     )(mine[None], owners, *partials))
 
 
+def bundle_kernel(kept_ref, brought_ref, *out_refs):
+    deep = ROOM * PAIRS
+    for j, out_ref in enumerate(out_refs):
+        out_ref[:deep] = kept_ref[j * deep : (j + 1) * deep]
+        out_ref[deep:] = brought_ref[j * deep : (j + 1) * deep]
+
+
+def bundle(kept, brought):
+    count = kept.shape[0] // (ROOM * PAIRS)
+    return list(pl.pallas_call(
+        bundle_kernel,
+        out_shape=[jax.ShapeDtypeStruct((2 * ROOM * PAIRS, LAGS), jnp.bfloat16)] * count,
+        compiler_params=pltpu.CompilerParams(vmem_limit_bytes=VMEM_LIMIT),
+        name="bundle",
+    )(kept, brought))
+
+
 def widen_kernel(mine_ref, *refs):
     part_refs, out_ref = refs[:-1], refs[-1]
-    for m, part_ref in enumerate(part_refs):
+    for j, part_ref in enumerate(part_refs):
         values = part_ref[...].astype(jnp.float32)
-        first = jnp.bitwise_xor(mine_ref[0], m) * MOST
-        for r in range(MOST):
-            out_ref[first + r] = values[r * PAIRS : (r + 1) * PAIRS]
+        for side in range(2):
+            first = jnp.bitwise_xor(mine_ref[0], 2 * j + side) * MOST
+            for r in range(MOST):
+                at = (side * ROOM + r) * PAIRS
+                out_ref[first + r] = values[at : at + PAIRS]
 
 
 def widen(pieces, mine):
-    shape = (len(pieces) * MOST, PAIRS, LAGS)
+    shape = (2 * len(pieces) * MOST, PAIRS, LAGS)
     return pl.pallas_call(
         widen_kernel,
         grid_spec=pltpu.PrefetchScalarGridSpec(
@@ -400,7 +420,9 @@
         return lax.ppermute(array, "chan", [(i, i ^ d) for i in range(parts)])
 
     def exchange(panels):
-        moved = {d: swap(panels[d], d) for d in reversed(range(1, parts))}
+        order = list(reversed(range(1, parts)))
+        order.insert(1, order.pop())
+        moved = {d: swap(panels[d], d) for d in order}
         return panels[:1] + [moved[d] for d in range(1, parts)]
 
     first, second = whiten(spectra, pair_blocks[0, 0].T, place, parts)
@@ -418,9 +440,14 @@
         for d, rows in zip(wanted, correlate(second, table, place, parts, wanted, 1, before)):
             partials.append(swap(rows, d) if d else rows)
     mine = lax.axis_index("grp")
-    pieces = settle(owners[0, 0].T, partials, mine, groups)
-    for m in reversed(range(1, groups)):
-        pieces[m] = lax.ppermute(pieces[m], "grp", [(i, i ^ m) for i in range(groups)])
+
+    def trade(array, m):
+        return lax.ppermute(array, "grp", [(i, i ^ m) for i in range(groups)])
+
+    kept, cross = settle(owners[0, 0].T, partials, mine, groups)
+    pieces = bundle(kept, trade(cross, 1))
+    for j in reversed(range(1, groups // 2)):
+        pieces[j] = trade(pieces[j], 2 * j)
     return widen(pieces, mine)[None, None]
 
 

time: 59.1 us -> 58.4 us (0.988)
  starting transfers between devices: 21.2 us -> 18.5 us
  waiting for transfers between devices: 22.8 us -> 24.8 us
    ppermute x7 -> x4, starting transfers between devices: 6.32 us -> 3.62 us  [trade(): return lax.ppermute(array, 'grp', [(i, i ^ m) for i in range(groups)])]
    ppermute x7 -> x4, waiting for transfers between devices: 4 us -> 6.02 us  [trade(): return lax.ppermute(array, 'grp', [(i, i ^ m) for i in range(groups)])]
  transfers between devices with their start and end apart: 16 -> 13, of which waited for: 7 -> 8; matrix products, arithmetic and copies ran while one was open for 1% -> 1% of each run, Pallas kernels for 13% -> 13%
where the time goes in v3:
time: 58.4 us; the launch traced here: 58.2 us
  waiting for transfers between devices  24.8 us (42%)
  starting transfers between devices  18.5 us (32%)
  Pallas kernels  11.7 us (20%)
  local copies, waits for them, and re-layouts  2.51 us (4%)
    ppermute x9, waiting for transfers between devices, swap(): return lax.ppermute(array, 'chan', [(i, i ^ d) for i in range(parts)])  18.8 us
    ppermute x9, starting transfers between devices, swap(): return lax.ppermute(array, 'chan', [(i, i ^ d) for i in range(parts)])  14.9 us
    pallas_call x4, Pallas kernels, correlate(): pl.pallas_call(functools.partial(corr_kernel, per_step, parts, lists, wav...  8.48 us
    ppermute x4, waiting for transfers between devices, trade(): return lax.ppermute(array, 'grp', [(i, i ^ m) for i in range(groups)])  6.02 us
    ppermute x4, starting transfers between devices, trade(): return lax.ppermute(array, 'grp', [(i, i ^ m) for i in range(groups)])  3.62 us
    reshape x1, local copies, waits for them, and re-layouts, whiten(): planes = jnp.transpose(spectra.reshape(rows, 2, F), (1, 0, 2))  1.82 us
    pallas_call x1, Pallas kernels, tables(): pl.pallas_call(table_kernel, grid_spec=pltpu.PrefetchScalarGridSpec(num_s...  1.33 us
  transfers between devices with their start and end apart: 13, of which 8 were waited for; matrix products, arithmetic and copies ran while one was open for 1% of the time, Pallas kernels for 13%

profile of v3, /device:TPU:0, one launch (start us, length us, event | category | flops | bytes accessed | tf_op | source)
XLA Modules:
  0.0 58.2 jit_solution(4009541704524924260)
XLA Ops:
  0.0 1.8 %copy.11 = bf16[32,2,8192]{2,0,1:T(8,128)(2,1)S(1)} copy(bf16[32,2,8192]{2,1,0:T(2,128)(2,1)} %bitcast.14) | data formatting | bytes 2097152 | tf_op jit(solution)/shard_map/reshape | solution.py:63
  3.1 3.1 %collective-permute-start.3 = (bf16[32,2176]{1,0:T(8,128)(2,1)S(1)}, bf16[32,2176]{1,0:T(8,128)(2,1)S(1)}, u32[]{:S(2)}, u32[]{:S(2)}) collective-permute-start(bf16[32,2176]{1,0:T(8,128)(2,1)S(1)} %get-tuple-element.53), channel_id=1, source_target_pairs={{0,1},{1,0},{2,3},{3,2},{4,5},{5,4},{6,7},{7,6},{8,9},{9,8},{10,11... | collective-permute-start | bytes 417800 | tf_op jit(solution)/shard_map/ppermute | solution.py:420
  6.2 2.6 %collective-permute-start.4 = (bf16[32,2176]{1,0:T(8,128)(2,1)S(1)}, bf16[32,2176]{1,0:T(8,128)(2,1)S(1)}, u32[]{:S(2)}, u32[]{:S(2)}) collective-permute-start(bf16[32,2176]{1,0:T(8,128)(2,1)S(1)} %get-tuple-element.54), channel_id=1, source_target_pairs={{0,2},{1,3},{2,0},{3,1},{4,6},{5,7},{6,4},{7,5},{8,10},{9,11},{10,... | collective-permute-start | bytes 417800 | tf_op jit(solution)/shard_map/ppermute | solution.py:420
  9.4 1.3 %tables.1.refs_4_ = bf16[2048,1024]{1,0:T(8,128)(2,1)S(1)} custom-call(s32[1]{0:T(128)} %bitcast.2.first_ref.place_ref.place, f32[16,512]{1,0:T(8,128)S(1)} %get-tuple-element.89.hi_cos_ref, f32[16,512]{1,0:T(8,128)S(1)} %get-tuple-element.84.hi_sin_ref, f32[16,512]{1,0:T(8,128)S(1)} %get-tuple-element.90.mid_cos_ref, ...), custom_call_target="tpu_custom_call" | custom-call | flops 8388608 | bytes 4194304 | tf_op jit(solution)/shard_map/tables/pallas_call | solution.py:128
  10.7 1.0 %collective-permute-start = (bf16[32,2048]{1,0:T(8,128)(2,1)S(1)}, bf16[32,2048]{1,0:T(8,128)(2,1)S(1)}, u32[]{:S(2)}, u32[]{:S(2)}) collective-permute-start(bf16[32,2048]{1,0:T(8,128)(2,1)S(1)} %get-tuple-element.49), channel_id=1, source_target_pairs={{0,1},{1,0},{2,3},{3,2},{4,5},{5,4},{6,7},{7,6},{8,9},{9,8},{10,11... | collective-permute-start | bytes 393224 | tf_op jit(solution)/shard_map/ppermute | solution.py:420
  11.6 3.5 %collective-permute-start.1 = (bf16[32,2048]{1,0:T(8,128)(2,1)S(1)}, bf16[32,2048]{1,0:T(8,128)(2,1)S(1)}, u32[]{:S(2)}, u32[]{:S(2)}) collective-permute-start(bf16[32,2048]{1,0:T(8,128)(2,1)S(1)} %get-tuple-element.50), channel_id=1, source_target_pairs={{0,2},{1,3},{2,0},{3,1},{4,6},{5,7},{6,4},{7,5},{8,10},{9,11},{10,... | collective-permute-start | bytes 393224 | tf_op jit(solution)/shard_map/ppermute | solution.py:420
  15.4 4.3 %collective-permute-done.4.refs_2_.refs_7_ = bf16[32,2176]{1,0:T(8,128)(2,1)S(1)} collective-permute-done((bf16[32,2176]{1,0:T(8,128)(2,1)S(1)}, bf16[32,2176]{1,0:T(8,128)(2,1)S(1)}, u32[]{:S(2)}, u32[]{:S(2)}) %collective-permute-start.4) | collective-permute-done | bytes 139296 | tf_op jit(solution)/shard_map/ppermute | solution.py:420
  19.7 2.2 %correlate.5 = (f32[160,1024]{1,0:T(8,128)S(1)}, f32[160,128]{1,0:T(8,128)S(1)}, bf16[320,128]{1,0:T(8,128)(2,1)S(1)}) custom-call(s32[1]{0:T(128)} %bitcast.2.first_ref.place_ref.place, bf16[32,2176]{1,0:T(8,128)(2,1)S(1)} %get-tuple-element.52.refs_0_.refs_7_, bf16[32,2176]{1,0:T(8,128)(2,1)S(1)} %collective-permute-done.3.refs_1_.refs_6_, ...), custom_call_target="tpu_custom_call" | custom-call | flops 335544320 | bytes 2097152 | tf_op jit(solution)/shard_map/correlate/pallas_call | solution.py:298
  21.9 2.2 %correlate.4 = (f32[160,1024]{1,0:T(8,128)S(1)}, f32[160,128]{1,0:T(8,128)S(1)}, bf16[320,128]{1,0:T(8,128)(2,1)S(1)}) custom-call(s32[1]{0:T(128)} %bitcast.2.first_ref.place_ref.place, bf16[32,2176]{1,0:T(8,128)(2,1)S(1)} %get-tuple-element.52.refs_0_.refs_7_, bf16[32,2176]{1,0:T(8,128)(2,1)S(1)} %collective-permute-done.3.refs_1_.refs_6_, ...), custom_call_target="tpu_custom_call" | custom-call | flops 335544320 | bytes 2097152 | tf_op jit(solution)/shard_map/correlate/pallas_call | solution.py:298
  24.1 7.0 %collective-permute-done.1.refs_2_ = bf16[32,2048]{1,0:T(8,128)(2,1)S(1)} collective-permute-done((bf16[32,2048]{1,0:T(8,128)(2,1)S(1)}, bf16[32,2048]{1,0:T(8,128)(2,1)S(1)}, u32[]{:S(2)}, u32[]{:S(2)}) %collective-permute-start.1) | collective-permute-done | bytes 131104 | tf_op jit(solution)/shard_map/ppermute | solution.py:420
  31.1 2.1 %correlate.6 = (bf16[72,1024]{1,0:T(8,128)(2,1)S(1)}, bf16[72,1024]{1,0:T(8,128)(2,1)S(1)}) custom-call(s32[1]{0:T(128)} %bitcast.2.first_ref.place_ref.place, bf16[32,2048]{1,0:T(8,128)(2,1)S(1)} %get-tuple-element.63.refs_0_, bf16[32,2048]{1,0:T(8,128)(2,1)S(1)} %collective-permute-done.refs_1_, bf16[32,2048]{1,0:T(8,128)(2,1)S(1)} %collective-permute-done.1.refs_2_, ...), custom_call_target="tpu_custom_call" | custom-call | flops 335544320 | bytes 2097152 | tf_op jit(solution)/shard_map/correlate/pallas_call | solution.py:298
  33.2 2.4 %collective-permute-start.6 = (bf16[72,1024]{1,0:T(8,128)(2,1)S(1)}, bf16[72,1024]{1,0:T(8,128)(2,1)S(1)}, u32[]{:S(2)}, u32[]{:S(2)}) collective-permute-start(bf16[72,1024]{1,0:T(8,128)(2,1)S(1)} %get-tuple-element.70), channel_id=1, source_target_pairs={{0,3},{1,2},{2,1},{3,0},{4,7},{5,6},{6,5},{7,4},{8,11},{9,10},{10,... | collective-permute-start | bytes 442376 | tf_op jit(solution)/shard_map/ppermute | solution.py:420
  35.6 1.3 %collective-permute-start.7 = (bf16[72,1024]{1,0:T(8,128)(2,1)S(1)}, bf16[72,1024]{1,0:T(8,128)(2,1)S(1)}, u32[]{:S(2)}, u32[]{:S(2)}) collective-permute-start(bf16[72,1024]{1,0:T(8,128)(2,1)S(1)} %get-tuple-element.71), channel_id=1, source_target_pairs={{0,2},{1,3},{2,0},{3,1},{4,6},{5,7},{6,4},{7,5},{8,10},{9,11},{10,... | collective-permute-start | bytes 442376 | tf_op jit(solution)/shard_map/ppermute | solution.py:420
  36.9 2.1 %correlate.7 = (bf16[72,1024]{1,0:T(8,128)(2,1)S(1)}, bf16[72,1024]{1,0:T(8,128)(2,1)S(1)}) custom-call(s32[1]{0:T(128)} %bitcast.2.first_ref.place_ref.place, bf16[32,2048]{1,0:T(8,128)(2,1)S(1)} %get-tuple-element.63.refs_0_, bf16[32,2048]{1,0:T(8,128)(2,1)S(1)} %collective-permute-done.refs_1_, bf16[32,2048]{1,0:T(8,128)(2,1)S(1)} %collective-permute-done.1.refs_2_, ...), custom_call_target="tpu_custom_call" | custom-call | flops 335544320 | bytes 2097152 | tf_op jit(solution)/shard_map/correlate/pallas_call | solution.py:298
  38.9 0.8 %collective-permute-start.8 = (bf16[72,1024]{1,0:T(8,128)(2,1)S(1)}, bf16[72,1024]{1,0:T(8,128)(2,1)S(1)}, u32[]{:S(2)}, u32[]{:S(2)}) collective-permute-start(bf16[72,1024]{1,0:T(8,128)(2,1)S(1)} %get-tuple-element.75), channel_id=1, source_target_pairs={{0,1},{1,0},{2,3},{3,2},{4,5},{5,4},{6,7},{7,6},{8,9},{9,8},{10,11... | collective-permute-start | bytes 442376 | tf_op jit(solution)/shard_map/ppermute | solution.py:420
  39.8 2.1 %collective-permute-done.6.refs_0_ = bf16[72,1024]{1,0:T(8,128)(2,1)S(1)} collective-permute-done((bf16[72,1024]{1,0:T(8,128)(2,1)S(1)}, bf16[72,1024]{1,0:T(8,128)(2,1)S(1)}, u32[]{:S(2)}, u32[]{:S(2)}) %collective-permute-start.6) | collective-permute-done | bytes 147488 | tf_op jit(solution)/shard_map/ppermute | solution.py:420
  41.8 5.4 %collective-permute-done.7.refs_1_ = bf16[72,1024]{1,0:T(8,128)(2,1)S(1)} collective-permute-done((bf16[72,1024]{1,0:T(8,128)(2,1)S(1)}, bf16[72,1024]{1,0:T(8,128)(2,1)S(1)}, u32[]{:S(2)}, u32[]{:S(2)}) %collective-permute-start.7) | collective-permute-done | bytes 147488 | tf_op jit(solution)/shard_map/ppermute | solution.py:420
  47.9 1.3 %collective-permute-done.9.brought_ref = bf16[64,1024]{1,0:T(8,128)(2,1)S(1)} collective-permute-done((bf16[64,1024]{1,0:T(8,128)(2,1)S(1)}, bf16[64,1024]{1,0:T(8,128)(2,1)S(1)}, u32[]{:S(2)}, u32[]{:S(2)}) %collective-permute-start.9) | collective-permute-done | bytes 131104 | tf_op jit(solution)/shard_map/ppermute | solution.py:445
  49.2 1.6 %collective-permute-start.10 = (bf16[32,1024]{1,0:T(8,128)(2,1)S(1)}, bf16[32,1024]{1,0:T(8,128)(2,1)S(1)}, u32[]{:S(2)}, u32[]{:S(2)}) collective-permute-start(bf16[32,1024]{1,0:T(8,128)(2,1)S(1)} %get-tuple-element.80), channel_id=1, source_target_pairs={{0,8},{4,12},{8,0},{12,4},{16,24},{20,28},{24,16},{28,20},{1,9},{5... | collective-permute-start | bytes 196616 | tf_op jit(solution)/shard_map/ppermute | solution.py:445
  50.8 1.5 %collective-permute-start.11 = (bf16[32,1024]{1,0:T(8,128)(2,1)S(1)}, bf16[32,1024]{1,0:T(8,128)(2,1)S(1)}, u32[]{:S(2)}, u32[]{:S(2)}) collective-permute-start(bf16[32,1024]{1,0:T(8,128)(2,1)S(1)} %get-tuple-element.81), channel_id=1, source_target_pairs={{0,16},{4,20},{8,24},{12,28},{16,0},{20,4},{24,8},{28,12},{1,17},{... | collective-permute-start | bytes 196616 | tf_op jit(solution)/shard_map/ppermute | solution.py:445
  52.8 0.8 %collective-permute-done.10.refs_1_ = bf16[32,1024]{1,0:T(8,128)(2,1)S(1)} collective-permute-done((bf16[32,1024]{1,0:T(8,128)(2,1)S(1)}, bf16[32,1024]{1,0:T(8,128)(2,1)S(1)}, u32[]{:S(2)}, u32[]{:S(2)}) %collective-permute-start.10) | collective-permute-done | bytes 65568 | tf_op jit(solution)/shard_map/ppermute | solution.py:445
  53.6 1.5 %collective-permute-done.11.refs_2_ = bf16[32,1024]{1,0:T(8,128)(2,1)S(1)} collective-permute-done((bf16[32,1024]{1,0:T(8,128)(2,1)S(1)}, bf16[32,1024]{1,0:T(8,128)(2,1)S(1)}, u32[]{:S(2)}, u32[]{:S(2)}) %collective-permute-start.11) | collective-permute-done | bytes 65568 | tf_op jit(solution)/shard_map/ppermute | solution.py:445
  55.0 2.4 %collective-permute-done.12.refs_3_ = bf16[32,1024]{1,0:T(8,128)(2,1)S(1)} collective-permute-done((bf16[32,1024]{1,0:T(8,128)(2,1)S(1)}, bf16[32,1024]{1,0:T(8,128)(2,1)S(1)}, u32[]{:S(2)}, u32[]{:S(2)}) %collective-permute-start.12) | collective-permute-done | bytes 65568 | tf_op jit(solution)/shard_map/ppermute | solution.py:445
  57.5 0.8 %widen.1 = f32[24,4,1024]{2,1,0:T(4,128)} custom-call(s32[1]{0:T(128)} %bitcast.mine_ref, bf16[32,1024]{1,0:T(8,128)(2,1)S(1)} %get-tuple-element.79.refs_0_, bf16[32,1024]{1,0:T(8,128)(2,1)S(1)} %collective-permute-done.10.refs_1_, bf16[32,1024]{1,0:T(8,128)(2,1)S(1)} %collective-permute-done.11.refs_2_, bf16[32,1024]{1,0:T(8,128)(2,1)S(1)} %collective-permute-done.12.refs_3_), custom_call_target="tpu_custom_call" | custom-call | tf_op jit(solution)/shard_map/widen/pallas_call | solution.py:399
  (26 shorter events, 3.2 us)
Async XLA Ops:
  0.0 19.7 %copy-start = (f32[2,128]{1,0:T(2,128)S(1)}, f32[2,128]{1,0:T(2,128)}, u32[]{:S(2)}) copy-start(f32[2,128]{1,0:T(2,128)} %constant.36.clone.refs_5_) | copy-start | bytes 3076
  1.8 0.7 %copy-start.1 = (s32[1,1,18,2]{2,3,1,0:T(2,128)S(1)}, s32[1,1,18,2]{2,3,1,0:T(2,128)}, u32[]{:S(2)}) copy-start(s32[1,1,18,2]{2,3,1,0:T(2,128)} %param.8) | copy-start | bytes 436
  3.1 12.0 %collective-permute-start.3 = (bf16[32,2176]{1,0:T(8,128)(2,1)S(1)}, bf16[32,2176]{1,0:T(8,128)(2,1)S(1)}, u32[]{:S(2)}, u32[]{:S(2)}) collective-permute-start(bf16[32,2176]{1,0:T(8,128)(2,1)S(1)} %get-tuple-element.53), channel_id=1, source_target_pairs={{0,1},{1,0},{2,3},{3,2},{4,5},{5,4},{6,7},{7,6},{8,9},{9,8},{10,11... | collective-permute-start | bytes 417800 | tf_op jit(solution)/shard_map/ppermute | solution.py:420
  6.2 13.5 %collective-permute-start.4 = (bf16[32,2176]{1,0:T(8,128)(2,1)S(1)}, bf16[32,2176]{1,0:T(8,128)(2,1)S(1)}, u32[]{:S(2)}, u32[]{:S(2)}) collective-permute-start(bf16[32,2176]{1,0:T(8,128)(2,1)S(1)} %get-tuple-element.54), channel_id=1, source_target_pairs={{0,2},{1,3},{2,0},{3,1},{4,6},{5,7},{6,4},{7,5},{8,10},{9,11},{10,... | collective-permute-start | bytes 417800 | tf_op jit(solution)/shard_map/ppermute | solution.py:420
  8.8 10.9 %collective-permute-start.5 = (bf16[32,2176]{1,0:T(8,128)(2,1)S(1)}, bf16[32,2176]{1,0:T(8,128)(2,1)S(1)}, u32[]{:S(2)}, u32[]{:S(2)}) collective-permute-start(bf16[32,2176]{1,0:T(8,128)(2,1)S(1)} %get-tuple-element.55), channel_id=1, source_target_pairs={{0,3},{1,2},{2,1},{3,0},{4,7},{5,6},{6,5},{7,4},{8,11},{9,10},{10,... | collective-permute-start | bytes 417800 | tf_op jit(solution)/shard_map/ppermute | solution.py:420
  10.7 13.4 %collective-permute-start = (bf16[32,2048]{1,0:T(8,128)(2,1)S(1)}, bf16[32,2048]{1,0:T(8,128)(2,1)S(1)}, u32[]{:S(2)}, u32[]{:S(2)}) collective-permute-start(bf16[32,2048]{1,0:T(8,128)(2,1)S(1)} %get-tuple-element.49), channel_id=1, source_target_pairs={{0,1},{1,0},{2,3},{3,2},{4,5},{5,4},{6,7},{7,6},{8,9},{9,8},{10,11... | collective-permute-start | bytes 393224 | tf_op jit(solution)/shard_map/ppermute | solution.py:420
  11.6 19.4 %collective-permute-start.1 = (bf16[32,2048]{1,0:T(8,128)(2,1)S(1)}, bf16[32,2048]{1,0:T(8,128)(2,1)S(1)}, u32[]{:S(2)}, u32[]{:S(2)}) collective-permute-start(bf16[32,2048]{1,0:T(8,128)(2,1)S(1)} %get-tuple-element.50), channel_id=1, source_target_pairs={{0,2},{1,3},{2,0},{3,1},{4,6},{5,7},{6,4},{7,5},{8,10},{9,11},{10,... | collective-permute-start | bytes 393224 | tf_op jit(solution)/shard_map/ppermute | solution.py:420
  15.1 15.9 %collective-permute-start.2 = (bf16[32,2048]{1,0:T(8,128)(2,1)S(1)}, bf16[32,2048]{1,0:T(8,128)(2,1)S(1)}, u32[]{:S(2)}, u32[]{:S(2)}) collective-permute-start(bf16[32,2048]{1,0:T(8,128)(2,1)S(1)} %get-tuple-element.51), channel_id=1, source_target_pairs={{0,3},{1,2},{2,1},{3,0},{4,7},{5,6},{6,5},{7,4},{8,11},{9,10},{10,... | collective-permute-start | bytes 393224 | tf_op jit(solution)/shard_map/ppermute | solution.py:420
  31.1 16.2 %copy-start.2 = (s32[1,1,18,1]{2,3,1,0:T(1,128)S(1)}, s32[1,1,18,1]{2,3,1,0:T(1,128)}, u32[]{:S(2)}) copy-start(s32[1,1,18,1]{2,3,1,0:T(1,128)} %param.9) | copy-start | bytes 220
  33.2 8.7 %collective-permute-start.6 = (bf16[72,1024]{1,0:T(8,128)(2,1)S(1)}, bf16[72,1024]{1,0:T(8,128)(2,1)S(1)}, u32[]{:S(2)}, u32[]{:S(2)}) collective-permute-start(bf16[72,1024]{1,0:T(8,128)(2,1)S(1)} %get-tuple-element.70), channel_id=1, source_target_pairs={{0,3},{1,2},{2,1},{3,0},{4,7},{5,6},{6,5},{7,4},{8,11},{9,10},{10,... | collective-permute-start | bytes 442376 | tf_op jit(solution)/shard_map/ppermute | solution.py:420
  35.6 11.7 %collective-permute-start.7 = (bf16[72,1024]{1,0:T(8,128)(2,1)S(1)}, bf16[72,1024]{1,0:T(8,128)(2,1)S(1)}, u32[]{:S(2)}, u32[]{:S(2)}) collective-permute-start(bf16[72,1024]{1,0:T(8,128)(2,1)S(1)} %get-tuple-element.71), channel_id=1, source_target_pairs={{0,2},{1,3},{2,0},{3,1},{4,6},{5,7},{6,4},{7,5},{8,10},{9,11},{10,... | collective-permute-start | bytes 442376 | tf_op jit(solution)/shard_map/ppermute | solution.py:420
  38.9 8.3 %collective-permute-start.8 = (bf16[72,1024]{1,0:T(8,128)(2,1)S(1)}, bf16[72,1024]{1,0:T(8,128)(2,1)S(1)}, u32[]{:S(2)}, u32[]{:S(2)}) collective-permute-start(bf16[72,1024]{1,0:T(8,128)(2,1)S(1)} %get-tuple-element.75), channel_id=1, source_target_pairs={{0,1},{1,0},{2,3},{3,2},{4,5},{5,4},{6,7},{7,6},{8,9},{9,8},{10,11... | collective-permute-start | bytes 442376 | tf_op jit(solution)/shard_map/ppermute | solution.py:420
  47.8 1.4 %collective-permute-start.9 = (bf16[64,1024]{1,0:T(8,128)(2,1)S(1)}, bf16[64,1024]{1,0:T(8,128)(2,1)S(1)}, u32[]{:S(2)}, u32[]{:S(2)}) collective-permute-start(bf16[64,1024]{1,0:T(8,128)(2,1)S(1)} %get-tuple-element.78), channel_id=1, source_target_pairs={{0,4},{4,0},{8,12},{12,8},{16,20},{20,16},{24,28},{28,24},{1,5},{5... | collective-permute-start | bytes 393224 | tf_op jit(solution)/shard_map/ppermute | solution.py:445
  49.2 4.3 %collective-permute-start.10 = (bf16[32,1024]{1,0:T(8,128)(2,1)S(1)}, bf16[32,1024]{1,0:T(8,128)(2,1)S(1)}, u32[]{:S(2)}, u32[]{:S(2)}) collective-permute-start(bf16[32,1024]{1,0:T(8,128)(2,1)S(1)} %get-tuple-element.80), channel_id=1, source_target_pairs={{0,8},{4,12},{8,0},{12,4},{16,24},{20,28},{24,16},{28,20},{1,9},{5... | collective-permute-start | bytes 196616 | tf_op jit(solution)/shard_map/ppermute | solution.py:445
  50.8 4.3 %collective-permute-start.11 = (bf16[32,1024]{1,0:T(8,128)(2,1)S(1)}, bf16[32,1024]{1,0:T(8,128)(2,1)S(1)}, u32[]{:S(2)}, u32[]{:S(2)}) collective-permute-start(bf16[32,1024]{1,0:T(8,128)(2,1)S(1)} %get-tuple-element.81), channel_id=1, source_target_pairs={{0,16},{4,20},{8,24},{12,28},{16,0},{20,4},{24,8},{28,12},{1,17},{... | collective-permute-start | bytes 196616 | tf_op jit(solution)/shard_map/ppermute | solution.py:445
  52.3 5.2 %collective-permute-start.12 = (bf16[32,1024]{1,0:T(8,128)(2,1)S(1)}, bf16[32,1024]{1,0:T(8,128)(2,1)S(1)}, u32[]{:S(2)}, u32[]{:S(2)}) collective-permute-start(bf16[32,1024]{1,0:T(8,128)(2,1)S(1)} %get-tuple-element.82), channel_id=1, source_target_pairs={{0,24},{4,28},{8,16},{12,20},{16,8},{20,12},{24,0},{28,4},{1,25},{... | collective-permute-start | bytes 196616 | tf_op jit(solution)/shard_map/ppermute | solution.py:445

commit v4 on v3

--- a/solution.py
+++ b/solution.py
@@ -20,12 +20,13 @@
 HALF = LAGS // 2
 ROOM = 4
 WAVES = 2
+LATE = 4
 
 
 def whiten_kernel(parts, place_ref, spec_ref, pairs_ref, *out_refs):
     blocks = F // LANES
     each = blocks // parts
-    share = each // WAVES
+    late = each // LATE
     place = place_ref[0]
 
     def values(start):
@@ -41,7 +42,7 @@
     notes = jnp.where(line == 0, wide(pairs_ref[0:1]), wide(pairs_ref[1:2]))
     notes = notes.astype(jnp.float32).astype(jnp.bfloat16)
     for out_ref in out_refs[:parts]:
-        out_ref[:, share * 2 * LANES :] = notes
+        out_ref[:, (each - late) * 2 * LANES :] = notes
     sums = [None] * 4
     for k in range(blocks):
         power = values(k * LANES)[2]
@@ -49,8 +50,9 @@
     total = jnp.sum((sums[0] + sums[1]) + (sums[2] + sums[3]), axis=1, keepdims=True)
     level = 0.1 * (total * (1.0 / F) + 1e-05)
     for index, out_ref in enumerate(out_refs):
-        first = jnp.bitwise_xor(place, index % parts) * each + index // parts * share
-        for k in range(share):
+        wave, d = divmod(index, parts)
+        first = jnp.bitwise_xor(place, d) * each + wave * (each - late)
+        for k in range(late if wave else each - late):
             re, im, power = values(pl.multiple_of((first + k) * LANES, LANES))
             scale = lax.rsqrt(power + level)
             at = k * 2 * LANES
@@ -61,8 +63,9 @@
 def whiten(spectra, pairs, place, parts):
     rows = spectra.shape[0] * WINDOWS
     planes = jnp.transpose(spectra.reshape(rows, 2, F), (1, 0, 2))
-    width = 2 * F // parts // WAVES
-    shapes = [(rows, width + LANES)] * parts + [(rows, width)] * parts * (WAVES - 1)
+    width = 2 * F // parts
+    late = width // LATE
+    shapes = [(rows, width - late + LANES)] * parts + [(rows, late)] * parts
     whole = lambda array: pl.BlockSpec(array.shape, lambda i, place: (0,) * array.ndim)
     outs = pl.pallas_call(
         functools.partial(whiten_kernel, parts),
@@ -176,8 +179,13 @@
     rows_ref[...] = jnp.concatenate(picks, axis=0).astype(jnp.bfloat16)
 
 
+def sequence(parts):
+    order = list(reversed(range(parts)))
+    return [order[0], order[-2], *order[1:-2], order[-1]]
+
+
 def corr_kernel(per_step, parts, lists, wave, place, *refs):
-    panel_refs, (table_ref, ends_ref), refs = refs[:parts], refs[parts : parts + 2], refs[parts + 2 :]
+    panel_refs, (table_ref, ends_ref), refs = dict(zip(sequence(parts), refs)), refs[parts : parts + 2], refs[parts + 2 :]
     step = pl.program_id(0)
     if wave:
         (total_in, edge_in, rows_ref), out_refs, (total, edge) = refs[:3], refs[3:-2], refs[-2:]
@@ -189,7 +197,7 @@
             choose_rows(lists, place[0], jnp.concatenate([ref[...] for ref in note_refs]), rows_ref)
 
     count = total.shape[0] // PAIRS
-    panel = jnp.concatenate([ref[...] for ref in panel_refs])
+    panel = jnp.concatenate([panel_refs[d][...] for d in range(parts)])
     chosen = jnp.dot(rows_ref[...], panel, preferred_element_type=jnp.float32)
 
     def row(side, channel, window, start):
@@ -270,10 +278,11 @@
 
 
 def correlate(panels, table, place, parts, wanted, wave, before):
-    per_step = 4
+    per_step = table.shape[0] // LANES // LATE
     span = per_step * 2 * LANES
     rows = panels[0].shape[0]
-    steps = 2 * table.shape[0] // span // WAVES
+    early = LATE - 1
+    steps = 1 if wave else early
     lists = len(wanted)
     count = -(-lists * NB_SRC // 8) * 8
     each = NB_SRC * PAIRS
@@ -302,7 +311,7 @@
             grid=(steps,),
             in_specs=[
                 *[pl.BlockSpec((rows, span), lambda i, place: (0, i))] * parts,
-                pl.BlockSpec((span // 2, LAGS), lambda i, place: (i + wave * steps, 0)),
+                pl.BlockSpec((span // 2, LAGS), lambda i, place: (i + wave * early, 0)),
                 pl.BlockSpec((2, LANES), lambda i, place: (0, 0)),
                 *extra_specs,
             ],
@@ -317,7 +326,7 @@
             transcendentals=0,
         ),
         name="correlate",
-    )(place[None], *panels, table, jnp.asarray(ends, jnp.float32), *extra)
+    )(place[None], *[panels[d] for d in sequence(parts)], table, jnp.asarray(ends, jnp.float32), *extra)
 
 
 def settle_kernel(groups, mine_ref, owners_ref, *refs):
@@ -420,9 +429,7 @@
         return lax.ppermute(array, "chan", [(i, i ^ d) for i in range(parts)])
 
     def exchange(panels):
-        order = list(reversed(range(1, parts)))
-        order.insert(1, order.pop())
-        moved = {d: swap(panels[d], d) for d in order}
+        moved = {d: swap(panels[d], d) for d in sequence(parts)[:-1]}
         return panels[:1] + [moved[d] for d in range(1, parts)]
 
     first, second = whiten(spectra, pair_blocks[0, 0].T, place, parts)
@@ -434,7 +441,9 @@
     order = list(reversed(range(parts)))
     halves = (order[: parts // 2], order[parts // 2 :])
     sums = [correlate(first, table, place, parts, wanted, 0, None) for wanted in halves]
-    second, sums = lax.optimization_barrier((second, sums))
+    ordered, sums = lax.optimization_barrier(([second[d] for d in sequence(parts)], sums))
+    for d, panel in zip(sequence(parts), ordered):
+        second[d] = panel
     partials = []
     for wanted, before in zip(halves, sums):
         for d, rows in zip(wanted, correlate(second, table, place, parts, wanted, 1, before)):

time: 58.4 us -> 61.8 us (1.058)
  starting transfers between devices: 18.5 us -> 23 us
  waiting for transfers between devices: 24.8 us -> 23.6 us
    ppermute x9, starting transfers between devices: 14.9 us -> 19.4 us  [swap(): return lax.ppermute(array, 'chan', [(i, i ^ d) for i in range(parts)])]
    ppermute x9, waiting for transfers between devices: 18.8 us -> 17.6 us  [swap(): return lax.ppermute(array, 'chan', [(i, i ^ d) for i in range(parts)])]
  transfers between devices with their start and end apart: 13 -> 13, of which waited for: 8 -> 7; matrix products, arithmetic and copies ran while one was open for 1% -> 1% of each run, Pallas kernels for 13% -> 14%
where the time goes in v4:
time: 61.8 us; the launch traced here: 61.6 us
  waiting for transfers between devices  23.6 us (38%)
  starting transfers between devices  23 us (37%)
  Pallas kernels  11.9 us (19%)
  local copies, waits for them, and re-layouts  2.51 us (4%)
    ppermute x9, starting transfers between devices, swap(): return lax.ppermute(array, 'chan', [(i, i ^ d) for i in range(parts)])  19.4 us
    ppermute x9, waiting for transfers between devices, swap(): return lax.ppermute(array, 'chan', [(i, i ^ d) for i in range(parts)])  17.6 us
    pallas_call x4, Pallas kernels, correlate(): pl.pallas_call(functools.partial(corr_kernel, per_step, parts, lists, wav...  8.62 us
    ppermute x4, waiting for transfers between devices, trade(): return lax.ppermute(array, 'grp', [(i, i ^ m) for i in range(groups)])  6.03 us
    ppermute x4, starting transfers between devices, trade(): return lax.ppermute(array, 'grp', [(i, i ^ m) for i in range(groups)])  3.62 us
    reshape x1, local copies, waits for them, and re-layouts, whiten(): planes = jnp.transpose(spectra.reshape(rows, 2, F), (1, 0, 2))  1.82 us
    pallas_call x1, Pallas kernels, tables(): pl.pallas_call(table_kernel, grid_spec=pltpu.PrefetchScalarGridSpec(num_s...  1.33 us
  transfers between devices with their start and end apart: 13, of which 7 were waited for; matrix products, arithmetic and copies ran while one was open for 1% of the time, Pallas kernels for 14%

profile of v4, /device:TPU:0, one launch (start us, length us, event | category | flops | bytes accessed | tf_op | source)
XLA Modules:
  0.0 61.6 jit_solution(12779427052909466660)
XLA Ops:
  0.0 1.8 %copy.11 = bf16[32,2,8192]{2,0,1:T(8,128)(2,1)S(1)} copy(bf16[32,2,8192]{2,1,0:T(2,128)(2,1)} %bitcast.14) | data formatting | bytes 2097152 | tf_op jit(solution)/shard_map/reshape | solution.py:65
  1.8 0.7 %copy-done.1 = s32[1,1,18,2]{2,3,1,0:T(2,128)S(1)} copy-done((s32[1,1,18,2]{2,3,1,0:T(2,128)S(1)}, s32[1,1,18,2]{2,3,1,0:T(2,128)}, u32[]{:S(2)}) %copy-start.1) | copy-done | bytes 168
  2.5 0.6 whiten.1
  3.1 5.1 %collective-permute-start.3 = (bf16[32,3200]{1,0:T(8,128)(2,1)S(1)}, bf16[32,3200]{1,0:T(8,128)(2,1)S(1)}, u32[]{:S(2)}, u32[]{:S(2)}) collective-permute-start(bf16[32,3200]{1,0:T(8,128)(2,1)S(1)} %get-tuple-element.52), channel_id=1, source_target_pairs={{0,3},{1,2},{2,1},{3,0},{4,7},{5,6},{6,5},{7,4},{8,11},{9,10},{10,... | collective-permute-start | bytes 614408 | tf_op jit(solution)/shard_map/ppermute | solution.py:429
  8.2 0.6 %collective-permute-start.5 = (bf16[32,3200]{1,0:T(8,128)(2,1)S(1)}, bf16[32,3200]{1,0:T(8,128)(2,1)S(1)}, u32[]{:S(2)}, u32[]{:S(2)}) collective-permute-start(bf16[32,3200]{1,0:T(8,128)(2,1)S(1)} %get-tuple-element.54), channel_id=1, source_target_pairs={{0,2},{1,3},{2,0},{3,1},{4,6},{5,7},{6,4},{7,5},{8,10},{9,11},{10,... | collective-permute-start | bytes 614408 | tf_op jit(solution)/shard_map/ppermute | solution.py:429
  9.4 1.3 %tables.1.refs_4_ = bf16[2048,1024]{1,0:T(8,128)(2,1)S(1)} custom-call(s32[1]{0:T(128)} %bitcast.2.first_ref.place_ref.place, f32[16,512]{1,0:T(8,128)S(1)} %get-tuple-element.89.hi_cos_ref, f32[16,512]{1,0:T(8,128)S(1)} %get-tuple-element.84.hi_sin_ref, f32[16,512]{1,0:T(8,128)S(1)} %get-tuple-element.90.mid_cos_ref, ...), custom_call_target="tpu_custom_call" | custom-call | flops 8388608 | bytes 4194304 | tf_op jit(solution)/shard_map/tables/pallas_call | solution.py:131
  10.8 3.8 %collective-permute-start = (bf16[32,1024]{1,0:T(8,128)(2,1)S(1)}, bf16[32,1024]{1,0:T(8,128)(2,1)S(1)}, u32[]{:S(2)}, u32[]{:S(2)}) collective-permute-start(bf16[32,1024]{1,0:T(8,128)(2,1)S(1)} %get-tuple-element.48), channel_id=1, source_target_pairs={{0,3},{1,2},{2,1},{3,0},{4,7},{5,6},{6,5},{7,4},{8,11},{9,10},{10,... | collective-permute-start | bytes 196616 | tf_op jit(solution)/shard_map/ppermute | solution.py:429
  14.6 5.3 %collective-permute-start.2 = (bf16[32,1024]{1,0:T(8,128)(2,1)S(1)}, bf16[32,1024]{1,0:T(8,128)(2,1)S(1)}, u32[]{:S(2)}, u32[]{:S(2)}) collective-permute-start(bf16[32,1024]{1,0:T(8,128)(2,1)S(1)} %get-tuple-element.50), channel_id=1, source_target_pairs={{0,2},{1,3},{2,0},{3,1},{4,6},{5,7},{6,4},{7,5},{8,10},{9,11},{10,... | collective-permute-start | bytes 196616 | tf_op jit(solution)/shard_map/ppermute | solution.py:429
  19.9 9.5 %collective-permute-done.5.refs_2_.refs_7_ = bf16[32,3200]{1,0:T(8,128)(2,1)S(1)} collective-permute-done((bf16[32,3200]{1,0:T(8,128)(2,1)S(1)}, bf16[32,3200]{1,0:T(8,128)(2,1)S(1)}, u32[]{:S(2)}, u32[]{:S(2)}) %collective-permute-start.5) | collective-permute-done | bytes 204832 | tf_op jit(solution)/shard_map/ppermute | solution.py:429
  29.4 3.1 %correlate.5 = (f32[160,1024]{1,0:T(8,128)S(1)}, f32[160,128]{1,0:T(8,128)S(1)}, bf16[320,128]{1,0:T(8,128)(2,1)S(1)}) custom-call(s32[1]{0:T(128)} %bitcast.2.first_ref.place_ref.place, bf16[32,3200]{1,0:T(8,128)(2,1)S(1)} %collective-permute-done.3.refs_0_.refs_6_, bf16[32,3200]{1,0:T(8,128)(2,1)S(1)} %collective-permute-done.4.refs_1_.refs_6_, ...), custom_call_target="tpu_custom_call" | custom-call | flops 503316480 | bytes 3145728 | tf_op jit(solution)/shard_map/correlate/pallas_call | solution.py:307
  32.5 3.2 %correlate.4 = (f32[160,1024]{1,0:T(8,128)S(1)}, f32[160,128]{1,0:T(8,128)S(1)}, bf16[320,128]{1,0:T(8,128)(2,1)S(1)}) custom-call(s32[1]{0:T(128)} %bitcast.2.first_ref.place_ref.place, bf16[32,3200]{1,0:T(8,128)(2,1)S(1)} %collective-permute-done.3.refs_0_.refs_6_, bf16[32,3200]{1,0:T(8,128)(2,1)S(1)} %collective-permute-done.4.refs_1_.refs_6_, ...), custom_call_target="tpu_custom_call" | custom-call | flops 503316480 | bytes 3145728 | tf_op jit(solution)/shard_map/correlate/pallas_call | solution.py:307
  35.8 1.1 %correlate.6 = (bf16[72,1024]{1,0:T(8,128)(2,1)S(1)}, bf16[72,1024]{1,0:T(8,128)(2,1)S(1)}) custom-call(s32[1]{0:T(128)} %bitcast.2.first_ref.place_ref.place, bf16[32,1024]{1,0:T(8,128)(2,1)S(1)} %collective-permute-done.refs_0_, bf16[32,1024]{1,0:T(8,128)(2,1)S(1)} %collective-permute-done.1.refs_1_, bf16[32,1024]{1,0:T(8,128)(2,1)S(1)} %collective-permute-done.2.refs_2_, ...), custom_call_target="tpu_custom_call" | custom-call | flops 167772160 | bytes 1048576 | tf_op jit(solution)/shard_map/correlate/pallas_call | solution.py:307
  36.9 2.7 %collective-permute-start.6 = (bf16[72,1024]{1,0:T(8,128)(2,1)S(1)}, bf16[72,1024]{1,0:T(8,128)(2,1)S(1)}, u32[]{:S(2)}, u32[]{:S(2)}) collective-permute-start(bf16[72,1024]{1,0:T(8,128)(2,1)S(1)} %get-tuple-element.70), channel_id=1, source_target_pairs={{0,3},{1,2},{2,1},{3,0},{4,7},{5,6},{6,5},{7,4},{8,11},{9,10},{10,... | collective-permute-start | bytes 442376 | tf_op jit(solution)/shard_map/ppermute | solution.py:429
  39.7 1.1 %correlate.7 = (bf16[72,1024]{1,0:T(8,128)(2,1)S(1)}, bf16[72,1024]{1,0:T(8,128)(2,1)S(1)}) custom-call(s32[1]{0:T(128)} %bitcast.2.first_ref.place_ref.place, bf16[32,1024]{1,0:T(8,128)(2,1)S(1)} %collective-permute-done.refs_0_, bf16[32,1024]{1,0:T(8,128)(2,1)S(1)} %collective-permute-done.1.refs_1_, bf16[32,1024]{1,0:T(8,128)(2,1)S(1)} %collective-permute-done.2.refs_2_, ...), custom_call_target="tpu_custom_call" | custom-call | flops 167772160 | bytes 1048576 | tf_op jit(solution)/shard_map/correlate/pallas_call | solution.py:307
  40.8 1.8 %collective-permute-start.8 = (bf16[72,1024]{1,0:T(8,128)(2,1)S(1)}, bf16[72,1024]{1,0:T(8,128)(2,1)S(1)}, u32[]{:S(2)}, u32[]{:S(2)}) collective-permute-start(bf16[72,1024]{1,0:T(8,128)(2,1)S(1)} %get-tuple-element.75), channel_id=1, source_target_pairs={{0,1},{1,0},{2,3},{3,2},{4,5},{5,4},{6,7},{7,6},{8,9},{9,8},{10,11... | collective-permute-start | bytes 442376 | tf_op jit(solution)/shard_map/ppermute | solution.py:429
  42.6 3.0 %collective-permute-done.6.refs_0_ = bf16[72,1024]{1,0:T(8,128)(2,1)S(1)} collective-permute-done((bf16[72,1024]{1,0:T(8,128)(2,1)S(1)}, bf16[72,1024]{1,0:T(8,128)(2,1)S(1)}, u32[]{:S(2)}, u32[]{:S(2)}) %collective-permute-start.6) | collective-permute-done | bytes 147488 | tf_op jit(solution)/shard_map/ppermute | solution.py:429
  45.6 5.1 %collective-permute-done.7.refs_1_ = bf16[72,1024]{1,0:T(8,128)(2,1)S(1)} collective-permute-done((bf16[72,1024]{1,0:T(8,128)(2,1)S(1)}, bf16[72,1024]{1,0:T(8,128)(2,1)S(1)}, u32[]{:S(2)}, u32[]{:S(2)}) %collective-permute-start.7) | collective-permute-done | bytes 147488 | tf_op jit(solution)/shard_map/ppermute | solution.py:429
  51.3 1.3 %collective-permute-done.9.brought_ref = bf16[64,1024]{1,0:T(8,128)(2,1)S(1)} collective-permute-done((bf16[64,1024]{1,0:T(8,128)(2,1)S(1)}, bf16[64,1024]{1,0:T(8,128)(2,1)S(1)}, u32[]{:S(2)}, u32[]{:S(2)}) %collective-permute-start.9) | collective-permute-done | bytes 131104 | tf_op jit(solution)/shard_map/ppermute | solution.py:454
  52.6 1.6 %collective-permute-start.10 = (bf16[32,1024]{1,0:T(8,128)(2,1)S(1)}, bf16[32,1024]{1,0:T(8,128)(2,1)S(1)}, u32[]{:S(2)}, u32[]{:S(2)}) collective-permute-start(bf16[32,1024]{1,0:T(8,128)(2,1)S(1)} %get-tuple-element.80), channel_id=1, source_target_pairs={{0,8},{4,12},{8,0},{12,4},{16,24},{20,28},{24,16},{28,20},{1,9},{5... | collective-permute-start | bytes 196616 | tf_op jit(solution)/shard_map/ppermute | solution.py:454
  54.2 1.5 %collective-permute-start.11 = (bf16[32,1024]{1,0:T(8,128)(2,1)S(1)}, bf16[32,1024]{1,0:T(8,128)(2,1)S(1)}, u32[]{:S(2)}, u32[]{:S(2)}) collective-permute-start(bf16[32,1024]{1,0:T(8,128)(2,1)S(1)} %get-tuple-element.81), channel_id=1, source_target_pairs={{0,16},{4,20},{8,24},{12,28},{16,0},{20,4},{24,8},{28,12},{1,17},{... | collective-permute-start | bytes 196616 | tf_op jit(solution)/shard_map/ppermute | solution.py:454
  56.2 0.8 %collective-permute-done.10.refs_1_ = bf16[32,1024]{1,0:T(8,128)(2,1)S(1)} collective-permute-done((bf16[32,1024]{1,0:T(8,128)(2,1)S(1)}, bf16[32,1024]{1,0:T(8,128)(2,1)S(1)}, u32[]{:S(2)}, u32[]{:S(2)}) %collective-permute-start.10) | collective-permute-done | bytes 65568 | tf_op jit(solution)/shard_map/ppermute | solution.py:454
  56.9 1.5 %collective-permute-done.11.refs_2_ = bf16[32,1024]{1,0:T(8,128)(2,1)S(1)} collective-permute-done((bf16[32,1024]{1,0:T(8,128)(2,1)S(1)}, bf16[32,1024]{1,0:T(8,128)(2,1)S(1)}, u32[]{:S(2)}, u32[]{:S(2)}) %collective-permute-start.11) | collective-permute-done | bytes 65568 | tf_op jit(solution)/shard_map/ppermute | solution.py:454
  58.4 2.4 %collective-permute-done.12.refs_3_ = bf16[32,1024]{1,0:T(8,128)(2,1)S(1)} collective-permute-done((bf16[32,1024]{1,0:T(8,128)(2,1)S(1)}, bf16[32,1024]{1,0:T(8,128)(2,1)S(1)}, u32[]{:S(2)}, u32[]{:S(2)}) %collective-permute-start.12) | collective-permute-done | bytes 65568 | tf_op jit(solution)/shard_map/ppermute | solution.py:454
  60.9 0.8 %widen.1 = f32[24,4,1024]{2,1,0:T(4,128)} custom-call(s32[1]{0:T(128)} %bitcast.mine_ref, bf16[32,1024]{1,0:T(8,128)(2,1)S(1)} %get-tuple-element.79.refs_0_, bf16[32,1024]{1,0:T(8,128)(2,1)S(1)} %collective-permute-done.10.refs_1_, bf16[32,1024]{1,0:T(8,128)(2,1)S(1)} %collective-permute-done.11.refs_2_, bf16[32,1024]{1,0:T(8,128)(2,1)S(1)} %collective-permute-done.12.refs_3_), custom_call_target="tpu_custom_call" | custom-call | tf_op jit(solution)/shard_map/widen/pallas_call | solution.py:408
  (26 shorter events, 1.6 us)
Async XLA Ops:
  0.0 29.4 %copy-start = (f32[2,128]{1,0:T(2,128)S(1)}, f32[2,128]{1,0:T(2,128)}, u32[]{:S(2)}) copy-start(f32[2,128]{1,0:T(2,128)} %constant.36.clone.refs_5_) | copy-start | bytes 3076
  1.8 0.7 %copy-start.1 = (s32[1,1,18,2]{2,3,1,0:T(2,128)S(1)}, s32[1,1,18,2]{2,3,1,0:T(2,128)}, u32[]{:S(2)}) copy-start(s32[1,1,18,2]{2,3,1,0:T(2,128)} %param.8) | copy-start | bytes 436
  3.1 11.5 %collective-permute-start.3 = (bf16[32,3200]{1,0:T(8,128)(2,1)S(1)}, bf16[32,3200]{1,0:T(8,128)(2,1)S(1)}, u32[]{:S(2)}, u32[]{:S(2)}) collective-permute-start(bf16[32,3200]{1,0:T(8,128)(2,1)S(1)} %get-tuple-element.52), channel_id=1, source_target_pairs={{0,3},{1,2},{2,1},{3,0},{4,7},{5,6},{6,5},{7,4},{8,11},{9,10},{10,... | collective-permute-start | bytes 614408 | tf_op jit(solution)/shard_map/ppermute | solution.py:429
  8.2 11.6 %collective-permute-start.4 = (bf16[32,3200]{1,0:T(8,128)(2,1)S(1)}, bf16[32,3200]{1,0:T(8,128)(2,1)S(1)}, u32[]{:S(2)}, u32[]{:S(2)}) collective-permute-start(bf16[32,3200]{1,0:T(8,128)(2,1)S(1)} %get-tuple-element.53), channel_id=1, source_target_pairs={{0,1},{1,0},{2,3},{3,2},{4,5},{5,4},{6,7},{7,6},{8,9},{9,8},{10,11... | collective-permute-start | bytes 614408 | tf_op jit(solution)/shard_map/ppermute | solution.py:429
  8.2 21.2 %collective-permute-start.5 = (bf16[32,3200]{1,0:T(8,128)(2,1)S(1)}, bf16[32,3200]{1,0:T(8,128)(2,1)S(1)}, u32[]{:S(2)}, u32[]{:S(2)}) collective-permute-start(bf16[32,3200]{1,0:T(8,128)(2,1)S(1)} %get-tuple-element.54), channel_id=1, source_target_pairs={{0,2},{1,3},{2,0},{3,1},{4,6},{5,7},{6,4},{7,5},{8,10},{9,11},{10,... | collective-permute-start | bytes 614408 | tf_op jit(solution)/shard_map/ppermute | solution.py:429
  10.8 25.0 %collective-permute-start = (bf16[32,1024]{1,0:T(8,128)(2,1)S(1)}, bf16[32,1024]{1,0:T(8,128)(2,1)S(1)}, u32[]{:S(2)}, u32[]{:S(2)}) collective-permute-start(bf16[32,1024]{1,0:T(8,128)(2,1)S(1)} %get-tuple-element.48), channel_id=1, source_target_pairs={{0,3},{1,2},{2,1},{3,0},{4,7},{5,6},{6,5},{7,4},{8,11},{9,10},{10,... | collective-permute-start | bytes 196616 | tf_op jit(solution)/shard_map/ppermute | solution.py:429
  14.6 21.2 %collective-permute-start.1 = (bf16[32,1024]{1,0:T(8,128)(2,1)S(1)}, bf16[32,1024]{1,0:T(8,128)(2,1)S(1)}, u32[]{:S(2)}, u32[]{:S(2)}) collective-permute-start(bf16[32,1024]{1,0:T(8,128)(2,1)S(1)} %get-tuple-element.49), channel_id=1, source_target_pairs={{0,1},{1,0},{2,3},{3,2},{4,5},{5,4},{6,7},{7,6},{8,9},{9,8},{10,11... | collective-permute-start | bytes 196616 | tf_op jit(solution)/shard_map/ppermute | solution.py:429
  14.6 21.2 %collective-permute-start.2 = (bf16[32,1024]{1,0:T(8,128)(2,1)S(1)}, bf16[32,1024]{1,0:T(8,128)(2,1)S(1)}, u32[]{:S(2)}, u32[]{:S(2)}) collective-permute-start(bf16[32,1024]{1,0:T(8,128)(2,1)S(1)} %get-tuple-element.50), channel_id=1, source_target_pairs={{0,2},{1,3},{2,0},{3,1},{4,6},{5,7},{6,4},{7,5},{8,10},{9,11},{10,... | collective-permute-start | bytes 196616 | tf_op jit(solution)/shard_map/ppermute | solution.py:429
  35.8 14.9 %copy-start.2 = (s32[1,1,18,1]{2,3,1,0:T(1,128)S(1)}, s32[1,1,18,1]{2,3,1,0:T(1,128)}, u32[]{:S(2)}) copy-start(s32[1,1,18,1]{2,3,1,0:T(1,128)} %param.9) | copy-start | bytes 220
  36.9 8.6 %collective-permute-start.6 = (bf16[72,1024]{1,0:T(8,128)(2,1)S(1)}, bf16[72,1024]{1,0:T(8,128)(2,1)S(1)}, u32[]{:S(2)}, u32[]{:S(2)}) collective-permute-start(bf16[72,1024]{1,0:T(8,128)(2,1)S(1)} %get-tuple-element.70), channel_id=1, source_target_pairs={{0,3},{1,2},{2,1},{3,0},{4,7},{5,6},{6,5},{7,4},{8,11},{9,10},{10,... | collective-permute-start | bytes 442376 | tf_op jit(solution)/shard_map/ppermute | solution.py:429
  39.7 11.0 %collective-permute-start.7 = (bf16[72,1024]{1,0:T(8,128)(2,1)S(1)}, bf16[72,1024]{1,0:T(8,128)(2,1)S(1)}, u32[]{:S(2)}, u32[]{:S(2)}) collective-permute-start(bf16[72,1024]{1,0:T(8,128)(2,1)S(1)} %get-tuple-element.71), channel_id=1, source_target_pairs={{0,2},{1,3},{2,0},{3,1},{4,6},{5,7},{6,4},{7,5},{8,10},{9,11},{10,... | collective-permute-start | bytes 442376 | tf_op jit(solution)/shard_map/ppermute | solution.py:429
  40.8 9.8 %collective-permute-start.8 = (bf16[72,1024]{1,0:T(8,128)(2,1)S(1)}, bf16[72,1024]{1,0:T(8,128)(2,1)S(1)}, u32[]{:S(2)}, u32[]{:S(2)}) collective-permute-start(bf16[72,1024]{1,0:T(8,128)(2,1)S(1)} %get-tuple-element.75), channel_id=1, source_target_pairs={{0,1},{1,0},{2,3},{3,2},{4,5},{5,4},{6,7},{7,6},{8,9},{9,8},{10,11... | collective-permute-start | bytes 442376 | tf_op jit(solution)/shard_map/ppermute | solution.py:429
  51.2 1.4 %collective-permute-start.9 = (bf16[64,1024]{1,0:T(8,128)(2,1)S(1)}, bf16[64,1024]{1,0:T(8,128)(2,1)S(1)}, u32[]{:S(2)}, u32[]{:S(2)}) collective-permute-start(bf16[64,1024]{1,0:T(8,128)(2,1)S(1)} %get-tuple-element.78), channel_id=1, source_target_pairs={{0,4},{4,0},{8,12},{12,8},{16,20},{20,16},{24,28},{28,24},{1,5},{5... | collective-permute-start | bytes 393224 | tf_op jit(solution)/shard_map/ppermute | solution.py:454
  52.6 4.3 %collective-permute-start.10 = (bf16[32,1024]{1,0:T(8,128)(2,1)S(1)}, bf16[32,1024]{1,0:T(8,128)(2,1)S(1)}, u32[]{:S(2)}, u32[]{:S(2)}) collective-permute-start(bf16[32,1024]{1,0:T(8,128)(2,1)S(1)} %get-tuple-element.80), channel_id=1, source_target_pairs={{0,8},{4,12},{8,0},{12,4},{16,24},{20,28},{24,16},{28,20},{1,9},{5... | collective-permute-start | bytes 196616 | tf_op jit(solution)/shard_map/ppermute | solution.py:454
  54.2 4.3 %collective-permute-start.11 = (bf16[32,1024]{1,0:T(8,128)(2,1)S(1)}, bf16[32,1024]{1,0:T(8,128)(2,1)S(1)}, u32[]{:S(2)}, u32[]{:S(2)}) collective-permute-start(bf16[32,1024]{1,0:T(8,128)(2,1)S(1)} %get-tuple-element.81), channel_id=1, source_target_pairs={{0,16},{4,20},{8,24},{12,28},{16,0},{20,4},{24,8},{28,12},{1,17},{... | collective-permute-start | bytes 196616 | tf_op jit(solution)/shard_map/ppermute | solution.py:454
  55.7 5.2 %collective-permute-start.12 = (bf16[32,1024]{1,0:T(8,128)(2,1)S(1)}, bf16[32,1024]{1,0:T(8,128)(2,1)S(1)}, u32[]{:S(2)}, u32[]{:S(2)}) collective-permute-start(bf16[32,1024]{1,0:T(8,128)(2,1)S(1)} %get-tuple-element.82), channel_id=1, source_target_pairs={{0,24},{4,28},{8,16},{12,20},{16,8},{20,12},{24,0},{28,4},{1,25},{... | collective-permute-start | bytes 196616 | tf_op jit(solution)/shard_map/ppermute | solution.py:454

commit v5 on v4

--- a/solution.py
+++ b/solution.py
@@ -20,7 +20,7 @@
 HALF = LAGS // 2
 ROOM = 4
 WAVES = 2
-LATE = 4
+LATE = 2
 
 
 def whiten_kernel(parts, place_ref, spec_ref, pairs_ref, *out_refs):
@@ -278,11 +278,13 @@
 
 
 def correlate(panels, table, place, parts, wanted, wave, before):
-    per_step = table.shape[0] // LANES // LATE
+    chunks = table.shape[0] // LANES
+    per_step = min(4, chunks // LATE)
     span = per_step * 2 * LANES
     rows = panels[0].shape[0]
-    early = LATE - 1
-    steps = 1 if wave else early
+    late = chunks // LATE // per_step
+    early = chunks // per_step - late
+    steps = late if wave else early
     lists = len(wanted)
     count = -(-lists * NB_SRC // 8) * 8
     each = NB_SRC * PAIRS
@@ -435,7 +437,10 @@
     first, second = whiten(spectra, pair_blocks[0, 0].T, place, parts)
     first = exchange(first)
     table = tables(place, chunks)
-    table, second = lax.optimization_barrier((table, second))
+    gates = [d for d in sequence(parts)[:2] if d]
+    here, second = lax.optimization_barrier(([first[d] for d in gates], second))
+    for d, panel in zip(gates, here):
+        first[d] = panel
     second = exchange(second)
 
     order = list(reversed(range(parts)))

time: 61.8 us -> 58.3 us (0.943)
  starting transfers between devices: 23 us -> 18.3 us
  waiting for transfers between devices: 23.6 us -> 24.9 us
    ppermute x9, starting transfers between devices: 19.4 us -> 14.7 us  [swap(): return lax.ppermute(array, 'chan', [(i, i ^ d) for i in range(parts)])]
    ppermute x9, waiting for transfers between devices: 17.6 us -> 18.9 us  [swap(): return lax.ppermute(array, 'chan', [(i, i ^ d) for i in range(parts)])]
  transfers between devices with their start and end apart: 13 -> 13, of which waited for: 7 -> 10; matrix products, arithmetic and copies ran while one was open for 1% -> 1% of each run, Pallas kernels for 14% -> 13%
where the time goes in v5:
time: 58.3 us; the launch traced here: 58.1 us
  waiting for transfers between devices  24.9 us (43%)
  starting transfers between devices  18.3 us (31%)
  Pallas kernels  11.7 us (20%)
  local copies, waits for them, and re-layouts  2.51 us (4%)
    ppermute x9, waiting for transfers between devices, swap(): return lax.ppermute(array, 'chan', [(i, i ^ d) for i in range(parts)])  18.9 us
    ppermute x9, starting transfers between devices, swap(): return lax.ppermute(array, 'chan', [(i, i ^ d) for i in range(parts)])  14.7 us
    pallas_call x4, Pallas kernels, correlate(): pl.pallas_call(functools.partial(corr_kernel, per_step, parts, lists, wav...  8.48 us
    ppermute x4, waiting for transfers between devices, trade(): return lax.ppermute(array, 'grp', [(i, i ^ m) for i in range(groups)])  6.03 us
    ppermute x4, starting transfers between devices, trade(): return lax.ppermute(array, 'grp', [(i, i ^ m) for i in range(groups)])  3.62 us
    reshape x1, local copies, waits for them, and re-layouts, whiten(): planes = jnp.transpose(spectra.reshape(rows, 2, F), (1, 0, 2))  1.82 us
    pallas_call x1, Pallas kernels, tables(): pl.pallas_call(table_kernel, grid_spec=pltpu.PrefetchScalarGridSpec(num_s...  1.33 us
  transfers between devices with their start and end apart: 13, of which 10 were waited for; matrix products, arithmetic and copies ran while one was open for 1% of the time, Pallas kernels for 13%

profile of v5, /device:TPU:0, one launch (start us, length us, event | category | flops | bytes accessed | tf_op | source)
XLA Modules:
  0.0 58.1 jit_solution(13576316189815367278)
XLA Ops:
  0.0 1.8 %copy.11 = bf16[32,2,8192]{2,0,1:T(8,128)(2,1)S(1)} copy(bf16[32,2,8192]{2,1,0:T(2,128)(2,1)} %bitcast.14) | data formatting | bytes 2097152 | tf_op jit(solution)/shard_map/reshape | solution.py:65
  3.1 5.1 %collective-permute-start = (bf16[32,2176]{1,0:T(8,128)(2,1)S(1)}, bf16[32,2176]{1,0:T(8,128)(2,1)S(1)}, u32[]{:S(2)}, u32[]{:S(2)}) collective-permute-start(bf16[32,2176]{1,0:T(8,128)(2,1)S(1)} %get-tuple-element.45), channel_id=1, source_target_pairs={{0,3},{1,2},{2,1},{3,0},{4,7},{5,6},{6,5},{7,4},{8,11},{9,10},{10,... | collective-permute-start | bytes 417800 | tf_op jit(solution)/shard_map/ppermute | solution.py:431
  9.4 3.4 %collective-permute-done.refs_0_.refs_6_ = bf16[32,2176]{1,0:T(8,128)(2,1)S(1)} collective-permute-done((bf16[32,2176]{1,0:T(8,128)(2,1)S(1)}, bf16[32,2176]{1,0:T(8,128)(2,1)S(1)}, u32[]{:S(2)}, u32[]{:S(2)}) %collective-permute-start) | collective-permute-done | bytes 139296 | tf_op jit(solution)/shard_map/ppermute | solution.py:431
  12.8 3.2 %collective-permute-done.1.refs_1_.refs_6_ = bf16[32,2176]{1,0:T(8,128)(2,1)S(1)} collective-permute-done((bf16[32,2176]{1,0:T(8,128)(2,1)S(1)}, bf16[32,2176]{1,0:T(8,128)(2,1)S(1)}, u32[]{:S(2)}, u32[]{:S(2)}) %collective-permute-start.1) | collective-permute-done | bytes 139296 | tf_op jit(solution)/shard_map/ppermute | solution.py:431
  16.0 1.8 %collective-permute-start.2 = (bf16[32,2048]{1,0:T(8,128)(2,1)S(1)}, bf16[32,2048]{1,0:T(8,128)(2,1)S(1)}, u32[]{:S(2)}, u32[]{:S(2)}) collective-permute-start(bf16[32,2048]{1,0:T(8,128)(2,1)S(1)} %get-tuple-element.51), channel_id=1, source_target_pairs={{0,3},{1,2},{2,1},{3,0},{4,7},{5,6},{6,5},{7,4},{8,11},{9,10},{10,... | collective-permute-start | bytes 393224 | tf_op jit(solution)/shard_map/ppermute | solution.py:431
  17.8 2.6 %collective-permute-start.4 = (bf16[32,2048]{1,0:T(8,128)(2,1)S(1)}, bf16[32,2048]{1,0:T(8,128)(2,1)S(1)}, u32[]{:S(2)}, u32[]{:S(2)}) collective-permute-start(bf16[32,2048]{1,0:T(8,128)(2,1)S(1)} %get-tuple-element.53), channel_id=1, source_target_pairs={{0,2},{1,3},{2,0},{3,1},{4,6},{5,7},{6,4},{7,5},{8,10},{9,11},{10,... | collective-permute-start | bytes 393224 | tf_op jit(solution)/shard_map/ppermute | solution.py:431
  20.4 1.3 %tables.1.refs_4_ = bf16[2048,1024]{1,0:T(8,128)(2,1)S(1)} custom-call(s32[1]{0:T(128)} %bitcast.2.place_ref.first_ref.place, f32[16,512]{1,0:T(8,128)S(1)} %get-tuple-element.91.hi_cos_ref, f32[16,512]{1,0:T(8,128)S(1)} %get-tuple-element.86.hi_sin_ref, f32[16,512]{1,0:T(8,128)S(1)} %get-tuple-element.92.mid_cos_ref, ...), custom_call_target="tpu_custom_call" | custom-call | flops 8388608 | bytes 4194304 | tf_op jit(solution)/shard_map/tables/pallas_call | solution.py:131
  21.8 1.6 %collective-permute-done.5.refs_2_.refs_7_ = bf16[32,2176]{1,0:T(8,128)(2,1)S(1)} collective-permute-done((bf16[32,2176]{1,0:T(8,128)(2,1)S(1)}, bf16[32,2176]{1,0:T(8,128)(2,1)S(1)}, u32[]{:S(2)}, u32[]{:S(2)}) %collective-permute-start.5) | collective-permute-done | bytes 139296 | tf_op jit(solution)/shard_map/ppermute | solution.py:431
  23.4 2.1 %correlate.5 = (f32[160,1024]{1,0:T(8,128)S(1)}, f32[160,128]{1,0:T(8,128)S(1)}, bf16[320,128]{1,0:T(8,128)(2,1)S(1)}) custom-call(s32[1]{0:T(128)} %bitcast.2.place_ref.first_ref.place, bf16[32,2176]{1,0:T(8,128)(2,1)S(1)} %collective-permute-done.refs_0_.refs_6_, bf16[32,2176]{1,0:T(8,128)(2,1)S(1)} %collective-permute-done.1.refs_1_.refs_6_, ...), custom_call_target="tpu_custom_call" | custom-call | flops 335544320 | bytes 2097152 | tf_op jit(solution)/shard_map/correlate/pallas_call | solution.py:309
  25.5 2.2 %correlate.4 = (f32[160,1024]{1,0:T(8,128)S(1)}, f32[160,128]{1,0:T(8,128)S(1)}, bf16[320,128]{1,0:T(8,128)(2,1)S(1)}) custom-call(s32[1]{0:T(128)} %bitcast.2.place_ref.first_ref.place, bf16[32,2176]{1,0:T(8,128)(2,1)S(1)} %collective-permute-done.refs_0_.refs_6_, bf16[32,2176]{1,0:T(8,128)(2,1)S(1)} %collective-permute-done.1.refs_1_.refs_6_, ...), custom_call_target="tpu_custom_call" | custom-call | flops 335544320 | bytes 2097152 | tf_op jit(solution)/shard_map/correlate/pallas_call | solution.py:309
  27.8 3.5 %collective-permute-done.4.refs_2_ = bf16[32,2048]{1,0:T(8,128)(2,1)S(1)} collective-permute-done((bf16[32,2048]{1,0:T(8,128)(2,1)S(1)}, bf16[32,2048]{1,0:T(8,128)(2,1)S(1)}, u32[]{:S(2)}, u32[]{:S(2)}) %collective-permute-start.4) | collective-permute-done | bytes 131104 | tf_op jit(solution)/shard_map/ppermute | solution.py:431
  31.3 2.1 %correlate.6 = (bf16[72,1024]{1,0:T(8,128)(2,1)S(1)}, bf16[72,1024]{1,0:T(8,128)(2,1)S(1)}) custom-call(s32[1]{0:T(128)} %bitcast.2.place_ref.first_ref.place, bf16[32,2048]{1,0:T(8,128)(2,1)S(1)} %collective-permute-done.2.refs_0_, bf16[32,2048]{1,0:T(8,128)(2,1)S(1)} %collective-permute-done.3.refs_1_, ...), custom_call_target="tpu_custom_call" | custom-call | flops 335544320 | bytes 2097152 | tf_op jit(solution)/shard_map/correlate/pallas_call | solution.py:309
  33.3 2.5 %collective-permute-start.6 = (bf16[72,1024]{1,0:T(8,128)(2,1)S(1)}, bf16[72,1024]{1,0:T(8,128)(2,1)S(1)}, u32[]{:S(2)}, u32[]{:S(2)}) collective-permute-start(bf16[72,1024]{1,0:T(8,128)(2,1)S(1)} %get-tuple-element.72), channel_id=1, source_target_pairs={{0,3},{1,2},{2,1},{3,0},{4,7},{5,6},{6,5},{7,4},{8,11},{9,10},{10,... | collective-permute-start | bytes 442376 | tf_op jit(solution)/shard_map/ppermute | solution.py:431
  35.9 2.1 %correlate.7 = (bf16[72,1024]{1,0:T(8,128)(2,1)S(1)}, bf16[72,1024]{1,0:T(8,128)(2,1)S(1)}) custom-call(s32[1]{0:T(128)} %bitcast.2.place_ref.first_ref.place, bf16[32,2048]{1,0:T(8,128)(2,1)S(1)} %collective-permute-done.2.refs_0_, bf16[32,2048]{1,0:T(8,128)(2,1)S(1)} %collective-permute-done.3.refs_1_, ...), custom_call_target="tpu_custom_call" | custom-call | flops 335544320 | bytes 2097152 | tf_op jit(solution)/shard_map/correlate/pallas_call | solution.py:309
  38.0 2.0 %collective-permute-start.8 = (bf16[72,1024]{1,0:T(8,128)(2,1)S(1)}, bf16[72,1024]{1,0:T(8,128)(2,1)S(1)}, u32[]{:S(2)}, u32[]{:S(2)}) collective-permute-start(bf16[72,1024]{1,0:T(8,128)(2,1)S(1)} %get-tuple-element.77), channel_id=1, source_target_pairs={{0,1},{1,0},{2,3},{3,2},{4,5},{5,4},{6,7},{7,6},{8,9},{9,8},{10,11... | collective-permute-start | bytes 442376 | tf_op jit(solution)/shard_map/ppermute | solution.py:431
  39.9 2.0 %collective-permute-done.6.refs_0_ = bf16[72,1024]{1,0:T(8,128)(2,1)S(1)} collective-permute-done((bf16[72,1024]{1,0:T(8,128)(2,1)S(1)}, bf16[72,1024]{1,0:T(8,128)(2,1)S(1)}, u32[]{:S(2)}, u32[]{:S(2)}) %collective-permute-start.6) | collective-permute-done | bytes 147488 | tf_op jit(solution)/shard_map/ppermute | solution.py:431
  41.9 5.2 %collective-permute-done.7.refs_1_ = bf16[72,1024]{1,0:T(8,128)(2,1)S(1)} collective-permute-done((bf16[72,1024]{1,0:T(8,128)(2,1)S(1)}, bf16[72,1024]{1,0:T(8,128)(2,1)S(1)}, u32[]{:S(2)}, u32[]{:S(2)}) %collective-permute-start.7) | collective-permute-done | bytes 147488 | tf_op jit(solution)/shard_map/ppermute | solution.py:431
  47.7 1.3 %collective-permute-done.9.brought_ref = bf16[64,1024]{1,0:T(8,128)(2,1)S(1)} collective-permute-done((bf16[64,1024]{1,0:T(8,128)(2,1)S(1)}, bf16[64,1024]{1,0:T(8,128)(2,1)S(1)}, u32[]{:S(2)}, u32[]{:S(2)}) %collective-permute-start.9) | collective-permute-done | bytes 131104 | tf_op jit(solution)/shard_map/ppermute | solution.py:459
  49.1 1.6 %collective-permute-start.10 = (bf16[32,1024]{1,0:T(8,128)(2,1)S(1)}, bf16[32,1024]{1,0:T(8,128)(2,1)S(1)}, u32[]{:S(2)}, u32[]{:S(2)}) collective-permute-start(bf16[32,1024]{1,0:T(8,128)(2,1)S(1)} %get-tuple-element.82), channel_id=1, source_target_pairs={{0,8},{4,12},{8,0},{12,4},{16,24},{20,28},{24,16},{28,20},{1,9},{5... | collective-permute-start | bytes 196616 | tf_op jit(solution)/shard_map/ppermute | solution.py:459
  50.7 1.5 %collective-permute-start.11 = (bf16[32,1024]{1,0:T(8,128)(2,1)S(1)}, bf16[32,1024]{1,0:T(8,128)(2,1)S(1)}, u32[]{:S(2)}, u32[]{:S(2)}) collective-permute-start(bf16[32,1024]{1,0:T(8,128)(2,1)S(1)} %get-tuple-element.83), channel_id=1, source_target_pairs={{0,16},{4,20},{8,24},{12,28},{16,0},{20,4},{24,8},{28,12},{1,17},{... | collective-permute-start | bytes 196616 | tf_op jit(solution)/shard_map/ppermute | solution.py:459
  52.6 0.8 %collective-permute-done.10.refs_1_ = bf16[32,1024]{1,0:T(8,128)(2,1)S(1)} collective-permute-done((bf16[32,1024]{1,0:T(8,128)(2,1)S(1)}, bf16[32,1024]{1,0:T(8,128)(2,1)S(1)}, u32[]{:S(2)}, u32[]{:S(2)}) %collective-permute-start.10) | collective-permute-done | bytes 65568 | tf_op jit(solution)/shard_map/ppermute | solution.py:459
  53.4 1.5 %collective-permute-done.11.refs_2_ = bf16[32,1024]{1,0:T(8,128)(2,1)S(1)} collective-permute-done((bf16[32,1024]{1,0:T(8,128)(2,1)S(1)}, bf16[32,1024]{1,0:T(8,128)(2,1)S(1)}, u32[]{:S(2)}, u32[]{:S(2)}) %collective-permute-start.11) | collective-permute-done | bytes 65568 | tf_op jit(solution)/shard_map/ppermute | solution.py:459
  54.9 2.4 %collective-permute-done.12.refs_3_ = bf16[32,1024]{1,0:T(8,128)(2,1)S(1)} collective-permute-done((bf16[32,1024]{1,0:T(8,128)(2,1)S(1)}, bf16[32,1024]{1,0:T(8,128)(2,1)S(1)}, u32[]{:S(2)}, u32[]{:S(2)}) %collective-permute-start.12) | collective-permute-done | bytes 65568 | tf_op jit(solution)/shard_map/ppermute | solution.py:459
  57.3 0.8 %widen.1 = f32[24,4,1024]{2,1,0:T(4,128)} custom-call(s32[1]{0:T(128)} %bitcast.mine_ref, bf16[32,1024]{1,0:T(8,128)(2,1)S(1)} %get-tuple-element.81.refs_0_, bf16[32,1024]{1,0:T(8,128)(2,1)S(1)} %collective-permute-done.10.refs_1_, bf16[32,1024]{1,0:T(8,128)(2,1)S(1)} %collective-permute-done.11.refs_2_, bf16[32,1024]{1,0:T(8,128)(2,1)S(1)} %collective-permute-done.12.refs_3_), custom_call_target="tpu_custom_call" | custom-call | tf_op jit(solution)/shard_map/widen/pallas_call | solution.py:410
  (26 shorter events, 3.6 us)
Async XLA Ops:
  0.0 23.4 %copy-start = (f32[2,128]{1,0:T(2,128)S(1)}, f32[2,128]{1,0:T(2,128)}, u32[]{:S(2)}) copy-start(f32[2,128]{1,0:T(2,128)} %constant.36.clone.refs_5_) | copy-start | bytes 3076
  1.8 0.7 %copy-start.1 = (s32[1,1,18,2]{2,3,1,0:T(2,128)S(1)}, s32[1,1,18,2]{2,3,1,0:T(2,128)}, u32[]{:S(2)}) copy-start(s32[1,1,18,2]{2,3,1,0:T(2,128)} %param.8) | copy-start | bytes 436
  3.1 9.7 %collective-permute-start = (bf16[32,2176]{1,0:T(8,128)(2,1)S(1)}, bf16[32,2176]{1,0:T(8,128)(2,1)S(1)}, u32[]{:S(2)}, u32[]{:S(2)}) collective-permute-start(bf16[32,2176]{1,0:T(8,128)(2,1)S(1)} %get-tuple-element.45), channel_id=1, source_target_pairs={{0,3},{1,2},{2,1},{3,0},{4,7},{5,6},{6,5},{7,4},{8,11},{9,10},{10,... | collective-permute-start | bytes 417800 | tf_op jit(solution)/shard_map/ppermute | solution.py:431
  8.2 7.7 %collective-permute-start.1 = (bf16[32,2176]{1,0:T(8,128)(2,1)S(1)}, bf16[32,2176]{1,0:T(8,128)(2,1)S(1)}, u32[]{:S(2)}, u32[]{:S(2)}) collective-permute-start(bf16[32,2176]{1,0:T(8,128)(2,1)S(1)} %get-tuple-element.46), channel_id=1, source_target_pairs={{0,1},{1,0},{2,3},{3,2},{4,5},{5,4},{6,7},{7,6},{8,9},{9,8},{10,11... | collective-permute-start | bytes 417800 | tf_op jit(solution)/shard_map/ppermute | solution.py:431
  8.2 15.1 %collective-permute-start.5 = (bf16[32,2176]{1,0:T(8,128)(2,1)S(1)}, bf16[32,2176]{1,0:T(8,128)(2,1)S(1)}, u32[]{:S(2)}, u32[]{:S(2)}) collective-permute-start(bf16[32,2176]{1,0:T(8,128)(2,1)S(1)} %get-tuple-element.57), channel_id=1, source_target_pairs={{0,2},{1,3},{2,0},{3,1},{4,6},{5,7},{6,4},{7,5},{8,10},{9,11},{10,... | collective-permute-start | bytes 417800 | tf_op jit(solution)/shard_map/ppermute | solution.py:431
  16.0 11.7 %collective-permute-start.2 = (bf16[32,2048]{1,0:T(8,128)(2,1)S(1)}, bf16[32,2048]{1,0:T(8,128)(2,1)S(1)}, u32[]{:S(2)}, u32[]{:S(2)}) collective-permute-start(bf16[32,2048]{1,0:T(8,128)(2,1)S(1)} %get-tuple-element.51), channel_id=1, source_target_pairs={{0,3},{1,2},{2,1},{3,0},{4,7},{5,6},{6,5},{7,4},{8,11},{9,10},{10,... | collective-permute-start | bytes 393224 | tf_op jit(solution)/shard_map/ppermute | solution.py:431
  17.8 10.0 %collective-permute-start.3 = (bf16[32,2048]{1,0:T(8,128)(2,1)S(1)}, bf16[32,2048]{1,0:T(8,128)(2,1)S(1)}, u32[]{:S(2)}, u32[]{:S(2)}) collective-permute-start(bf16[32,2048]{1,0:T(8,128)(2,1)S(1)} %get-tuple-element.52), channel_id=1, source_target_pairs={{0,1},{1,0},{2,3},{3,2},{4,5},{5,4},{6,7},{7,6},{8,9},{9,8},{10,11... | collective-permute-start | bytes 393224 | tf_op jit(solution)/shard_map/ppermute | solution.py:431
  17.8 13.5 %collective-permute-start.4 = (bf16[32,2048]{1,0:T(8,128)(2,1)S(1)}, bf16[32,2048]{1,0:T(8,128)(2,1)S(1)}, u32[]{:S(2)}, u32[]{:S(2)}) collective-permute-start(bf16[32,2048]{1,0:T(8,128)(2,1)S(1)} %get-tuple-element.53), channel_id=1, source_target_pairs={{0,2},{1,3},{2,0},{3,1},{4,6},{5,7},{6,4},{7,5},{8,10},{9,11},{10,... | collective-permute-start | bytes 393224 | tf_op jit(solution)/shard_map/ppermute | solution.py:431
  31.3 15.9 %copy-start.2 = (s32[1,1,18,1]{2,3,1,0:T(1,128)S(1)}, s32[1,1,18,1]{2,3,1,0:T(1,128)}, u32[]{:S(2)}) copy-start(s32[1,1,18,1]{2,3,1,0:T(1,128)} %param.9) | copy-start | bytes 220
  33.3 8.6 %collective-permute-start.6 = (bf16[72,1024]{1,0:T(8,128)(2,1)S(1)}, bf16[72,1024]{1,0:T(8,128)(2,1)S(1)}, u32[]{:S(2)}, u32[]{:S(2)}) collective-permute-start(bf16[72,1024]{1,0:T(8,128)(2,1)S(1)} %get-tuple-element.72), channel_id=1, source_target_pairs={{0,3},{1,2},{2,1},{3,0},{4,7},{5,6},{6,5},{7,4},{8,11},{9,10},{10,... | collective-permute-start | bytes 442376 | tf_op jit(solution)/shard_map/ppermute | solution.py:431
  35.9 11.2 %collective-permute-start.7 = (bf16[72,1024]{1,0:T(8,128)(2,1)S(1)}, bf16[72,1024]{1,0:T(8,128)(2,1)S(1)}, u32[]{:S(2)}, u32[]{:S(2)}) collective-permute-start(bf16[72,1024]{1,0:T(8,128)(2,1)S(1)} %get-tuple-element.73), channel_id=1, source_target_pairs={{0,2},{1,3},{2,0},{3,1},{4,6},{5,7},{6,4},{7,5},{8,10},{9,11},{10,... | collective-permute-start | bytes 442376 | tf_op jit(solution)/shard_map/ppermute | solution.py:431
  38.0 9.2 %collective-permute-start.8 = (bf16[72,1024]{1,0:T(8,128)(2,1)S(1)}, bf16[72,1024]{1,0:T(8,128)(2,1)S(1)}, u32[]{:S(2)}, u32[]{:S(2)}) collective-permute-start(bf16[72,1024]{1,0:T(8,128)(2,1)S(1)} %get-tuple-element.77), channel_id=1, source_target_pairs={{0,1},{1,0},{2,3},{3,2},{4,5},{5,4},{6,7},{7,6},{8,9},{9,8},{10,11... | collective-permute-start | bytes 442376 | tf_op jit(solution)/shard_map/ppermute | solution.py:431
  47.6 1.4 %collective-permute-start.9 = (bf16[64,1024]{1,0:T(8,128)(2,1)S(1)}, bf16[64,1024]{1,0:T(8,128)(2,1)S(1)}, u32[]{:S(2)}, u32[]{:S(2)}) collective-permute-start(bf16[64,1024]{1,0:T(8,128)(2,1)S(1)} %get-tuple-element.80), channel_id=1, source_target_pairs={{0,4},{4,0},{8,12},{12,8},{16,20},{20,16},{24,28},{28,24},{1,5},{5... | collective-permute-start | bytes 393224 | tf_op jit(solution)/shard_map/ppermute | solution.py:459
  49.1 4.3 %collective-permute-start.10 = (bf16[32,1024]{1,0:T(8,128)(2,1)S(1)}, bf16[32,1024]{1,0:T(8,128)(2,1)S(1)}, u32[]{:S(2)}, u32[]{:S(2)}) collective-permute-start(bf16[32,1024]{1,0:T(8,128)(2,1)S(1)} %get-tuple-element.82), channel_id=1, source_target_pairs={{0,8},{4,12},{8,0},{12,4},{16,24},{20,28},{24,16},{28,20},{1,9},{5... | collective-permute-start | bytes 196616 | tf_op jit(solution)/shard_map/ppermute | solution.py:459
  50.7 4.3 %collective-permute-start.11 = (bf16[32,1024]{1,0:T(8,128)(2,1)S(1)}, bf16[32,1024]{1,0:T(8,128)(2,1)S(1)}, u32[]{:S(2)}, u32[]{:S(2)}) collective-permute-start(bf16[32,1024]{1,0:T(8,128)(2,1)S(1)} %get-tuple-element.83), channel_id=1, source_target_pairs={{0,16},{4,20},{8,24},{12,28},{16,0},{20,4},{24,8},{28,12},{1,17},{... | collective-permute-start | bytes 196616 | tf_op jit(solution)/shard_map/ppermute | solution.py:459
  52.2 5.2 %collective-permute-start.12 = (bf16[32,1024]{1,0:T(8,128)(2,1)S(1)}, bf16[32,1024]{1,0:T(8,128)(2,1)S(1)}, u32[]{:S(2)}, u32[]{:S(2)}) collective-permute-start(bf16[32,1024]{1,0:T(8,128)(2,1)S(1)} %get-tuple-element.84), channel_id=1, source_target_pairs={{0,24},{4,28},{8,16},{12,20},{16,8},{20,12},{24,0},{28,4},{1,25},{... | collective-permute-start | bytes 196616 | tf_op jit(solution)/shard_map/ppermute | solution.py:459

commit v6 on v5

--- a/solution.py
+++ b/solution.py
@@ -23,9 +23,13 @@
 LATE = 2
 
 
+def works(place):
+    return bool((place ^ (place >> 1)) & 1)
+
+
 def whiten_kernel(parts, place_ref, spec_ref, pairs_ref, *out_refs):
     blocks = F // LANES
-    each = blocks // parts
+    each = blocks // (parts // 2)
     late = each // LATE
     place = place_ref[0]
 
@@ -51,7 +55,7 @@
     level = 0.1 * (total * (1.0 / F) + 1e-05)
     for index, out_ref in enumerate(out_refs):
         wave, d = divmod(index, parts)
-        first = jnp.bitwise_xor(place, d) * each + wave * (each - late)
+        first = lax.shift_right_logical(jnp.bitwise_xor(place, d), 1) * each + wave * (each - late)
         for k in range(late if wave else each - late):
             re, im, power = values(pl.multiple_of((first + k) * LANES, LANES))
             scale = lax.rsqrt(power + level)
@@ -63,7 +67,7 @@
 def whiten(spectra, pairs, place, parts):
     rows = spectra.shape[0] * WINDOWS
     planes = jnp.transpose(spectra.reshape(rows, 2, F), (1, 0, 2))
-    width = 2 * F // parts
+    width = 2 * F // (parts // 2)
     late = width // LATE
     shapes = [(rows, width - late + LANES)] * parts + [(rows, late)] * parts
     whole = lambda array: pl.BlockSpec(array.shape, lambda i, place: (0,) * array.ndim)
@@ -207,7 +211,7 @@
     reals = []
     imags = []
     lane = iota((1, LANES), 1)
-    first_bin = jnp.logical_and(jnp.logical_and(place[0] == 0, step == 0), lane == 0)
+    first_bin = jnp.logical_and(jnp.logical_and(place[0] < 2, step == 0), lane == 0)
     edge_part = 0.0
     for i in range(per_step):
         at = i * 2 * LANES
@@ -354,13 +358,15 @@
     block = jnp.dot(block, over, preferred_element_type=jnp.float32)
     same = jnp.bitwise_and(iota((rows, each), 0), PAIRS - 1) == jnp.bitwise_and(iota((rows, each), 1), PAIRS - 1)
     chosen = jnp.where(same, block, 0.0).astype(jnp.bfloat16)
-    total = sum(ref[...].astype(jnp.float32) for ref in part_refs)
+    total = jnp.where(mine_ref[1] == 1, part_refs[-1][...].astype(jnp.float32), 0.0)
+    for ref in part_refs[:-1]:
+        total = total + ref[...].astype(jnp.float32)
     placed = jnp.dot(chosen, total.astype(jnp.bfloat16), preferred_element_type=jnp.float32)
     for i, out_ref in enumerate(out_refs):
         out_ref[...] = placed[i * rows // 2 : (i + 1) * rows // 2].astype(jnp.bfloat16)
 
 
-def settle(owners, partials, mine, groups):
+def settle(owners, partials, mine, working, groups):
     whole = lambda array: pl.BlockSpec(array.shape, lambda i, mine: (0, 0))
     outs = [jax.ShapeDtypeStruct((groups * ROOM * PAIRS // 2, LAGS), jnp.bfloat16)] * 2
     return list(pl.pallas_call(
@@ -374,7 +380,7 @@
         out_shape=outs,
         compiler_params=pltpu.CompilerParams(vmem_limit_bytes=VMEM_LIMIT),
         name="settle",
-    )(mine[None], owners, *partials))
+    )(jnp.stack([mine, working]), owners, *partials))
 
 
 def bundle_kernel(kept_ref, brought_ref, *out_refs):
@@ -425,18 +431,21 @@
     groups = lax.axis_size("grp")
     parts = lax.axis_size("chan")
     place = lax.axis_index("chan")
-    chunks = F // LANES // parts
-
-    def swap(array, d):
-        return lax.ppermute(array, "chan", [(i, i ^ d) for i in range(parts)])
+    chunks = F // LANES // (parts // 2)
+    rank = lax.shift_right_logical(place, 1)
+    working = jnp.bitwise_and(jnp.bitwise_xor(place, rank), 1)
+
+    def swap(array, d, back):
+        pairs = [(i, i ^ d) for i in range(parts) if works(i if back else i ^ d)]
+        return lax.ppermute(array, "chan", pairs)
 
     def exchange(panels):
-        moved = {d: swap(panels[d], d) for d in sequence(parts)[:-1]}
+        moved = {d: swap(panels[d], d, False) for d in sequence(parts)[:-1]}
         return panels[:1] + [moved[d] for d in range(1, parts)]
 
     first, second = whiten(spectra, pair_blocks[0, 0].T, place, parts)
     first = exchange(first)
-    table = tables(place, chunks)
+    table = tables(rank, chunks)
     gates = [d for d in sequence(parts)[:2] if d]
     here, second = lax.optimization_barrier(([first[d] for d in gates], second))
     for d, panel in zip(gates, here):
@@ -452,13 +461,13 @@
     partials = []
     for wanted, before in zip(halves, sums):
         for d, rows in zip(wanted, correlate(second, table, place, parts, wanted, 1, before)):
-            partials.append(swap(rows, d) if d else rows)
+            partials.append(swap(rows, d, True) if d else rows)
     mine = lax.axis_index("grp")
 
     def trade(array, m):
         return lax.ppermute(array, "grp", [(i, i ^ m) for i in range(groups)])
 
-    kept, cross = settle(owners[0, 0].T, partials, mine, groups)
+    kept, cross = settle(owners[0, 0].T, partials, mine, working, groups)
     pieces = bundle(kept, trade(cross, 1))
     for j in reversed(range(1, groups // 2)):
         pieces[j] = trade(pieces[j], 2 * j)

time: 58.3 us -> 67.2 us (1.15)
  Pallas kernels: 11.7 us -> 21.2 us
  waiting for transfers between devices: 24.9 us -> 16.6 us
  starting transfers between devices: 18.3 us -> 25.7 us
    ppermute x9, waiting for transfers between devices: 18.9 us -> 10.5 us  [swap(): return lax.ppermute(array, 'chan', pairs)]
    ppermute x9, starting transfers between devices: 14.7 us -> 22 us  [swap(): return lax.ppermute(array, 'chan', pairs)]
    pallas_call x4, Pallas kernels: 8.48 us -> 15.7 us  [correlate(): pl.pallas_call(functools.partial(corr_kernel, per_step, parts, lists, wav...]
    pallas_call x1, Pallas kernels: 1.33 us -> 2.58 us  [tables(): pl.pallas_call(table_kernel, grid_spec=pltpu.PrefetchScalarGridSpec(num_s...]
  transfers between devices with their start and end apart: 13 -> 13, of which waited for: 10 -> 7; matrix products, arithmetic and copies ran while one was open for 1% -> 1% of each run, Pallas kernels for 13% -> 22%
where the time goes in v6:
time: 67.2 us; the launch traced here: 66.9 us
  starting transfers between devices  25.7 us (38%)
  Pallas kernels  21.2 us (32%)
  waiting for transfers between devices  16.6 us (25%)
  local copies, waits for them, and re-layouts  2.52 us (4%)
  other arithmetic  0.7 us (1%)
    ppermute x9, starting transfers between devices, swap(): return lax.ppermute(array, 'chan', pairs)  22 us
    pallas_call x4, Pallas kernels, correlate(): pl.pallas_call(functools.partial(corr_kernel, per_step, parts, lists, wav...  15.7 us
    ppermute x9, waiting for transfers between devices, swap(): return lax.ppermute(array, 'chan', pairs)  10.5 us
    ppermute x4, waiting for transfers between devices, trade(): return lax.ppermute(array, 'grp', [(i, i ^ m) for i in range(groups)])  6.02 us
    ppermute x4, starting transfers between devices, trade(): return lax.ppermute(array, 'grp', [(i, i ^ m) for i in range(groups)])  3.62 us
    pallas_call x1, Pallas kernels, tables(): pl.pallas_call(table_kernel, grid_spec=pltpu.PrefetchScalarGridSpec(num_s...  2.58 us
    reshape x1, local copies, waits for them, and re-layouts, whiten(): planes = jnp.transpose(spectra.reshape(rows, 2, F), (1, 0, 2))  1.82 us
  transfers between devices with their start and end apart: 13, of which 7 were waited for; matrix products, arithmetic and copies ran while one was open for 1% of the time, Pallas kernels for 22%

profile of v6, /device:TPU:0, one launch (start us, length us, event | category | flops | bytes accessed | tf_op | source)
XLA Modules:
  0.0 66.9 jit_solution(1512928761009050805)
XLA Ops:
  0.0 1.8 %copy.11 = bf16[32,2,8192]{2,0,1:T(8,128)(2,1)S(1)} copy(bf16[32,2,8192]{2,1,0:T(2,128)(2,1)} %bitcast.16) | data formatting | bytes 2097152 | tf_op jit(solution)/shard_map/reshape | solution.py:69
  2.5 1.0 %whiten.1 = (bf16[32,4224]{1,0:T(8,128)(2,1)S(1)}, bf16[32,4224]{1,0:T(8,128)(2,1)S(1)}, bf16[32,4224]{1,0:T(8,128)(2,1)S(1)}, bf16[32,4224]{1,0:T(8,128)(2,1)S(...) custom-call(s32[1]{0:T(128)} %bitcast.3.place_ref.place, ...), custom_call_target="tpu_custom_call" | custom-call | tf_op jit(solution)/shard_map/whiten/pallas_call | solution.py:74
  4.2 7.8 %collective-permute-start.1 = (bf16[32,4224]{1,0:T(8,128)(2,1)S(1)}, bf16[32,4224]{1,0:T(8,128)(2,1)S(1)}, u32[]{:S(2)}, u32[]{:S(2)}) collective-permute-start(bf16[32,4224]{1,0:T(8,128)(2,1)S(1)} %get-tuple-element.46), channel_id=1, source_target_pairs={{0,1},{3,2},{4,5},{7,6},{8,9},{11,10},{12,13},{15,14},{16,17},{19,... | collective-permute-start | bytes 811016 | tf_op jit(solution)/shard_map/ppermute | solution.py:440
  12.0 1.3 %collective-permute-start.5 = (bf16[32,4224]{1,0:T(8,128)(2,1)S(1)}, bf16[32,4224]{1,0:T(8,128)(2,1)S(1)}, u32[]{:S(2)}, u32[]{:S(2)}) collective-permute-start(bf16[32,4224]{1,0:T(8,128)(2,1)S(1)} %get-tuple-element.57), channel_id=1, source_target_pairs={{0,2},{3,1},{4,6},{7,5},{8,10},{11,9},{12,14},{15,13},{16,18},{19,... | collective-permute-start | bytes 811016 | tf_op jit(solution)/shard_map/ppermute | solution.py:440
  14.0 4.9 %collective-permute-done.1.refs_1_.refs_6_ = bf16[32,4224]{1,0:T(8,128)(2,1)S(1)} collective-permute-done((bf16[32,4224]{1,0:T(8,128)(2,1)S(1)}, bf16[32,4224]{1,0:T(8,128)(2,1)S(1)}, u32[]{:S(2)}, u32[]{:S(2)}) %collective-permute-start.1) | collective-permute-done | bytes 270368 | tf_op jit(solution)/shard_map/ppermute | solution.py:440
  19.5 6.1 %collective-permute-start.3 = (bf16[32,4096]{1,0:T(8,128)(2,1)S(1)}, bf16[32,4096]{1,0:T(8,128)(2,1)S(1)}, u32[]{:S(2)}, u32[]{:S(2)}) collective-permute-start(bf16[32,4096]{1,0:T(8,128)(2,1)S(1)} %get-tuple-element.52), channel_id=1, source_target_pairs={{0,1},{3,2},{4,5},{7,6},{8,9},{11,10},{12,13},{15,14},{16,17},{19,... | collective-permute-start | bytes 786440 | tf_op jit(solution)/shard_map/ppermute | solution.py:440
  25.6 2.3 %collective-permute-start.4 = (bf16[32,4096]{1,0:T(8,128)(2,1)S(1)}, bf16[32,4096]{1,0:T(8,128)(2,1)S(1)}, u32[]{:S(2)}, u32[]{:S(2)}) collective-permute-start(bf16[32,4096]{1,0:T(8,128)(2,1)S(1)} %get-tuple-element.53), channel_id=1, source_target_pairs={{0,2},{3,1},{4,6},{7,5},{8,10},{11,9},{12,14},{15,13},{16,18},{19,... | collective-permute-start | bytes 786440 | tf_op jit(solution)/shard_map/ppermute | solution.py:440
  28.0 2.6 %tables.1.refs_4_ = bf16[4096,1024]{1,0:T(8,128)(2,1)S(1)} custom-call(s32[1]{0:T(128)} %bitcast.8.first_ref, f32[32,512]{1,0:T(8,128)S(1)} %get-tuple-element.88.hi_cos_ref, f32[32,512]{1,0:T(8,128)S(1)} %get-tuple-element.87.hi_sin_ref, f32[16,512]{1,0:T(8,128)S(1)} %slice.26.mid_cos_ref, f32[16,512]{1,0:T(8,128)S(1)} %slice.27.mid_sin_ref, ...), custom_call_target="tpu_custom_call" | custom-call | flops 16777216 | bytes 8388608 | tf_op jit(solution)/shard_map/tables/pallas_call | solution.py:135
  30.6 4.2 %correlate.4 = (f32[160,1024]{1,0:T(8,128)S(1)}, f32[160,128]{1,0:T(8,128)S(1)}, bf16[320,128]{1,0:T(8,128)(2,1)S(1)}) custom-call(s32[1]{0:T(128)} %bitcast.3.place_ref.place, bf16[32,4224]{1,0:T(8,128)(2,1)S(1)} %collective-permute-done.refs_0_.refs_6_, bf16[32,4224]{1,0:T(8,128)(2,1)S(1)} %collective-permute-done.1.refs_1_.refs_6_, ...), custom_call_target="tpu_custom_call" | custom-call | flops 671088640 | bytes 4194304 | tf_op jit(solution)/shard_map/correlate/pallas_call | solution.py:313
  34.7 4.2 %correlate.5 = (f32[160,1024]{1,0:T(8,128)S(1)}, f32[160,128]{1,0:T(8,128)S(1)}, bf16[320,128]{1,0:T(8,128)(2,1)S(1)}) custom-call(s32[1]{0:T(128)} %bitcast.3.place_ref.place, bf16[32,4224]{1,0:T(8,128)(2,1)S(1)} %collective-permute-done.refs_0_.refs_6_, bf16[32,4224]{1,0:T(8,128)(2,1)S(1)} %collective-permute-done.1.refs_1_.refs_6_, ...), custom_call_target="tpu_custom_call" | custom-call | flops 671088640 | bytes 4194304 | tf_op jit(solution)/shard_map/correlate/pallas_call | solution.py:313
  39.0 3.7 %correlate.6 = (bf16[72,1024]{1,0:T(8,128)(2,1)S(1)}, bf16[72,1024]{1,0:T(8,128)(2,1)S(1)}) custom-call(s32[1]{0:T(128)} %bitcast.3.place_ref.place, bf16[32,4096]{1,0:T(8,128)(2,1)S(1)} %collective-permute-done.2.refs_0_, bf16[32,4096]{1,0:T(8,128)(2,1)S(1)} %collective-permute-done.3.refs_1_, bf16[32,4096]{1,0:T(8,128)(2,1)S(1)} %collective-permute-done.4.refs_2_, ...), custom_call_target="tpu_custom_call" | custom-call | flops 671088640 | bytes 4194304 | tf_op jit(solution)/shard_map/correlate/pallas_call | solution.py:313
  43.4 1.3 %collective-permute-start.7 = (bf16[72,1024]{1,0:T(8,128)(2,1)S(1)}, bf16[72,1024]{1,0:T(8,128)(2,1)S(1)}, u32[]{:S(2)}, u32[]{:S(2)}) collective-permute-start(bf16[72,1024]{1,0:T(8,128)(2,1)S(1)} %get-tuple-element.73), channel_id=1, source_target_pairs={{1,3},{2,0},{5,7},{6,4},{9,11},{10,8},{13,15},{14,12},{17,19},{18,... | collective-permute-start | bytes 442376 | tf_op jit(solution)/shard_map/ppermute | solution.py:440
  44.7 3.7 %correlate.7 = (bf16[72,1024]{1,0:T(8,128)(2,1)S(1)}, bf16[72,1024]{1,0:T(8,128)(2,1)S(1)}) custom-call(s32[1]{0:T(128)} %bitcast.3.place_ref.place, bf16[32,4096]{1,0:T(8,128)(2,1)S(1)} %collective-permute-done.2.refs_0_, bf16[32,4096]{1,0:T(8,128)(2,1)S(1)} %collective-permute-done.3.refs_1_, bf16[32,4096]{1,0:T(8,128)(2,1)S(1)} %collective-permute-done.4.refs_2_, ...), custom_call_target="tpu_custom_call" | custom-call | flops 671088640 | bytes 4194304 | tf_op jit(solution)/shard_map/correlate/pallas_call | solution.py:313
  48.4 1.3 %collective-permute-start.8 = (bf16[72,1024]{1,0:T(8,128)(2,1)S(1)}, bf16[72,1024]{1,0:T(8,128)(2,1)S(1)}, u32[]{:S(2)}, u32[]{:S(2)}) collective-permute-start(bf16[72,1024]{1,0:T(8,128)(2,1)S(1)} %get-tuple-element.77), channel_id=1, source_target_pairs={{1,0},{2,3},{5,4},{6,7},{9,8},{10,11},{13,12},{14,15},{17,16},{18,... | collective-permute-start | bytes 442376 | tf_op jit(solution)/shard_map/ppermute | solution.py:440
  49.7 1.7 %collective-permute-done.7.refs_1_ = bf16[72,1024]{1,0:T(8,128)(2,1)S(1)} collective-permute-done((bf16[72,1024]{1,0:T(8,128)(2,1)S(1)}, bf16[72,1024]{1,0:T(8,128)(2,1)S(1)}, u32[]{:S(2)}, u32[]{:S(2)}) %collective-permute-start.7) | collective-permute-done | bytes 147488 | tf_op jit(solution)/shard_map/ppermute | solution.py:440
  51.4 4.0 %collective-permute-done.8.refs_2_ = bf16[72,1024]{1,0:T(8,128)(2,1)S(1)} collective-permute-done((bf16[72,1024]{1,0:T(8,128)(2,1)S(1)}, bf16[72,1024]{1,0:T(8,128)(2,1)S(1)}, u32[]{:S(2)}, u32[]{:S(2)}) %collective-permute-start.8) | collective-permute-done | bytes 147488 | tf_op jit(solution)/shard_map/ppermute | solution.py:440
  55.4 1.1 %settle.1 = (bf16[64,1024]{1,0:T(8,128)(2,1)S(1)}, bf16[64,1024]{1,0:T(8,128)(2,1)S(1)}) custom-call(s32[2]{0:T(128)S(1)} %pad_add_fusion.mine_ref, s32[1,18]{1,0:T(1,128)S(1)} %bitcast.15, bf16[72,1024]{1,0:T(8,128)(2,1)S(1)} %collective-permute-done.6.refs_0_, bf16[72,1024]{1,0:T(8,128)(2,1)S(1)} %collective-permute-done.7.refs_1_, ...), custom_call_target="tpu_custom_call" | custom-call | tf_op jit(solution)/shard_map/settle/pallas_call | solution.py:372
  56.6 1.3 %collective-permute-done.9.brought_ref = bf16[64,1024]{1,0:T(8,128)(2,1)S(1)} collective-permute-done((bf16[64,1024]{1,0:T(8,128)(2,1)S(1)}, bf16[64,1024]{1,0:T(8,128)(2,1)S(1)}, u32[]{:S(2)}, u32[]{:S(2)}) %collective-permute-start.9) | collective-permute-done | bytes 131104 | tf_op jit(solution)/shard_map/ppermute | solution.py:468
  57.9 1.6 %collective-permute-start.10 = (bf16[32,1024]{1,0:T(8,128)(2,1)S(1)}, bf16[32,1024]{1,0:T(8,128)(2,1)S(1)}, u32[]{:S(2)}, u32[]{:S(2)}) collective-permute-start(bf16[32,1024]{1,0:T(8,128)(2,1)S(1)} %get-tuple-element.82), channel_id=1, source_target_pairs={{0,8},{4,12},{8,0},{12,4},{16,24},{20,28},{24,16},{28,20},{1,9},{5... | collective-permute-start | bytes 196616 | tf_op jit(solution)/shard_map/ppermute | solution.py:468
  59.5 1.5 %collective-permute-start.11 = (bf16[32,1024]{1,0:T(8,128)(2,1)S(1)}, bf16[32,1024]{1,0:T(8,128)(2,1)S(1)}, u32[]{:S(2)}, u32[]{:S(2)}) collective-permute-start(bf16[32,1024]{1,0:T(8,128)(2,1)S(1)} %get-tuple-element.83), channel_id=1, source_target_pairs={{0,16},{4,20},{8,24},{12,28},{16,0},{20,4},{24,8},{28,12},{1,17},{... | collective-permute-start | bytes 196616 | tf_op jit(solution)/shard_map/ppermute | solution.py:468
  61.5 0.8 %collective-permute-done.10.refs_1_ = bf16[32,1024]{1,0:T(8,128)(2,1)S(1)} collective-permute-done((bf16[32,1024]{1,0:T(8,128)(2,1)S(1)}, bf16[32,1024]{1,0:T(8,128)(2,1)S(1)}, u32[]{:S(2)}, u32[]{:S(2)}) %collective-permute-start.10) | collective-permute-done | bytes 65568 | tf_op jit(solution)/shard_map/ppermute | solution.py:468
  62.2 1.5 %collective-permute-done.11.refs_2_ = bf16[32,1024]{1,0:T(8,128)(2,1)S(1)} collective-permute-done((bf16[32,1024]{1,0:T(8,128)(2,1)S(1)}, bf16[32,1024]{1,0:T(8,128)(2,1)S(1)}, u32[]{:S(2)}, u32[]{:S(2)}) %collective-permute-start.11) | collective-permute-done | bytes 65568 | tf_op jit(solution)/shard_map/ppermute | solution.py:468
  63.7 2.4 %collective-permute-done.12.refs_3_ = bf16[32,1024]{1,0:T(8,128)(2,1)S(1)} collective-permute-done((bf16[32,1024]{1,0:T(8,128)(2,1)S(1)}, bf16[32,1024]{1,0:T(8,128)(2,1)S(1)}, u32[]{:S(2)}, u32[]{:S(2)}) %collective-permute-start.12) | collective-permute-done | bytes 65568 | tf_op jit(solution)/shard_map/ppermute | solution.py:468
  66.2 0.8 %widen.1 = f32[24,4,1024]{2,1,0:T(4,128)} custom-call(s32[1]{0:T(128)} %bitcast.mine_ref, bf16[32,1024]{1,0:T(8,128)(2,1)S(1)} %get-tuple-element.81.refs_0_, bf16[32,1024]{1,0:T(8,128)(2,1)S(1)} %collective-permute-done.10.refs_1_, bf16[32,1024]{1,0:T(8,128)(2,1)S(1)} %collective-permute-done.11.refs_2_, bf16[32,1024]{1,0:T(8,128)(2,1)S(1)} %collective-permute-done.12.refs_3_), custom_call_target="tpu_custom_call" | custom-call | tf_op jit(solution)/shard_map/widen/pallas_call | solution.py:416
  (29 shorter events, 4.0 us)
Async XLA Ops:
  0.0 30.6 %copy-start = (f32[2,128]{1,0:T(2,128)S(1)}, f32[2,128]{1,0:T(2,128)}, u32[]{:S(2)}) copy-start(f32[2,128]{1,0:T(2,128)} %constant.38.clone.refs_5_) | copy-start | bytes 3076
  1.8 0.7 %copy-start.1 = (s32[1,1,18,2]{2,3,1,0:T(2,128)S(1)}, s32[1,1,18,2]{2,3,1,0:T(2,128)}, u32[]{:S(2)}) copy-start(s32[1,1,18,2]{2,3,1,0:T(2,128)} %param.8) | copy-start | bytes 436
  3.5 10.5 %collective-permute-start = (bf16[32,4224]{1,0:T(8,128)(2,1)S(1)}, bf16[32,4224]{1,0:T(8,128)(2,1)S(1)}, u32[]{:S(2)}, u32[]{:S(2)}) collective-permute-start(bf16[32,4224]{1,0:T(8,128)(2,1)S(1)} %get-tuple-element.45), channel_id=1, source_target_pairs={{1,2},{2,1},{5,6},{6,5},{9,10},{10,9},{13,14},{14,13},{17,18},{18,... | collective-permute-start | bytes 811016 | tf_op jit(solution)/shard_map/ppermute | solution.py:440
  4.2 14.6 %collective-permute-start.1 = (bf16[32,4224]{1,0:T(8,128)(2,1)S(1)}, bf16[32,4224]{1,0:T(8,128)(2,1)S(1)}, u32[]{:S(2)}, u32[]{:S(2)}) collective-permute-start(bf16[32,4224]{1,0:T(8,128)(2,1)S(1)} %get-tuple-element.46), channel_id=1, source_target_pairs={{0,1},{3,2},{4,5},{7,6},{8,9},{11,10},{12,13},{15,14},{16,17},{19,... | collective-permute-start | bytes 811016 | tf_op jit(solution)/shard_map/ppermute | solution.py:440
  12.0 18.6 %collective-permute-start.5 = (bf16[32,4224]{1,0:T(8,128)(2,1)S(1)}, bf16[32,4224]{1,0:T(8,128)(2,1)S(1)}, u32[]{:S(2)}, u32[]{:S(2)}) collective-permute-start(bf16[32,4224]{1,0:T(8,128)(2,1)S(1)} %get-tuple-element.57), channel_id=1, source_target_pairs={{0,2},{3,1},{4,6},{7,5},{8,10},{11,9},{12,14},{15,13},{16,18},{19,... | collective-permute-start | bytes 811016 | tf_op jit(solution)/shard_map/ppermute | solution.py:440
  18.9 20.1 %collective-permute-start.2 = (bf16[32,4096]{1,0:T(8,128)(2,1)S(1)}, bf16[32,4096]{1,0:T(8,128)(2,1)S(1)}, u32[]{:S(2)}, u32[]{:S(2)}) collective-permute-start(bf16[32,4096]{1,0:T(8,128)(2,1)S(1)} %get-tuple-element.51), channel_id=1, source_target_pairs={{1,2},{2,1},{5,6},{6,5},{9,10},{10,9},{13,14},{14,13},{17,18},{18,... | collective-permute-start | bytes 786440 | tf_op jit(solution)/shard_map/ppermute | solution.py:440
  19.5 19.4 %collective-permute-start.3 = (bf16[32,4096]{1,0:T(8,128)(2,1)S(1)}, bf16[32,4096]{1,0:T(8,128)(2,1)S(1)}, u32[]{:S(2)}, u32[]{:S(2)}) collective-permute-start(bf16[32,4096]{1,0:T(8,128)(2,1)S(1)} %get-tuple-element.52), channel_id=1, source_target_pairs={{0,1},{3,2},{4,5},{7,6},{8,9},{11,10},{12,13},{15,14},{16,17},{19,... | collective-permute-start | bytes 786440 | tf_op jit(solution)/shard_map/ppermute | solution.py:440
  25.6 13.3 %collective-permute-start.4 = (bf16[32,4096]{1,0:T(8,128)(2,1)S(1)}, bf16[32,4096]{1,0:T(8,128)(2,1)S(1)}, u32[]{:S(2)}, u32[]{:S(2)}) collective-permute-start(bf16[32,4096]{1,0:T(8,128)(2,1)S(1)} %get-tuple-element.53), channel_id=1, source_target_pairs={{0,2},{3,1},{4,6},{7,5},{8,10},{11,9},{12,14},{15,13},{16,18},{19,... | collective-permute-start | bytes 786440 | tf_op jit(solution)/shard_map/ppermute | solution.py:440
  39.0 16.4 %copy-start.2 = (s32[1,1,18,1]{2,3,1,0:T(1,128)S(1)}, s32[1,1,18,1]{2,3,1,0:T(1,128)}, u32[]{:S(2)}) copy-start(s32[1,1,18,1]{2,3,1,0:T(1,128)} %param.9) | copy-start | bytes 220
  42.7 7.1 %collective-permute-start.6 = (bf16[72,1024]{1,0:T(8,128)(2,1)S(1)}, bf16[72,1024]{1,0:T(8,128)(2,1)S(1)}, u32[]{:S(2)}, u32[]{:S(2)}) collective-permute-start(bf16[72,1024]{1,0:T(8,128)(2,1)S(1)} %get-tuple-element.72), channel_id=1, source_target_pairs={{1,2},{2,1},{5,6},{6,5},{9,10},{10,9},{13,14},{14,13},{17,18},{18,... | collective-permute-start | bytes 442376 | tf_op jit(solution)/shard_map/ppermute | solution.py:440
  43.4 8.0 %collective-permute-start.7 = (bf16[72,1024]{1,0:T(8,128)(2,1)S(1)}, bf16[72,1024]{1,0:T(8,128)(2,1)S(1)}, u32[]{:S(2)}, u32[]{:S(2)}) collective-permute-start(bf16[72,1024]{1,0:T(8,128)(2,1)S(1)} %get-tuple-element.73), channel_id=1, source_target_pairs={{1,3},{2,0},{5,7},{6,4},{9,11},{10,8},{13,15},{14,12},{17,19},{18,... | collective-permute-start | bytes 442376 | tf_op jit(solution)/shard_map/ppermute | solution.py:440
  48.4 7.1 %collective-permute-start.8 = (bf16[72,1024]{1,0:T(8,128)(2,1)S(1)}, bf16[72,1024]{1,0:T(8,128)(2,1)S(1)}, u32[]{:S(2)}, u32[]{:S(2)}) collective-permute-start(bf16[72,1024]{1,0:T(8,128)(2,1)S(1)} %get-tuple-element.77), channel_id=1, source_target_pairs={{1,0},{2,3},{5,4},{6,7},{9,8},{10,11},{13,12},{14,15},{17,16},{18,... | collective-permute-start | bytes 442376 | tf_op jit(solution)/shard_map/ppermute | solution.py:440
  56.5 1.4 %collective-permute-start.9 = (bf16[64,1024]{1,0:T(8,128)(2,1)S(1)}, bf16[64,1024]{1,0:T(8,128)(2,1)S(1)}, u32[]{:S(2)}, u32[]{:S(2)}) collective-permute-start(bf16[64,1024]{1,0:T(8,128)(2,1)S(1)} %get-tuple-element.80), channel_id=1, source_target_pairs={{0,4},{4,0},{8,12},{12,8},{16,20},{20,16},{24,28},{28,24},{1,5},{5... | collective-permute-start | bytes 393224 | tf_op jit(solution)/shard_map/ppermute | solution.py:468
  57.9 4.3 %collective-permute-start.10 = (bf16[32,1024]{1,0:T(8,128)(2,1)S(1)}, bf16[32,1024]{1,0:T(8,128)(2,1)S(1)}, u32[]{:S(2)}, u32[]{:S(2)}) collective-permute-start(bf16[32,1024]{1,0:T(8,128)(2,1)S(1)} %get-tuple-element.82), channel_id=1, source_target_pairs={{0,8},{4,12},{8,0},{12,4},{16,24},{20,28},{24,16},{28,20},{1,9},{5... | collective-permute-start | bytes 196616 | tf_op jit(solution)/shard_map/ppermute | solution.py:468
  59.5 4.3 %collective-permute-start.11 = (bf16[32,1024]{1,0:T(8,128)(2,1)S(1)}, bf16[32,1024]{1,0:T(8,128)(2,1)S(1)}, u32[]{:S(2)}, u32[]{:S(2)}) collective-permute-start(bf16[32,1024]{1,0:T(8,128)(2,1)S(1)} %get-tuple-element.83), channel_id=1, source_target_pairs={{0,16},{4,20},{8,24},{12,28},{16,0},{20,4},{24,8},{28,12},{1,17},{... | collective-permute-start | bytes 196616 | tf_op jit(solution)/shard_map/ppermute | solution.py:468
  61.0 5.2 %collective-permute-start.12 = (bf16[32,1024]{1,0:T(8,128)(2,1)S(1)}, bf16[32,1024]{1,0:T(8,128)(2,1)S(1)}, u32[]{:S(2)}, u32[]{:S(2)}) collective-permute-start(bf16[32,1024]{1,0:T(8,128)(2,1)S(1)} %get-tuple-element.84), channel_id=1, source_target_pairs={{0,24},{4,28},{8,16},{12,20},{16,8},{20,12},{24,0},{28,4},{1,25},{... | collective-permute-start | bytes 196616 | tf_op jit(solution)/shard_map/ppermute | solution.py:468

commit v7 on v6

--- a/solution.py
+++ b/solution.py
@@ -19,8 +19,7 @@
 VMEM_LIMIT = 24 * 1024 * 1024
 HALF = LAGS // 2
 ROOM = 4
-WAVES = 2
-LATE = 2
+WAVES = (0, 2, 3, 4)
 
 
 def works(place):
@@ -30,7 +29,7 @@
 def whiten_kernel(parts, place_ref, spec_ref, pairs_ref, *out_refs):
     blocks = F // LANES
     each = blocks // (parts // 2)
-    late = each // LATE
+    bounds = [each * quarter // 4 for quarter in WAVES]
     place = place_ref[0]
 
     def values(start):
@@ -46,7 +45,7 @@
     notes = jnp.where(line == 0, wide(pairs_ref[0:1]), wide(pairs_ref[1:2]))
     notes = notes.astype(jnp.float32).astype(jnp.bfloat16)
     for out_ref in out_refs[:parts]:
-        out_ref[:, (each - late) * 2 * LANES :] = notes
+        out_ref[:, bounds[1] * 2 * LANES :] = notes
     sums = [None] * 4
     for k in range(blocks):
         power = values(k * LANES)[2]
@@ -55,8 +54,8 @@
     level = 0.1 * (total * (1.0 / F) + 1e-05)
     for index, out_ref in enumerate(out_refs):
         wave, d = divmod(index, parts)
-        first = lax.shift_right_logical(jnp.bitwise_xor(place, d), 1) * each + wave * (each - late)
-        for k in range(late if wave else each - late):
+        first = lax.shift_right_logical(jnp.bitwise_xor(place, d), 1) * each + bounds[wave]
+        for k in range(bounds[wave + 1] - bounds[wave]):
             re, im, power = values(pl.multiple_of((first + k) * LANES, LANES))
             scale = lax.rsqrt(power + level)
             at = k * 2 * LANES
@@ -68,8 +67,10 @@
     rows = spectra.shape[0] * WINDOWS
     planes = jnp.transpose(spectra.reshape(rows, 2, F), (1, 0, 2))
     width = 2 * F // (parts // 2)
-    late = width // LATE
-    shapes = [(rows, width - late + LANES)] * parts + [(rows, late)] * parts
+    bounds = [width * quarter // 4 for quarter in WAVES]
+    shapes = []
+    for wave in range(len(WAVES) - 1):
+        shapes += [(rows, bounds[wave + 1] - bounds[wave] + (0 if wave else LANES))] * parts
     whole = lambda array: pl.BlockSpec(array.shape, lambda i, place: (0,) * array.ndim)
     outs = pl.pallas_call(
         functools.partial(whiten_kernel, parts),
@@ -83,7 +84,7 @@
         compiler_params=pltpu.CompilerParams(vmem_limit_bytes=VMEM_LIMIT),
         name="whiten",
     )(place[None], planes, pairs)
-    return list(outs[:parts]), list(outs[parts:])
+    return [list(outs[i : i + parts]) for i in range(0, len(outs), parts)]
 
 
 def table_kernel(first_ref, hi_cos_ref, hi_sin_ref, mid_cos_ref, mid_sin_ref, lo_cos_ref, lo_sin_ref, out_ref, cos, sin):
@@ -189,6 +190,7 @@
 
 
 def corr_kernel(per_step, parts, lists, wave, place, *refs):
+    last = wave == len(WAVES) - 2
     panel_refs, (table_ref, ends_ref), refs = dict(zip(sequence(parts), refs)), refs[parts : parts + 2], refs[parts + 2 :]
     step = pl.program_id(0)
     if wave:
@@ -256,7 +258,7 @@
         total[:, HALF:] += odd
         edge[...] += edge_part
 
-    if wave < WAVES - 1:
+    if not last:
         return
 
     @pl.when(step == pl.num_programs(0) - 1)
@@ -283,12 +285,11 @@
 
 def correlate(panels, table, place, parts, wanted, wave, before):
     chunks = table.shape[0] // LANES
-    per_step = min(4, chunks // LATE)
+    per_step = min(4, chunks // 4)
     span = per_step * 2 * LANES
     rows = panels[0].shape[0]
-    late = chunks // LATE // per_step
-    early = chunks // per_step - late
-    steps = late if wave else early
+    base = chunks * WAVES[wave] // 4 // per_step
+    steps = chunks * WAVES[wave + 1] // 4 // per_step - base
     lists = len(wanted)
     count = -(-lists * NB_SRC // 8) * 8
     each = NB_SRC * PAIRS
@@ -303,8 +304,9 @@
     if wave:
         extra = before
         extra_specs = [whole(array) for array in before]
-        outs = [jax.ShapeDtypeStruct((each, LAGS), jnp.bfloat16)] * lists
-        scratch = [pltpu.VMEM(array.shape, array.dtype) for array in sums]
+        last = wave == len(WAVES) - 2
+        outs = [jax.ShapeDtypeStruct((each, LAGS), jnp.bfloat16)] * lists if last else sums
+        scratch = [pltpu.VMEM(array.shape, array.dtype) for array in sums] if last else []
     else:
         extra = [panels[d] for d in wanted]
         extra_specs = [pl.BlockSpec((rows, LANES), lambda i, place: (0, steps * span // LANES))] * lists
@@ -317,7 +319,7 @@
             grid=(steps,),
             in_specs=[
                 *[pl.BlockSpec((rows, span), lambda i, place: (0, i))] * parts,
-                pl.BlockSpec((span // 2, LAGS), lambda i, place: (i + wave * early, 0)),
+                pl.BlockSpec((span // 2, LAGS), lambda i, place: (i + base, 0)),
                 pl.BlockSpec((2, LANES), lambda i, place: (0, 0)),
                 *extra_specs,
             ],
@@ -443,24 +445,31 @@
         moved = {d: swap(panels[d], d, False) for d in sequence(parts)[:-1]}
         return panels[:1] + [moved[d] for d in range(1, parts)]
 
-    first, second = whiten(spectra, pair_blocks[0, 0].T, place, parts)
+    def hold(panels, other):
+        ordered, other = lax.optimization_barrier(([panels[d] for d in sequence(parts)], other))
+        held = dict(zip(sequence(parts), ordered))
+        return [held[d] for d in range(parts)], other
+
+    first, second, third = whiten(spectra, pair_blocks[0, 0].T, place, parts)
     first = exchange(first)
     table = tables(rank, chunks)
-    gates = [d for d in sequence(parts)[:2] if d]
-    here, second = lax.optimization_barrier(([first[d] for d in gates], second))
-    for d, panel in zip(gates, here):
-        first[d] = panel
+    second, table = hold(second, table)
     second = exchange(second)
-
     order = list(reversed(range(parts)))
     halves = (order[: parts // 2], order[parts // 2 :])
-    sums = [correlate(first, table, place, parts, wanted, 0, None) for wanted in halves]
-    ordered, sums = lax.optimization_barrier(([second[d] for d in sequence(parts)], sums))
-    for d, panel in zip(sequence(parts), ordered):
-        second[d] = panel
+    sums = [correlate(first, table, place, parts, halves[0], 0, None)]
+    third, sums = hold(third, sums)
+    third = exchange(third)
+    sums.append(correlate(first, table, place, parts, halves[1], 0, None))
+    second, sums = hold(second, sums)
+    sums = [
+        [*correlate(second, table, place, parts, wanted, 1, before), before[2]]
+        for wanted, before in zip(halves, sums)
+    ]
+    third, sums = hold(third, sums)
     partials = []
     for wanted, before in zip(halves, sums):
-        for d, rows in zip(wanted, correlate(second, table, place, parts, wanted, 1, before)):
+        for d, rows in zip(wanted, correlate(third, table, place, parts, wanted, 2, before)):
             partials.append(swap(rows, d, True) if d else rows)
     mine = lax.axis_index("grp")
 

time: 67.2 us -> 71.5 us (1.064)
  starting transfers between devices: 25.7 us -> 31.6 us
  waiting for transfers between devices: 16.6 us -> 14.7 us
    ppermute x9 -> x12, starting transfers between devices: 22 us -> 28 us  [swap(): return lax.ppermute(array, 'chan', pairs)]
    ppermute x9 -> x12, waiting for transfers between devices: 10.5 us -> 8.7 us  [swap(): return lax.ppermute(array, 'chan', pairs)]
    pallas_call x4 -> x6, Pallas kernels: 15.7 us -> 15.8 us  [correlate(): pl.pallas_call(functools.partial(corr_kernel, per_step, parts, lists, wav...]
  transfers between devices with their start and end apart: 13 -> 16, of which waited for: 7 -> 7; matrix products, arithmetic and copies ran while one was open for 1% -> 1% of each run, Pallas kernels for 22% -> 23%
where the time goes in v7:
time: 71.5 us; the launch traced here: 71.1 us
  starting transfers between devices  31.6 us (44%)
  Pallas kernels  21.2 us (30%)
  waiting for transfers between devices  14.7 us (21%)
  local copies, waits for them, and re-layouts  2.52 us (4%)
    ppermute x12, starting transfers between devices, swap(): return lax.ppermute(array, 'chan', pairs)  28 us
    pallas_call x6, Pallas kernels, correlate(): pl.pallas_call(functools.partial(corr_kernel, per_step, parts, lists, wav...  15.8 us
    ppermute x12, waiting for transfers between devices, swap(): return lax.ppermute(array, 'chan', pairs)  8.7 us
    ppermute x4, waiting for transfers between devices, trade(): return lax.ppermute(array, 'grp', [(i, i ^ m) for i in range(groups)])  6.02 us
    ppermute x4, starting transfers between devices, trade(): return lax.ppermute(array, 'grp', [(i, i ^ m) for i in range(groups)])  3.62 us
    pallas_call x1, Pallas kernels, tables(): pl.pallas_call(table_kernel, grid_spec=pltpu.PrefetchScalarGridSpec(num_s...  2.58 us
    reshape x1, local copies, waits for them, and re-layouts, whiten(): planes = jnp.transpose(spectra.reshape(rows, 2, F), (1, 0, 2))  1.82 us
  transfers between devices with their start and end apart: 16, of which 7 were waited for; matrix products, arithmetic and copies ran while one was open for 1% of the time, Pallas kernels for 23%

profile of v7, /device:TPU:0, one launch (start us, length us, event | category | flops | bytes accessed | tf_op | source)
XLA Modules:
  0.0 71.1 jit_solution(15215113666495898319)
XLA Ops:
  0.0 1.8 %copy.13 = bf16[32,2,8192]{2,0,1:T(8,128)(2,1)S(1)} copy(bf16[32,2,8192]{2,1,0:T(2,128)(2,1)} %bitcast.16) | data formatting | bytes 2097152 | tf_op jit(solution)/shard_map/reshape | solution.py:68
  4.2 7.8 %collective-permute-start.1 = (bf16[32,4224]{1,0:T(8,128)(2,1)S(1)}, bf16[32,4224]{1,0:T(8,128)(2,1)S(1)}, u32[]{:S(2)}, u32[]{:S(2)}) collective-permute-start(bf16[32,4224]{1,0:T(8,128)(2,1)S(1)} %get-tuple-element.74), channel_id=1, source_target_pairs={{0,1},{3,2},{4,5},{7,6},{8,9},{11,10},{12,13},{15,14},{16,17},{19,... | collective-permute-start | bytes 811016 | tf_op jit(solution)/shard_map/ppermute | solution.py:442
  12.0 1.3 %collective-permute-start.2 = (bf16[32,4224]{1,0:T(8,128)(2,1)S(1)}, bf16[32,4224]{1,0:T(8,128)(2,1)S(1)}, u32[]{:S(2)}, u32[]{:S(2)}) collective-permute-start(bf16[32,4224]{1,0:T(8,128)(2,1)S(1)} %get-tuple-element.75), channel_id=1, source_target_pairs={{0,2},{3,1},{4,6},{7,5},{8,10},{11,9},{12,14},{15,13},{16,18},{19,... | collective-permute-start | bytes 811016 | tf_op jit(solution)/shard_map/ppermute | solution.py:442
  14.0 2.6 %tables.1.refs_4_ = bf16[4096,1024]{1,0:T(8,128)(2,1)S(1)} custom-call(s32[1]{0:T(128)} %bitcast.8.first_ref, f32[32,512]{1,0:T(8,128)S(1)} %get-tuple-element.136.hi_cos_ref, f32[32,512]{1,0:T(8,128)S(1)} %get-tuple-element.135.hi_sin_ref, f32[16,512]{1,0:T(8,128)S(1)} %slice.26.mid_cos_ref, f32[16,512]{1,0:T(8,128)S(1)} %slice.27.mid_sin_ref, ...), custom_call_target="tpu_custom_call" | custom-call | flops 16777216 | bytes 8388608 | tf_op jit(solution)/shard_map/tables/pallas_call | solution.py:136
  17.3 3.0 %collective-permute-start.7 = (bf16[32,2048]{1,0:T(8,128)(2,1)S(1)}, bf16[32,2048]{1,0:T(8,128)(2,1)S(1)}, u32[]{:S(2)}, u32[]{:S(2)}) collective-permute-start(bf16[32,2048]{1,0:T(8,128)(2,1)S(1)} %get-tuple-element.90), channel_id=1, source_target_pairs={{0,1},{3,2},{4,5},{7,6},{8,9},{11,10},{12,13},{15,14},{16,17},{19,... | collective-permute-start | bytes 393224 | tf_op jit(solution)/shard_map/ppermute | solution.py:442
  20.2 2.3 %collective-permute-start.8 = (bf16[32,2048]{1,0:T(8,128)(2,1)S(1)}, bf16[32,2048]{1,0:T(8,128)(2,1)S(1)}, u32[]{:S(2)}, u32[]{:S(2)}) collective-permute-start(bf16[32,2048]{1,0:T(8,128)(2,1)S(1)} %get-tuple-element.91), channel_id=1, source_target_pairs={{0,2},{3,1},{4,6},{7,5},{8,10},{11,9},{12,14},{15,13},{16,18},{19,... | collective-permute-start | bytes 393224 | tf_op jit(solution)/shard_map/ppermute | solution.py:442
  22.6 2.1 %collective-permute-done.2.refs_2_.refs_7_ = bf16[32,4224]{1,0:T(8,128)(2,1)S(1)} collective-permute-done((bf16[32,4224]{1,0:T(8,128)(2,1)S(1)}, bf16[32,4224]{1,0:T(8,128)(2,1)S(1)}, u32[]{:S(2)}, u32[]{:S(2)}) %collective-permute-start.2) | collective-permute-done | bytes 270368 | tf_op jit(solution)/shard_map/ppermute | solution.py:442
  24.7 4.1 %correlate.6 = (f32[160,1024]{1,0:T(8,128)S(1)}, f32[160,128]{1,0:T(8,128)S(1)}, bf16[320,128]{1,0:T(8,128)(2,1)S(1)}) custom-call(s32[1]{0:T(128)} %bitcast.3.place_ref.place, bf16[32,4224]{1,0:T(8,128)(2,1)S(1)} %collective-permute-done.refs_0_.refs_6_, bf16[32,4224]{1,0:T(8,128)(2,1)S(1)} %collective-permute-done.1.refs_1_.refs_6_, ...), custom_call_target="tpu_custom_call" | custom-call | flops 671088640 | bytes 4194304 | tf_op jit(solution)/shard_map/correlate/pallas_call | solution.py:315
  29.5 7.1 %collective-permute-start.4 = (bf16[32,2048]{1,0:T(8,128)(2,1)S(1)}, bf16[32,2048]{1,0:T(8,128)(2,1)S(1)}, u32[]{:S(2)}, u32[]{:S(2)}) collective-permute-start(bf16[32,2048]{1,0:T(8,128)(2,1)S(1)} %get-tuple-element.86), channel_id=1, source_target_pairs={{0,1},{3,2},{4,5},{7,6},{8,9},{11,10},{12,13},{15,14},{16,17},{19,... | collective-permute-start | bytes 393224 | tf_op jit(solution)/shard_map/ppermute | solution.py:442
  36.6 1.3 %collective-permute-start.5 = (bf16[32,2048]{1,0:T(8,128)(2,1)S(1)}, bf16[32,2048]{1,0:T(8,128)(2,1)S(1)}, u32[]{:S(2)}, u32[]{:S(2)}) collective-permute-start(bf16[32,2048]{1,0:T(8,128)(2,1)S(1)} %get-tuple-element.87), channel_id=1, source_target_pairs={{0,2},{3,1},{4,6},{7,5},{8,10},{11,9},{12,14},{15,13},{16,18},{19,... | collective-permute-start | bytes 393224 | tf_op jit(solution)/shard_map/ppermute | solution.py:442
  37.9 4.2 %correlate.7 = (f32[160,1024]{1,0:T(8,128)S(1)}, f32[160,128]{1,0:T(8,128)S(1)}, bf16[320,128]{1,0:T(8,128)(2,1)S(1)}) custom-call(s32[1]{0:T(128)} %bitcast.3.place_ref.place, bf16[32,4224]{1,0:T(8,128)(2,1)S(1)} %collective-permute-done.refs_0_.refs_6_, bf16[32,4224]{1,0:T(8,128)(2,1)S(1)} %collective-permute-done.1.refs_1_.refs_6_, ...), custom_call_target="tpu_custom_call" | custom-call | flops 671088640 | bytes 4194304 | tf_op jit(solution)/shard_map/correlate/pallas_call | solution.py:315
  42.1 1.7 %correlate.8 = (f32[160,1024]{1,0:T(8,128)S(1)}, f32[160,128]{1,0:T(8,128)S(1)}) custom-call(s32[1]{0:T(128)} %bitcast.3.place_ref.place, bf16[32,2048]{1,0:T(8,128)(2,1)S(1)} %collective-permute-done.6.refs_0_, bf16[32,2048]{1,0:T(8,128)(2,1)S(1)} %collective-permute-done.7.refs_1_, bf16[32,2048]{1,0:T(8,128)(2,1)S(1)} %collective-permute-done.8.refs_2_, ...), custom_call_target="tpu_custom_call" | custom-call | flops 335544320 | bytes 2097152 | tf_op jit(solution)/shard_map/correlate/pallas_call | solution.py:315
  43.8 1.7 %correlate.9 = (f32[160,1024]{1,0:T(8,128)S(1)}, f32[160,128]{1,0:T(8,128)S(1)}) custom-call(s32[1]{0:T(128)} %bitcast.3.place_ref.place, bf16[32,2048]{1,0:T(8,128)(2,1)S(1)} %collective-permute-done.6.refs_0_, bf16[32,2048]{1,0:T(8,128)(2,1)S(1)} %collective-permute-done.7.refs_1_, bf16[32,2048]{1,0:T(8,128)(2,1)S(1)} %collective-permute-done.8.refs_2_, ...), custom_call_target="tpu_custom_call" | custom-call | flops 335544320 | bytes 2097152 | tf_op jit(solution)/shard_map/correlate/pallas_call | solution.py:315
  45.5 2.1 %correlate.10 = (bf16[72,1024]{1,0:T(8,128)(2,1)S(1)}, bf16[72,1024]{1,0:T(8,128)(2,1)S(1)}) custom-call(s32[1]{0:T(128)} %bitcast.3.place_ref.place, bf16[32,2048]{1,0:T(8,128)(2,1)S(1)} %collective-permute-done.3.refs_0_, bf16[32,2048]{1,0:T(8,128)(2,1)S(1)} %collective-permute-done.4.refs_1_, bf16[32,2048]{1,0:T(8,128)(2,1)S(1)} %collective-permute-done.5.refs_2_, ...), custom_call_target="tpu_custom_call" | custom-call | flops 335544320 | bytes 2097152 | tf_op jit(solution)/shard_map/correlate/pallas_call | solution.py:315
  48.3 1.3 %collective-permute-start.10 = (bf16[72,1024]{1,0:T(8,128)(2,1)S(1)}, bf16[72,1024]{1,0:T(8,128)(2,1)S(1)}, u32[]{:S(2)}, u32[]{:S(2)}) collective-permute-start(bf16[72,1024]{1,0:T(8,128)(2,1)S(1)} %get-tuple-element.121), channel_id=1, source_target_pairs={{1,3},{2,0},{5,7},{6,4},{9,11},{10,8},{13,15},{14,12},{17,19},{18,... | collective-permute-start | bytes 442376 | tf_op jit(solution)/shard_map/ppermute | solution.py:442
  49.6 2.1 %correlate.11 = (bf16[72,1024]{1,0:T(8,128)(2,1)S(1)}, bf16[72,1024]{1,0:T(8,128)(2,1)S(1)}) custom-call(s32[1]{0:T(128)} %bitcast.3.place_ref.place, bf16[32,2048]{1,0:T(8,128)(2,1)S(1)} %collective-permute-done.3.refs_0_, bf16[32,2048]{1,0:T(8,128)(2,1)S(1)} %collective-permute-done.4.refs_1_, bf16[32,2048]{1,0:T(8,128)(2,1)S(1)} %collective-permute-done.5.refs_2_, ...), custom_call_target="tpu_custom_call" | custom-call | flops 335544320 | bytes 2097152 | tf_op jit(solution)/shard_map/correlate/pallas_call | solution.py:315
  51.7 1.3 %collective-permute-start.11 = (bf16[72,1024]{1,0:T(8,128)(2,1)S(1)}, bf16[72,1024]{1,0:T(8,128)(2,1)S(1)}, u32[]{:S(2)}, u32[]{:S(2)}) collective-permute-start(bf16[72,1024]{1,0:T(8,128)(2,1)S(1)} %get-tuple-element.125), channel_id=1, source_target_pairs={{1,0},{2,3},{5,4},{6,7},{9,8},{10,11},{13,12},{14,15},{17,16},{18,... | collective-permute-start | bytes 442376 | tf_op jit(solution)/shard_map/ppermute | solution.py:442
  53.1 3.3 %collective-permute-done.10.refs_1_ = bf16[72,1024]{1,0:T(8,128)(2,1)S(1)} collective-permute-done((bf16[72,1024]{1,0:T(8,128)(2,1)S(1)}, bf16[72,1024]{1,0:T(8,128)(2,1)S(1)}, u32[]{:S(2)}, u32[]{:S(2)}) %collective-permute-start.10) | collective-permute-done | bytes 147488 | tf_op jit(solution)/shard_map/ppermute | solution.py:442
  56.3 3.3 %collective-permute-done.11.refs_2_ = bf16[72,1024]{1,0:T(8,128)(2,1)S(1)} collective-permute-done((bf16[72,1024]{1,0:T(8,128)(2,1)S(1)}, bf16[72,1024]{1,0:T(8,128)(2,1)S(1)}, u32[]{:S(2)}, u32[]{:S(2)}) %collective-permute-start.11) | collective-permute-done | bytes 147488 | tf_op jit(solution)/shard_map/ppermute | solution.py:442
  60.8 1.3 %collective-permute-done.12.brought_ref = bf16[64,1024]{1,0:T(8,128)(2,1)S(1)} collective-permute-done((bf16[64,1024]{1,0:T(8,128)(2,1)S(1)}, bf16[64,1024]{1,0:T(8,128)(2,1)S(1)}, u32[]{:S(2)}, u32[]{:S(2)}) %collective-permute-start.12) | collective-permute-done | bytes 131104 | tf_op jit(solution)/shard_map/ppermute | solution.py:477
  62.1 1.6 %collective-permute-start.13 = (bf16[32,1024]{1,0:T(8,128)(2,1)S(1)}, bf16[32,1024]{1,0:T(8,128)(2,1)S(1)}, u32[]{:S(2)}, u32[]{:S(2)}) collective-permute-start(bf16[32,1024]{1,0:T(8,128)(2,1)S(1)} %get-tuple-element.130), channel_id=1, source_target_pairs={{0,8},{4,12},{8,0},{12,4},{16,24},{20,28},{24,16},{28,20},{1,9},{5... | collective-permute-start | bytes 196616 | tf_op jit(solution)/shard_map/ppermute | solution.py:477
  63.7 1.5 %collective-permute-start.14 = (bf16[32,1024]{1,0:T(8,128)(2,1)S(1)}, bf16[32,1024]{1,0:T(8,128)(2,1)S(1)}, u32[]{:S(2)}, u32[]{:S(2)}) collective-permute-start(bf16[32,1024]{1,0:T(8,128)(2,1)S(1)} %get-tuple-element.131), channel_id=1, source_target_pairs={{0,16},{4,20},{8,24},{12,28},{16,0},{20,4},{24,8},{28,12},{1,17},{... | collective-permute-start | bytes 196616 | tf_op jit(solution)/shard_map/ppermute | solution.py:477
  66.5 1.5 %collective-permute-done.14.refs_2_ = bf16[32,1024]{1,0:T(8,128)(2,1)S(1)} collective-permute-done((bf16[32,1024]{1,0:T(8,128)(2,1)S(1)}, bf16[32,1024]{1,0:T(8,128)(2,1)S(1)}, u32[]{:S(2)}, u32[]{:S(2)}) %collective-permute-start.14) | collective-permute-done | bytes 65568 | tf_op jit(solution)/shard_map/ppermute | solution.py:477
  68.0 2.4 %collective-permute-done.15.refs_3_ = bf16[32,1024]{1,0:T(8,128)(2,1)S(1)} collective-permute-done((bf16[32,1024]{1,0:T(8,128)(2,1)S(1)}, bf16[32,1024]{1,0:T(8,128)(2,1)S(1)}, u32[]{:S(2)}, u32[]{:S(2)}) %collective-permute-start.15) | collective-permute-done | bytes 65568 | tf_op jit(solution)/shard_map/ppermute | solution.py:477
  (37 shorter events, 8.3 us)
Async XLA Ops:
  0.0 24.7 %copy-start = (f32[2,128]{1,0:T(2,128)S(1)}, f32[2,128]{1,0:T(2,128)}, u32[]{:S(2)}) copy-start(f32[2,128]{1,0:T(2,128)} %constant.38.clone.refs_5_) | copy-start | bytes 3076
  1.8 0.7 copy-start.1
  3.5 16.7 %collective-permute-start = (bf16[32,4224]{1,0:T(8,128)(2,1)S(1)}, bf16[32,4224]{1,0:T(8,128)(2,1)S(1)}, u32[]{:S(2)}, u32[]{:S(2)}) collective-permute-start(bf16[32,4224]{1,0:T(8,128)(2,1)S(1)} %get-tuple-element.73), channel_id=1, source_target_pairs={{1,2},{2,1},{5,6},{6,5},{9,10},{10,9},{13,14},{14,13},{17,18},{18,... | collective-permute-start | bytes 811016 | tf_op jit(solution)/shard_map/ppermute | solution.py:442
  4.2 18.3 %collective-permute-start.1 = (bf16[32,4224]{1,0:T(8,128)(2,1)S(1)}, bf16[32,4224]{1,0:T(8,128)(2,1)S(1)}, u32[]{:S(2)}, u32[]{:S(2)}) collective-permute-start(bf16[32,4224]{1,0:T(8,128)(2,1)S(1)} %get-tuple-element.74), channel_id=1, source_target_pairs={{0,1},{3,2},{4,5},{7,6},{8,9},{11,10},{12,13},{15,14},{16,17},{19,... | collective-permute-start | bytes 811016 | tf_op jit(solution)/shard_map/ppermute | solution.py:442
  12.0 12.7 %collective-permute-start.2 = (bf16[32,4224]{1,0:T(8,128)(2,1)S(1)}, bf16[32,4224]{1,0:T(8,128)(2,1)S(1)}, u32[]{:S(2)}, u32[]{:S(2)}) collective-permute-start(bf16[32,4224]{1,0:T(8,128)(2,1)S(1)} %get-tuple-element.75), channel_id=1, source_target_pairs={{0,2},{3,1},{4,6},{7,5},{8,10},{11,9},{12,14},{15,13},{16,18},{19,... | collective-permute-start | bytes 811016 | tf_op jit(solution)/shard_map/ppermute | solution.py:442
  16.6 20.0 %collective-permute-start.6 = (bf16[32,2048]{1,0:T(8,128)(2,1)S(1)}, bf16[32,2048]{1,0:T(8,128)(2,1)S(1)}, u32[]{:S(2)}, u32[]{:S(2)}) collective-permute-start(bf16[32,2048]{1,0:T(8,128)(2,1)S(1)} %get-tuple-element.89), channel_id=1, source_target_pairs={{1,2},{2,1},{5,6},{6,5},{9,10},{10,9},{13,14},{14,13},{17,18},{18,... | collective-permute-start | bytes 393224 | tf_op jit(solution)/shard_map/ppermute | solution.py:442
  17.3 24.8 %collective-permute-start.7 = (bf16[32,2048]{1,0:T(8,128)(2,1)S(1)}, bf16[32,2048]{1,0:T(8,128)(2,1)S(1)}, u32[]{:S(2)}, u32[]{:S(2)}) collective-permute-start(bf16[32,2048]{1,0:T(8,128)(2,1)S(1)} %get-tuple-element.90), channel_id=1, source_target_pairs={{0,1},{3,2},{4,5},{7,6},{8,9},{11,10},{12,13},{15,14},{16,17},{19,... | collective-permute-start | bytes 393224 | tf_op jit(solution)/shard_map/ppermute | solution.py:442
  20.2 21.9 %collective-permute-start.8 = (bf16[32,2048]{1,0:T(8,128)(2,1)S(1)}, bf16[32,2048]{1,0:T(8,128)(2,1)S(1)}, u32[]{:S(2)}, u32[]{:S(2)}) collective-permute-start(bf16[32,2048]{1,0:T(8,128)(2,1)S(1)} %get-tuple-element.91), channel_id=1, source_target_pairs={{0,2},{3,1},{4,6},{7,5},{8,10},{11,9},{12,14},{15,13},{16,18},{19,... | collective-permute-start | bytes 393224 | tf_op jit(solution)/shard_map/ppermute | solution.py:442
  28.8 16.7 %collective-permute-start.3 = (bf16[32,2048]{1,0:T(8,128)(2,1)S(1)}, bf16[32,2048]{1,0:T(8,128)(2,1)S(1)}, u32[]{:S(2)}, u32[]{:S(2)}) collective-permute-start(bf16[32,2048]{1,0:T(8,128)(2,1)S(1)} %get-tuple-element.85), channel_id=1, source_target_pairs={{1,2},{2,1},{5,6},{6,5},{9,10},{10,9},{13,14},{14,13},{17,18},{18,... | collective-permute-start | bytes 393224 | tf_op jit(solution)/shard_map/ppermute | solution.py:442
  29.5 16.0 %collective-permute-start.4 = (bf16[32,2048]{1,0:T(8,128)(2,1)S(1)}, bf16[32,2048]{1,0:T(8,128)(2,1)S(1)}, u32[]{:S(2)}, u32[]{:S(2)}) collective-permute-start(bf16[32,2048]{1,0:T(8,128)(2,1)S(1)} %get-tuple-element.86), channel_id=1, source_target_pairs={{0,1},{3,2},{4,5},{7,6},{8,9},{11,10},{12,13},{15,14},{16,17},{19,... | collective-permute-start | bytes 393224 | tf_op jit(solution)/shard_map/ppermute | solution.py:442
  36.6 8.9 %collective-permute-start.5 = (bf16[32,2048]{1,0:T(8,128)(2,1)S(1)}, bf16[32,2048]{1,0:T(8,128)(2,1)S(1)}, u32[]{:S(2)}, u32[]{:S(2)}) collective-permute-start(bf16[32,2048]{1,0:T(8,128)(2,1)S(1)} %get-tuple-element.87), channel_id=1, source_target_pairs={{0,2},{3,1},{4,6},{7,5},{8,10},{11,9},{12,14},{15,13},{16,18},{19,... | collective-permute-start | bytes 393224 | tf_op jit(solution)/shard_map/ppermute | solution.py:442
  45.5 14.1 %copy-start.2 = (s32[1,1,18,1]{2,3,1,0:T(1,128)S(1)}, s32[1,1,18,1]{2,3,1,0:T(1,128)}, u32[]{:S(2)}) copy-start(s32[1,1,18,1]{2,3,1,0:T(1,128)} %param.11) | copy-start | bytes 220
  47.6 5.5 %collective-permute-start.9 = (bf16[72,1024]{1,0:T(8,128)(2,1)S(1)}, bf16[72,1024]{1,0:T(8,128)(2,1)S(1)}, u32[]{:S(2)}, u32[]{:S(2)}) collective-permute-start(bf16[72,1024]{1,0:T(8,128)(2,1)S(1)} %get-tuple-element.120), channel_id=1, source_target_pairs={{1,2},{2,1},{5,6},{6,5},{9,10},{10,9},{13,14},{14,13},{17,18},{18,... | collective-permute-start | bytes 442376 | tf_op jit(solution)/shard_map/ppermute | solution.py:442
  48.3 8.0 %collective-permute-start.10 = (bf16[72,1024]{1,0:T(8,128)(2,1)S(1)}, bf16[72,1024]{1,0:T(8,128)(2,1)S(1)}, u32[]{:S(2)}, u32[]{:S(2)}) collective-permute-start(bf16[72,1024]{1,0:T(8,128)(2,1)S(1)} %get-tuple-element.121), channel_id=1, source_target_pairs={{1,3},{2,0},{5,7},{6,4},{9,11},{10,8},{13,15},{14,12},{17,19},{18,... | collective-permute-start | bytes 442376 | tf_op jit(solution)/shard_map/ppermute | solution.py:442
  51.7 7.9 %collective-permute-start.11 = (bf16[72,1024]{1,0:T(8,128)(2,1)S(1)}, bf16[72,1024]{1,0:T(8,128)(2,1)S(1)}, u32[]{:S(2)}, u32[]{:S(2)}) collective-permute-start(bf16[72,1024]{1,0:T(8,128)(2,1)S(1)} %get-tuple-element.125), channel_id=1, source_target_pairs={{1,0},{2,3},{5,4},{6,7},{9,8},{10,11},{13,12},{14,15},{17,16},{18,... | collective-permute-start | bytes 442376 | tf_op jit(solution)/shard_map/ppermute | solution.py:442
  60.7 1.4 %collective-permute-start.12 = (bf16[64,1024]{1,0:T(8,128)(2,1)S(1)}, bf16[64,1024]{1,0:T(8,128)(2,1)S(1)}, u32[]{:S(2)}, u32[]{:S(2)}) collective-permute-start(bf16[64,1024]{1,0:T(8,128)(2,1)S(1)} %get-tuple-element.128), channel_id=1, source_target_pairs={{0,4},{4,0},{8,12},{12,8},{16,20},{20,16},{24,28},{28,24},{1,5},{5... | collective-permute-start | bytes 393224 | tf_op jit(solution)/shard_map/ppermute | solution.py:477
  62.1 4.3 %collective-permute-start.13 = (bf16[32,1024]{1,0:T(8,128)(2,1)S(1)}, bf16[32,1024]{1,0:T(8,128)(2,1)S(1)}, u32[]{:S(2)}, u32[]{:S(2)}) collective-permute-start(bf16[32,1024]{1,0:T(8,128)(2,1)S(1)} %get-tuple-element.130), channel_id=1, source_target_pairs={{0,8},{4,12},{8,0},{12,4},{16,24},{20,28},{24,16},{28,20},{1,9},{5... | collective-permute-start | bytes 196616 | tf_op jit(solution)/shard_map/ppermute | solution.py:477
  63.7 4.3 %collective-permute-start.14 = (bf16[32,1024]{1,0:T(8,128)(2,1)S(1)}, bf16[32,1024]{1,0:T(8,128)(2,1)S(1)}, u32[]{:S(2)}, u32[]{:S(2)}) collective-permute-start(bf16[32,1024]{1,0:T(8,128)(2,1)S(1)} %get-tuple-element.131), channel_id=1, source_target_pairs={{0,16},{4,20},{8,24},{12,28},{16,0},{20,4},{24,8},{28,12},{1,17},{... | collective-permute-start | bytes 196616 | tf_op jit(solution)/shard_map/ppermute | solution.py:477
  65.2 5.2 %collective-permute-start.15 = (bf16[32,1024]{1,0:T(8,128)(2,1)S(1)}, bf16[32,1024]{1,0:T(8,128)(2,1)S(1)}, u32[]{:S(2)}, u32[]{:S(2)}) collective-permute-start(bf16[32,1024]{1,0:T(8,128)(2,1)S(1)} %get-tuple-element.132), channel_id=1, source_target_pairs={{0,24},{4,28},{8,16},{12,20},{16,8},{20,12},{24,0},{28,4},{1,25},{... | collective-permute-start | bytes 196616 | tf_op jit(solution)/shard_map/ppermute | solution.py:477

commit v8 on v5

--- a/solution.py
+++ b/solution.py
@@ -444,7 +444,7 @@
     second = exchange(second)
 
     order = list(reversed(range(parts)))
-    halves = (order[: parts // 2], order[parts // 2 :])
+    halves = (order[:1], order[1:])
     sums = [correlate(first, table, place, parts, wanted, 0, None) for wanted in halves]
     ordered, sums = lax.optimization_barrier(([second[d] for d in sequence(parts)], sums))
     for d, panel in zip(sequence(parts), ordered):

time: 58.3 us -> 57.8 us (level)
  waiting for transfers between devices: 24.9 us -> 23.7 us
    ppermute x9, waiting for transfers between devices: 18.9 us -> 17.6 us  [swap(): return lax.ppermute(array, 'chan', [(i, i ^ d) for i in range(parts)])]
  transfers between devices with their start and end apart: 13 -> 13, of which waited for: 10 -> 9; matrix products, arithmetic and copies ran while one was open for 1% -> 1% of each run, Pallas kernels for 13% -> 13%
where the time goes in v8:
time: 57.8 us; the launch traced here: 57.1 us
  waiting for transfers between devices  23.7 us (41%)
  starting transfers between devices  18.3 us (32%)
  Pallas kernels  12 us (21%)
  local copies, waits for them, and re-layouts  2.51 us (4%)
    ppermute x9, waiting for transfers between devices, swap(): return lax.ppermute(array, 'chan', [(i, i ^ d) for i in range(parts)])  17.6 us
    ppermute x9, starting transfers between devices, swap(): return lax.ppermute(array, 'chan', [(i, i ^ d) for i in range(parts)])  14.7 us
    pallas_call x4, Pallas kernels, correlate(): pl.pallas_call(functools.partial(corr_kernel, per_step, parts, lists, wav...  8.76 us
    ppermute x4, waiting for transfers between devices, trade(): return lax.ppermute(array, 'grp', [(i, i ^ m) for i in range(groups)])  6.03 us
    ppermute x4, starting transfers between devices, trade(): return lax.ppermute(array, 'grp', [(i, i ^ m) for i in range(groups)])  3.62 us
    reshape x1, local copies, waits for them, and re-layouts, whiten(): planes = jnp.transpose(spectra.reshape(rows, 2, F), (1, 0, 2))  1.82 us
    pallas_call x1, Pallas kernels, tables(): pl.pallas_call(table_kernel, grid_spec=pltpu.PrefetchScalarGridSpec(num_s...  1.33 us
  transfers between devices with their start and end apart: 13, of which 9 were waited for; matrix products, arithmetic and copies ran while one was open for 1% of the time, Pallas kernels for 13%

profile of v8, /device:TPU:0, one launch (start us, length us, event | category | flops | bytes accessed | tf_op | source)
XLA Modules:
  0.0 57.1 jit_solution(9493249573853131097)
XLA Ops:
  0.0 1.8 %copy.11 = bf16[32,2,8192]{2,0,1:T(8,128)(2,1)S(1)} copy(bf16[32,2,8192]{2,1,0:T(2,128)(2,1)} %bitcast.14) | data formatting | bytes 2097152 | tf_op jit(solution)/shard_map/reshape | solution.py:65
  1.8 0.7 %copy-done.1 = s32[1,1,18,2]{2,3,1,0:T(2,128)S(1)} copy-done((s32[1,1,18,2]{2,3,1,0:T(2,128)S(1)}, s32[1,1,18,2]{2,3,1,0:T(2,128)}, u32[]{:S(2)}) %copy-start.1) | copy-done | bytes 168
  3.1 5.1 %collective-permute-start = (bf16[32,2176]{1,0:T(8,128)(2,1)S(1)}, bf16[32,2176]{1,0:T(8,128)(2,1)S(1)}, u32[]{:S(2)}, u32[]{:S(2)}) collective-permute-start(bf16[32,2176]{1,0:T(8,128)(2,1)S(1)} %get-tuple-element.44), channel_id=1, source_target_pairs={{0,3},{1,2},{2,1},{3,0},{4,7},{5,6},{6,5},{7,4},{8,11},{9,10},{10,... | collective-permute-start | bytes 417800 | tf_op jit(solution)/shard_map/ppermute | solution.py:431
  9.4 3.4 %collective-permute-done.refs_0_.refs_6_ = bf16[32,2176]{1,0:T(8,128)(2,1)S(1)} collective-permute-done((bf16[32,2176]{1,0:T(8,128)(2,1)S(1)}, bf16[32,2176]{1,0:T(8,128)(2,1)S(1)}, u32[]{:S(2)}, u32[]{:S(2)}) %collective-permute-start) | collective-permute-done | bytes 139296 | tf_op jit(solution)/shard_map/ppermute | solution.py:431
  12.8 3.2 %collective-permute-done.1.refs_1_.refs_7_ = bf16[32,2176]{1,0:T(8,128)(2,1)S(1)} collective-permute-done((bf16[32,2176]{1,0:T(8,128)(2,1)S(1)}, bf16[32,2176]{1,0:T(8,128)(2,1)S(1)}, u32[]{:S(2)}, u32[]{:S(2)}) %collective-permute-start.1) | collective-permute-done | bytes 139296 | tf_op jit(solution)/shard_map/ppermute | solution.py:431
  16.0 1.8 %collective-permute-start.2 = (bf16[32,2048]{1,0:T(8,128)(2,1)S(1)}, bf16[32,2048]{1,0:T(8,128)(2,1)S(1)}, u32[]{:S(2)}, u32[]{:S(2)}) collective-permute-start(bf16[32,2048]{1,0:T(8,128)(2,1)S(1)} %get-tuple-element.50), channel_id=1, source_target_pairs={{0,3},{1,2},{2,1},{3,0},{4,7},{5,6},{6,5},{7,4},{8,11},{9,10},{10,... | collective-permute-start | bytes 393224 | tf_op jit(solution)/shard_map/ppermute | solution.py:431
  17.8 2.6 %collective-permute-start.4 = (bf16[32,2048]{1,0:T(8,128)(2,1)S(1)}, bf16[32,2048]{1,0:T(8,128)(2,1)S(1)}, u32[]{:S(2)}, u32[]{:S(2)}) collective-permute-start(bf16[32,2048]{1,0:T(8,128)(2,1)S(1)} %get-tuple-element.52), channel_id=1, source_target_pairs={{0,2},{1,3},{2,0},{3,1},{4,6},{5,7},{6,4},{7,5},{8,10},{9,11},{10,... | collective-permute-start | bytes 393224 | tf_op jit(solution)/shard_map/ppermute | solution.py:431
  20.4 1.3 %tables.1.refs_4_ = bf16[2048,1024]{1,0:T(8,128)(2,1)S(1)} custom-call(s32[1]{0:T(128)} %bitcast.2.place_ref.first_ref.place, f32[16,512]{1,0:T(8,128)S(1)} %get-tuple-element.89.hi_cos_ref, f32[16,512]{1,0:T(8,128)S(1)} %get-tuple-element.84.hi_sin_ref, f32[16,512]{1,0:T(8,128)S(1)} %get-tuple-element.90.mid_cos_ref, ...), custom_call_target="tpu_custom_call" | custom-call | flops 8388608 | bytes 4194304 | tf_op jit(solution)/shard_map/tables/pallas_call | solution.py:131
  21.8 1.6 %collective-permute-done.5.refs_2_.refs_6_ = bf16[32,2176]{1,0:T(8,128)(2,1)S(1)} collective-permute-done((bf16[32,2176]{1,0:T(8,128)(2,1)S(1)}, bf16[32,2176]{1,0:T(8,128)(2,1)S(1)}, u32[]{:S(2)}, u32[]{:S(2)}) %collective-permute-start.5) | collective-permute-done | bytes 139296 | tf_op jit(solution)/shard_map/ppermute | solution.py:431
  23.4 1.8 %correlate.4 = (f32[96,1024]{1,0:T(8,128)S(1)}, f32[96,128]{1,0:T(8,128)S(1)}, bf16[192,128]{1,0:T(8,128)(2,1)S(1)}) custom-call(s32[1]{0:T(128)} %bitcast.2.place_ref.first_ref.place, bf16[32,2176]{1,0:T(8,128)(2,1)S(1)} %collective-permute-done.refs_0_.refs_6_, bf16[32,2176]{1,0:T(8,128)(2,1)S(1)} %collective-permute-done.1.refs_1_.refs_7_, ...), custom_call_target="tpu_custom_call" | custom-call | flops 201326592 | bytes 2097152 | tf_op jit(solution)/shard_map/correlate/pallas_call | solution.py:309
  25.2 2.7 %correlate.5 = (f32[224,1024]{1,0:T(8,128)S(1)}, f32[224,128]{1,0:T(8,128)S(1)}, bf16[448,128]{1,0:T(8,128)(2,1)S(1)}) custom-call(s32[1]{0:T(128)} %bitcast.2.place_ref.first_ref.place, bf16[32,2176]{1,0:T(8,128)(2,1)S(1)} %collective-permute-done.refs_0_.refs_6_, bf16[32,2176]{1,0:T(8,128)(2,1)S(1)} %collective-permute-done.1.refs_1_.refs_7_, ...), custom_call_target="tpu_custom_call" | custom-call | flops 469762048 | bytes 2097152 | tf_op jit(solution)/shard_map/correlate/pallas_call | solution.py:309
  27.9 3.3 %collective-permute-done.4.refs_2_ = bf16[32,2048]{1,0:T(8,128)(2,1)S(1)} collective-permute-done((bf16[32,2048]{1,0:T(8,128)(2,1)S(1)}, bf16[32,2048]{1,0:T(8,128)(2,1)S(1)}, u32[]{:S(2)}, u32[]{:S(2)}) %collective-permute-start.4) | collective-permute-done | bytes 131104 | tf_op jit(solution)/shard_map/ppermute | solution.py:431
  31.3 2.6 %correlate.7 = (bf16[72,1024]{1,0:T(8,128)(2,1)S(1)}, bf16[72,1024]{1,0:T(8,128)(2,1)S(1)}, bf16[72,1024]{1,0:T(8,128)(2,1)S(1)}) custom-call(s32[1]{0:T(128)} %bitcast.2.place_ref.first_ref.place, bf16[32,2048]{1,0:T(8,128)(2,1)S(1)} %collective-permute-done.2.refs_0_, bf16[32,2048]{1,0:T(8,128)(2,1)S(1)} %collective-permute-done.3.refs_1_, ...), custom_call_target="tpu_custom_call" | custom-call | flops 469762048 | bytes 2097152 | tf_op jit(solution)/shard_map/correlate/pallas_call | solution.py:309
  33.9 3.0 %collective-permute-start.8 = (bf16[72,1024]{1,0:T(8,128)(2,1)S(1)}, bf16[72,1024]{1,0:T(8,128)(2,1)S(1)}, u32[]{:S(2)}, u32[]{:S(2)}) collective-permute-start(bf16[72,1024]{1,0:T(8,128)(2,1)S(1)} %get-tuple-element.75), channel_id=1, source_target_pairs={{0,1},{1,0},{2,3},{3,2},{4,5},{5,4},{6,7},{7,6},{8,9},{9,8},{10,11... | collective-permute-start | bytes 442376 | tf_op jit(solution)/shard_map/ppermute | solution.py:431
  37.0 1.7 %correlate.6 = bf16[72,1024]{1,0:T(8,128)(2,1)S(1)} custom-call(s32[1]{0:T(128)} %bitcast.2.place_ref.first_ref.place, bf16[32,2048]{1,0:T(8,128)(2,1)S(1)} %collective-permute-done.2.refs_0_, bf16[32,2048]{1,0:T(8,128)(2,1)S(1)} %collective-permute-done.3.refs_1_, bf16[32,2048]{1,0:T(8,128)(2,1)S(1)} %collective-permute-done.4.refs_2_, ...), custom_call_target="tpu_custom_call" | custom-call | flops 201326592 | bytes 2097152 | tf_op jit(solution)/shard_map/correlate/pallas_call | solution.py:309
  38.6 1.4 %collective-permute-start.6 = (bf16[72,1024]{1,0:T(8,128)(2,1)S(1)}, bf16[72,1024]{1,0:T(8,128)(2,1)S(1)}, u32[]{:S(2)}, u32[]{:S(2)}) collective-permute-start(bf16[72,1024]{1,0:T(8,128)(2,1)S(1)} %correlate.6), channel_id=1, source_target_pairs={{0,3},{1,2},{2,1},{3,0},{4,7},{5,6},{6,5},{7,4},{8,11},{9,10},{10,... | collective-permute-start | bytes 442376 | tf_op jit(solution)/shard_map/ppermute | solution.py:431
  40.1 6.1 %collective-permute-done.7.refs_1_ = bf16[72,1024]{1,0:T(8,128)(2,1)S(1)} collective-permute-done((bf16[72,1024]{1,0:T(8,128)(2,1)S(1)}, bf16[72,1024]{1,0:T(8,128)(2,1)S(1)}, u32[]{:S(2)}, u32[]{:S(2)}) %collective-permute-start.7) | collective-permute-done | bytes 147488 | tf_op jit(solution)/shard_map/ppermute | solution.py:431
  46.8 1.3 %collective-permute-done.9.brought_ref = bf16[64,1024]{1,0:T(8,128)(2,1)S(1)} collective-permute-done((bf16[64,1024]{1,0:T(8,128)(2,1)S(1)}, bf16[64,1024]{1,0:T(8,128)(2,1)S(1)}, u32[]{:S(2)}, u32[]{:S(2)}) %collective-permute-start.9) | collective-permute-done | bytes 131104 | tf_op jit(solution)/shard_map/ppermute | solution.py:459
  48.1 1.6 %collective-permute-start.10 = (bf16[32,1024]{1,0:T(8,128)(2,1)S(1)}, bf16[32,1024]{1,0:T(8,128)(2,1)S(1)}, u32[]{:S(2)}, u32[]{:S(2)}) collective-permute-start(bf16[32,1024]{1,0:T(8,128)(2,1)S(1)} %get-tuple-element.80), channel_id=1, source_target_pairs={{0,8},{4,12},{8,0},{12,4},{16,24},{20,28},{24,16},{28,20},{1,9},{5... | collective-permute-start | bytes 196616 | tf_op jit(solution)/shard_map/ppermute | solution.py:459
  49.7 1.5 %collective-permute-start.11 = (bf16[32,1024]{1,0:T(8,128)(2,1)S(1)}, bf16[32,1024]{1,0:T(8,128)(2,1)S(1)}, u32[]{:S(2)}, u32[]{:S(2)}) collective-permute-start(bf16[32,1024]{1,0:T(8,128)(2,1)S(1)} %get-tuple-element.81), channel_id=1, source_target_pairs={{0,16},{4,20},{8,24},{12,28},{16,0},{20,4},{24,8},{28,12},{1,17},{... | collective-permute-start | bytes 196616 | tf_op jit(solution)/shard_map/ppermute | solution.py:459
  51.7 0.8 %collective-permute-done.10.refs_1_ = bf16[32,1024]{1,0:T(8,128)(2,1)S(1)} collective-permute-done((bf16[32,1024]{1,0:T(8,128)(2,1)S(1)}, bf16[32,1024]{1,0:T(8,128)(2,1)S(1)}, u32[]{:S(2)}, u32[]{:S(2)}) %collective-permute-start.10) | collective-permute-done | bytes 65568 | tf_op jit(solution)/shard_map/ppermute | solution.py:459
  52.4 1.5 %collective-permute-done.11.refs_2_ = bf16[32,1024]{1,0:T(8,128)(2,1)S(1)} collective-permute-done((bf16[32,1024]{1,0:T(8,128)(2,1)S(1)}, bf16[32,1024]{1,0:T(8,128)(2,1)S(1)}, u32[]{:S(2)}, u32[]{:S(2)}) %collective-permute-start.11) | collective-permute-done | bytes 65568 | tf_op jit(solution)/shard_map/ppermute | solution.py:459
  53.9 2.4 %collective-permute-done.12.refs_3_ = bf16[32,1024]{1,0:T(8,128)(2,1)S(1)} collective-permute-done((bf16[32,1024]{1,0:T(8,128)(2,1)S(1)}, bf16[32,1024]{1,0:T(8,128)(2,1)S(1)}, u32[]{:S(2)}, u32[]{:S(2)}) %collective-permute-start.12) | collective-permute-done | bytes 65568 | tf_op jit(solution)/shard_map/ppermute | solution.py:459
  56.4 0.8 %widen.1 = f32[24,4,1024]{2,1,0:T(4,128)} custom-call(s32[1]{0:T(128)} %bitcast.mine_ref, bf16[32,1024]{1,0:T(8,128)(2,1)S(1)} %get-tuple-element.79.refs_0_, bf16[32,1024]{1,0:T(8,128)(2,1)S(1)} %collective-permute-done.10.refs_1_, bf16[32,1024]{1,0:T(8,128)(2,1)S(1)} %collective-permute-done.11.refs_2_, bf16[32,1024]{1,0:T(8,128)(2,1)S(1)} %collective-permute-done.12.refs_3_), custom_call_target="tpu_custom_call" | custom-call | tf_op jit(solution)/shard_map/widen/pallas_call | solution.py:410
  (26 shorter events, 3.0 us)
Async XLA Ops:
  0.0 23.4 %copy-start = (f32[2,128]{1,0:T(2,128)S(1)}, f32[2,128]{1,0:T(2,128)}, u32[]{:S(2)}) copy-start(f32[2,128]{1,0:T(2,128)} %constant.36.clone.refs_5_) | copy-start | bytes 3076
  1.8 0.7 %copy-start.1 = (s32[1,1,18,2]{2,3,1,0:T(2,128)S(1)}, s32[1,1,18,2]{2,3,1,0:T(2,128)}, u32[]{:S(2)}) copy-start(s32[1,1,18,2]{2,3,1,0:T(2,128)} %param.8) | copy-start | bytes 436
  3.1 9.7 %collective-permute-start = (bf16[32,2176]{1,0:T(8,128)(2,1)S(1)}, bf16[32,2176]{1,0:T(8,128)(2,1)S(1)}, u32[]{:S(2)}, u32[]{:S(2)}) collective-permute-start(bf16[32,2176]{1,0:T(8,128)(2,1)S(1)} %get-tuple-element.44), channel_id=1, source_target_pairs={{0,3},{1,2},{2,1},{3,0},{4,7},{5,6},{6,5},{7,4},{8,11},{9,10},{10,... | collective-permute-start | bytes 417800 | tf_op jit(solution)/shard_map/ppermute | solution.py:431
  8.2 7.7 %collective-permute-start.1 = (bf16[32,2176]{1,0:T(8,128)(2,1)S(1)}, bf16[32,2176]{1,0:T(8,128)(2,1)S(1)}, u32[]{:S(2)}, u32[]{:S(2)}) collective-permute-start(bf16[32,2176]{1,0:T(8,128)(2,1)S(1)} %get-tuple-element.45), channel_id=1, source_target_pairs={{0,1},{1,0},{2,3},{3,2},{4,5},{5,4},{6,7},{7,6},{8,9},{9,8},{10,11... | collective-permute-start | bytes 417800 | tf_op jit(solution)/shard_map/ppermute | solution.py:431
  8.2 15.1 %collective-permute-start.5 = (bf16[32,2176]{1,0:T(8,128)(2,1)S(1)}, bf16[32,2176]{1,0:T(8,128)(2,1)S(1)}, u32[]{:S(2)}, u32[]{:S(2)}) collective-permute-start(bf16[32,2176]{1,0:T(8,128)(2,1)S(1)} %get-tuple-element.56), channel_id=1, source_target_pairs={{0,2},{1,3},{2,0},{3,1},{4,6},{5,7},{6,4},{7,5},{8,10},{9,11},{10,... | collective-permute-start | bytes 417800 | tf_op jit(solution)/shard_map/ppermute | solution.py:431
  16.0 11.9 %collective-permute-start.2 = (bf16[32,2048]{1,0:T(8,128)(2,1)S(1)}, bf16[32,2048]{1,0:T(8,128)(2,1)S(1)}, u32[]{:S(2)}, u32[]{:S(2)}) collective-permute-start(bf16[32,2048]{1,0:T(8,128)(2,1)S(1)} %get-tuple-element.50), channel_id=1, source_target_pairs={{0,3},{1,2},{2,1},{3,0},{4,7},{5,6},{6,5},{7,4},{8,11},{9,10},{10,... | collective-permute-start | bytes 393224 | tf_op jit(solution)/shard_map/ppermute | solution.py:431
  17.8 10.2 %collective-permute-start.3 = (bf16[32,2048]{1,0:T(8,128)(2,1)S(1)}, bf16[32,2048]{1,0:T(8,128)(2,1)S(1)}, u32[]{:S(2)}, u32[]{:S(2)}) collective-permute-start(bf16[32,2048]{1,0:T(8,128)(2,1)S(1)} %get-tuple-element.51), channel_id=1, source_target_pairs={{0,1},{1,0},{2,3},{3,2},{4,5},{5,4},{6,7},{7,6},{8,9},{9,8},{10,11... | collective-permute-start | bytes 393224 | tf_op jit(solution)/shard_map/ppermute | solution.py:431
  17.8 13.5 %collective-permute-start.4 = (bf16[32,2048]{1,0:T(8,128)(2,1)S(1)}, bf16[32,2048]{1,0:T(8,128)(2,1)S(1)}, u32[]{:S(2)}, u32[]{:S(2)}) collective-permute-start(bf16[32,2048]{1,0:T(8,128)(2,1)S(1)} %get-tuple-element.52), channel_id=1, source_target_pairs={{0,2},{1,3},{2,0},{3,1},{4,6},{5,7},{6,4},{7,5},{8,10},{9,11},{10,... | collective-permute-start | bytes 393224 | tf_op jit(solution)/shard_map/ppermute | solution.py:431
  31.3 14.9 %copy-start.2 = (s32[1,1,18,1]{2,3,1,0:T(1,128)S(1)}, s32[1,1,18,1]{2,3,1,0:T(1,128)}, u32[]{:S(2)}) copy-start(s32[1,1,18,1]{2,3,1,0:T(1,128)} %param.9) | copy-start | bytes 220
  33.9 12.3 %collective-permute-start.7 = (bf16[72,1024]{1,0:T(8,128)(2,1)S(1)}, bf16[72,1024]{1,0:T(8,128)(2,1)S(1)}, u32[]{:S(2)}, u32[]{:S(2)}) collective-permute-start(bf16[72,1024]{1,0:T(8,128)(2,1)S(1)} %get-tuple-element.74), channel_id=1, source_target_pairs={{0,2},{1,3},{2,0},{3,1},{4,6},{5,7},{6,4},{7,5},{8,10},{9,11},{10,... | collective-permute-start | bytes 442376 | tf_op jit(solution)/shard_map/ppermute | solution.py:431
  33.9 12.2 %collective-permute-start.8 = (bf16[72,1024]{1,0:T(8,128)(2,1)S(1)}, bf16[72,1024]{1,0:T(8,128)(2,1)S(1)}, u32[]{:S(2)}, u32[]{:S(2)}) collective-permute-start(bf16[72,1024]{1,0:T(8,128)(2,1)S(1)} %get-tuple-element.75), channel_id=1, source_target_pairs={{0,1},{1,0},{2,3},{3,2},{4,5},{5,4},{6,7},{7,6},{8,9},{9,8},{10,11... | collective-permute-start | bytes 442376 | tf_op jit(solution)/shard_map/ppermute | solution.py:431
  38.6 7.5 %collective-permute-start.6 = (bf16[72,1024]{1,0:T(8,128)(2,1)S(1)}, bf16[72,1024]{1,0:T(8,128)(2,1)S(1)}, u32[]{:S(2)}, u32[]{:S(2)}) collective-permute-start(bf16[72,1024]{1,0:T(8,128)(2,1)S(1)} %correlate.6), channel_id=1, source_target_pairs={{0,3},{1,2},{2,1},{3,0},{4,7},{5,6},{6,5},{7,4},{8,11},{9,10},{10,... | collective-permute-start | bytes 442376 | tf_op jit(solution)/shard_map/ppermute | solution.py:431
  46.7 1.4 %collective-permute-start.9 = (bf16[64,1024]{1,0:T(8,128)(2,1)S(1)}, bf16[64,1024]{1,0:T(8,128)(2,1)S(1)}, u32[]{:S(2)}, u32[]{:S(2)}) collective-permute-start(bf16[64,1024]{1,0:T(8,128)(2,1)S(1)} %get-tuple-element.78), channel_id=1, source_target_pairs={{0,4},{4,0},{8,12},{12,8},{16,20},{20,16},{24,28},{28,24},{1,5},{5... | collective-permute-start | bytes 393224 | tf_op jit(solution)/shard_map/ppermute | solution.py:459
  48.1 4.3 %collective-permute-start.10 = (bf16[32,1024]{1,0:T(8,128)(2,1)S(1)}, bf16[32,1024]{1,0:T(8,128)(2,1)S(1)}, u32[]{:S(2)}, u32[]{:S(2)}) collective-permute-start(bf16[32,1024]{1,0:T(8,128)(2,1)S(1)} %get-tuple-element.80), channel_id=1, source_target_pairs={{0,8},{4,12},{8,0},{12,4},{16,24},{20,28},{24,16},{28,20},{1,9},{5... | collective-permute-start | bytes 196616 | tf_op jit(solution)/shard_map/ppermute | solution.py:459
  49.7 4.3 %collective-permute-start.11 = (bf16[32,1024]{1,0:T(8,128)(2,1)S(1)}, bf16[32,1024]{1,0:T(8,128)(2,1)S(1)}, u32[]{:S(2)}, u32[]{:S(2)}) collective-permute-start(bf16[32,1024]{1,0:T(8,128)(2,1)S(1)} %get-tuple-element.81), channel_id=1, source_target_pairs={{0,16},{4,20},{8,24},{12,28},{16,0},{20,4},{24,8},{28,12},{1,17},{... | collective-permute-start | bytes 196616 | tf_op jit(solution)/shard_map/ppermute | solution.py:459
  51.2 5.2 %collective-permute-start.12 = (bf16[32,1024]{1,0:T(8,128)(2,1)S(1)}, bf16[32,1024]{1,0:T(8,128)(2,1)S(1)}, u32[]{:S(2)}, u32[]{:S(2)}) collective-permute-start(bf16[32,1024]{1,0:T(8,128)(2,1)S(1)} %get-tuple-element.82), channel_id=1, source_target_pairs={{0,24},{4,28},{8,16},{12,20},{16,8},{20,12},{24,0},{28,4},{1,25},{... | collective-permute-start | bytes 196616 | tf_op jit(solution)/shard_map/ppermute | solution.py:459

commit v9 on v8

--- a/solution.py
+++ b/solution.py
@@ -450,9 +450,11 @@
     for d, panel in zip(sequence(parts), ordered):
         second[d] = panel
     partials = []
-    for wanted, before in zip(halves, sums):
-        for d, rows in zip(wanted, correlate(second, table, place, parts, wanted, 1, before)):
-            partials.append(swap(rows, d) if d else rows)
+    (foremost,) = correlate(second, table, place, parts, halves[0], 1, sums[0])
+    foremost, before = lax.optimization_barrier((foremost, sums[1]))
+    rest = correlate(second, table, place, parts, halves[1], 1, before)
+    for d, rows in zip(order, [foremost, *rest]):
+        partials.append(swap(rows, d) if d else rows)
     mine = lax.axis_index("grp")
 
     def trade(array, m):

time: 57.8 us -> 59.4 us (1.028)
  waiting for transfers between devices: 23.7 us -> 25.4 us
    ppermute x9, waiting for transfers between devices: 17.6 us -> 19.4 us  [swap(): return lax.ppermute(array, 'chan', [(i, i ^ d) for i in range(parts)])]
  transfers between devices with their start and end apart: 13 -> 13, of which waited for: 9 -> 9; matrix products, arithmetic and copies ran while one was open for 1% -> 1% of each run, Pallas kernels for 13% -> 10%
where the time goes in v9:
time: 59.4 us; the launch traced here: 58.8 us
  waiting for transfers between devices  25.4 us (43%)
  starting transfers between devices  18.2 us (31%)
  Pallas kernels  12 us (20%)
  local copies, waits for them, and re-layouts  2.51 us (4%)
    ppermute x9, waiting for transfers between devices, swap(): return lax.ppermute(array, 'chan', [(i, i ^ d) for i in range(parts)])  19.4 us
    ppermute x9, starting transfers between devices, swap(): return lax.ppermute(array, 'chan', [(i, i ^ d) for i in range(parts)])  14.6 us
    pallas_call x4, Pallas kernels, correlate(): pl.pallas_call(functools.partial(corr_kernel, per_step, parts, lists, wav...  8.77 us
    ppermute x4, waiting for transfers between devices, trade(): return lax.ppermute(array, 'grp', [(i, i ^ m) for i in range(groups)])  6.01 us
    ppermute x4, starting transfers between devices, trade(): return lax.ppermute(array, 'grp', [(i, i ^ m) for i in range(groups)])  3.62 us
    reshape x1, local copies, waits for them, and re-layouts, whiten(): planes = jnp.transpose(spectra.reshape(rows, 2, F), (1, 0, 2))  1.82 us
    pallas_call x1, Pallas kernels, tables(): pl.pallas_call(table_kernel, grid_spec=pltpu.PrefetchScalarGridSpec(num_s...  1.33 us
  transfers between devices with their start and end apart: 13, of which 9 were waited for; matrix products, arithmetic and copies ran while one was open for 1% of the time, Pallas kernels for 10%

profile of v9, /device:TPU:0, one launch (start us, length us, event | category | flops | bytes accessed | tf_op | source)
XLA Modules:
  0.0 58.8 jit_solution(17493534454271935307)
XLA Ops:
  0.0 1.8 %copy.11 = bf16[32,2,8192]{2,0,1:T(8,128)(2,1)S(1)} copy(bf16[32,2,8192]{2,1,0:T(2,128)(2,1)} %bitcast.14) | data formatting | bytes 2097152 | tf_op jit(solution)/shard_map/reshape | solution.py:65
  1.8 0.7 %copy-done.1 = s32[1,1,18,2]{2,3,1,0:T(2,128)S(1)} copy-done((s32[1,1,18,2]{2,3,1,0:T(2,128)S(1)}, s32[1,1,18,2]{2,3,1,0:T(2,128)}, u32[]{:S(2)}) %copy-start.1) | copy-done | bytes 168
  3.1 5.1 %collective-permute-start = (bf16[32,2176]{1,0:T(8,128)(2,1)S(1)}, bf16[32,2176]{1,0:T(8,128)(2,1)S(1)}, u32[]{:S(2)}, u32[]{:S(2)}) collective-permute-start(bf16[32,2176]{1,0:T(8,128)(2,1)S(1)} %get-tuple-element.48), channel_id=1, source_target_pairs={{0,3},{1,2},{2,1},{3,0},{4,7},{5,6},{6,5},{7,4},{8,11},{9,10},{10,... | collective-permute-start | bytes 417800 | tf_op jit(solution)/shard_map/ppermute | solution.py:431
  9.4 3.4 %collective-permute-done.refs_0_.refs_6_ = bf16[32,2176]{1,0:T(8,128)(2,1)S(1)} collective-permute-done((bf16[32,2176]{1,0:T(8,128)(2,1)S(1)}, bf16[32,2176]{1,0:T(8,128)(2,1)S(1)}, u32[]{:S(2)}, u32[]{:S(2)}) %collective-permute-start) | collective-permute-done | bytes 139296 | tf_op jit(solution)/shard_map/ppermute | solution.py:431
  12.8 3.2 %collective-permute-done.1.refs_1_.refs_7_ = bf16[32,2176]{1,0:T(8,128)(2,1)S(1)} collective-permute-done((bf16[32,2176]{1,0:T(8,128)(2,1)S(1)}, bf16[32,2176]{1,0:T(8,128)(2,1)S(1)}, u32[]{:S(2)}, u32[]{:S(2)}) %collective-permute-start.1) | collective-permute-done | bytes 139296 | tf_op jit(solution)/shard_map/ppermute | solution.py:431
  16.0 1.8 %collective-permute-start.2 = (bf16[32,2048]{1,0:T(8,128)(2,1)S(1)}, bf16[32,2048]{1,0:T(8,128)(2,1)S(1)}, u32[]{:S(2)}, u32[]{:S(2)}) collective-permute-start(bf16[32,2048]{1,0:T(8,128)(2,1)S(1)} %get-tuple-element.54), channel_id=1, source_target_pairs={{0,3},{1,2},{2,1},{3,0},{4,7},{5,6},{6,5},{7,4},{8,11},{9,10},{10,... | collective-permute-start | bytes 393224 | tf_op jit(solution)/shard_map/ppermute | solution.py:431
  17.8 2.6 %collective-permute-start.4 = (bf16[32,2048]{1,0:T(8,128)(2,1)S(1)}, bf16[32,2048]{1,0:T(8,128)(2,1)S(1)}, u32[]{:S(2)}, u32[]{:S(2)}) collective-permute-start(bf16[32,2048]{1,0:T(8,128)(2,1)S(1)} %get-tuple-element.56), channel_id=1, source_target_pairs={{0,2},{1,3},{2,0},{3,1},{4,6},{5,7},{6,4},{7,5},{8,10},{9,11},{10,... | collective-permute-start | bytes 393224 | tf_op jit(solution)/shard_map/ppermute | solution.py:431
  20.4 1.3 %tables.1.refs_4_ = bf16[2048,1024]{1,0:T(8,128)(2,1)S(1)} custom-call(s32[1]{0:T(128)} %bitcast.2.place_ref.first_ref.place, f32[16,512]{1,0:T(8,128)S(1)} %get-tuple-element.97.hi_cos_ref, f32[16,512]{1,0:T(8,128)S(1)} %get-tuple-element.92.hi_sin_ref, f32[16,512]{1,0:T(8,128)S(1)} %get-tuple-element.98.mid_cos_ref, ...), custom_call_target="tpu_custom_call" | custom-call | flops 8388608 | bytes 4194304 | tf_op jit(solution)/shard_map/tables/pallas_call | solution.py:131
  21.8 1.6 %collective-permute-done.5.refs_2_.refs_6_ = bf16[32,2176]{1,0:T(8,128)(2,1)S(1)} collective-permute-done((bf16[32,2176]{1,0:T(8,128)(2,1)S(1)}, bf16[32,2176]{1,0:T(8,128)(2,1)S(1)}, u32[]{:S(2)}, u32[]{:S(2)}) %collective-permute-start.5) | collective-permute-done | bytes 139296 | tf_op jit(solution)/shard_map/ppermute | solution.py:431
  23.4 1.8 %correlate.4 = (f32[96,1024]{1,0:T(8,128)S(1)}, f32[96,128]{1,0:T(8,128)S(1)}, bf16[192,128]{1,0:T(8,128)(2,1)S(1)}) custom-call(s32[1]{0:T(128)} %bitcast.2.place_ref.first_ref.place, bf16[32,2176]{1,0:T(8,128)(2,1)S(1)} %collective-permute-done.refs_0_.refs_6_, bf16[32,2176]{1,0:T(8,128)(2,1)S(1)} %collective-permute-done.1.refs_1_.refs_7_, ...), custom_call_target="tpu_custom_call" | custom-call | flops 201326592 | bytes 2097152 | tf_op jit(solution)/shard_map/correlate/pallas_call | solution.py:309
  25.2 2.7 %correlate.5 = (f32[224,1024]{1,0:T(8,128)S(1)}, f32[224,128]{1,0:T(8,128)S(1)}, bf16[448,128]{1,0:T(8,128)(2,1)S(1)}) custom-call(s32[1]{0:T(128)} %bitcast.2.place_ref.first_ref.place, bf16[32,2176]{1,0:T(8,128)(2,1)S(1)} %collective-permute-done.refs_0_.refs_6_, bf16[32,2176]{1,0:T(8,128)(2,1)S(1)} %collective-permute-done.1.refs_1_.refs_7_, ...), custom_call_target="tpu_custom_call" | custom-call | flops 469762048 | bytes 2097152 | tf_op jit(solution)/shard_map/correlate/pallas_call | solution.py:309
  27.9 3.3 %collective-permute-done.4.refs_2_ = bf16[32,2048]{1,0:T(8,128)(2,1)S(1)} collective-permute-done((bf16[32,2048]{1,0:T(8,128)(2,1)S(1)}, bf16[32,2048]{1,0:T(8,128)(2,1)S(1)}, u32[]{:S(2)}, u32[]{:S(2)}) %collective-permute-start.4) | collective-permute-done | bytes 131104 | tf_op jit(solution)/shard_map/ppermute | solution.py:431
  31.3 1.7 %correlate.6 = bf16[72,1024]{1,0:T(8,128)(2,1)S(1)} custom-call(s32[1]{0:T(128)} %bitcast.2.place_ref.first_ref.place, bf16[32,2048]{1,0:T(8,128)(2,1)S(1)} %collective-permute-done.2.refs_0_, bf16[32,2048]{1,0:T(8,128)(2,1)S(1)} %collective-permute-done.3.refs_1_, bf16[32,2048]{1,0:T(8,128)(2,1)S(1)} %collective-permute-done.4.refs_2_, ...), custom_call_target="tpu_custom_call" | custom-call | flops 201326592 | bytes 2097152 | tf_op jit(solution)/shard_map/correlate/pallas_call | solution.py:309
  32.9 2.6 %correlate.7 = (bf16[72,1024]{1,0:T(8,128)(2,1)S(1)}, bf16[72,1024]{1,0:T(8,128)(2,1)S(1)}, bf16[72,1024]{1,0:T(8,128)(2,1)S(1)}) custom-call(s32[1]{0:T(128)} %bitcast.2.place_ref.first_ref.place, bf16[32,2048]{1,0:T(8,128)(2,1)S(1)} %collective-permute-done.2.refs_0_, bf16[32,2048]{1,0:T(8,128)(2,1)S(1)} %collective-permute-done.3.refs_1_, ...), custom_call_target="tpu_custom_call" | custom-call | flops 469762048 | bytes 2097152 | tf_op jit(solution)/shard_map/correlate/pallas_call | solution.py:309
  35.6 3.0 %collective-permute-start.8 = (bf16[72,1024]{1,0:T(8,128)(2,1)S(1)}, bf16[72,1024]{1,0:T(8,128)(2,1)S(1)}, u32[]{:S(2)}, u32[]{:S(2)}) collective-permute-start(bf16[72,1024]{1,0:T(8,128)(2,1)S(1)} %get-tuple-element.83), channel_id=1, source_target_pairs={{0,1},{1,0},{2,3},{3,2},{4,5},{5,4},{6,7},{7,6},{8,9},{9,8},{10,11... | collective-permute-start | bytes 442376 | tf_op jit(solution)/shard_map/ppermute | solution.py:431
  38.6 1.3 %collective-permute-start.6 = (bf16[72,1024]{1,0:T(8,128)(2,1)S(1)}, bf16[72,1024]{1,0:T(8,128)(2,1)S(1)}, u32[]{:S(2)}, u32[]{:S(2)}) collective-permute-start(bf16[72,1024]{1,0:T(8,128)(2,1)S(1)} %correlate.6), channel_id=1, source_target_pairs={{0,3},{1,2},{2,1},{3,0},{4,7},{5,6},{6,5},{7,4},{8,11},{9,10},{10,... | collective-permute-start | bytes 442376 | tf_op jit(solution)/shard_map/ppermute | solution.py:431
  40.0 7.8 %collective-permute-done.7.refs_1_ = bf16[72,1024]{1,0:T(8,128)(2,1)S(1)} collective-permute-done((bf16[72,1024]{1,0:T(8,128)(2,1)S(1)}, bf16[72,1024]{1,0:T(8,128)(2,1)S(1)}, u32[]{:S(2)}, u32[]{:S(2)}) %collective-permute-start.7) | collective-permute-done | bytes 147488 | tf_op jit(solution)/shard_map/ppermute | solution.py:431
  48.5 1.3 %collective-permute-done.9.brought_ref = bf16[64,1024]{1,0:T(8,128)(2,1)S(1)} collective-permute-done((bf16[64,1024]{1,0:T(8,128)(2,1)S(1)}, bf16[64,1024]{1,0:T(8,128)(2,1)S(1)}, u32[]{:S(2)}, u32[]{:S(2)}) %collective-permute-start.9) | collective-permute-done | bytes 131104 | tf_op jit(solution)/shard_map/ppermute | solution.py:461
  49.8 1.6 %collective-permute-start.10 = (bf16[32,1024]{1,0:T(8,128)(2,1)S(1)}, bf16[32,1024]{1,0:T(8,128)(2,1)S(1)}, u32[]{:S(2)}, u32[]{:S(2)}) collective-permute-start(bf16[32,1024]{1,0:T(8,128)(2,1)S(1)} %get-tuple-element.88), channel_id=1, source_target_pairs={{0,8},{4,12},{8,0},{12,4},{16,24},{20,28},{24,16},{28,20},{1,9},{5... | collective-permute-start | bytes 196616 | tf_op jit(solution)/shard_map/ppermute | solution.py:461
  51.4 1.5 %collective-permute-start.11 = (bf16[32,1024]{1,0:T(8,128)(2,1)S(1)}, bf16[32,1024]{1,0:T(8,128)(2,1)S(1)}, u32[]{:S(2)}, u32[]{:S(2)}) collective-permute-start(bf16[32,1024]{1,0:T(8,128)(2,1)S(1)} %get-tuple-element.89), channel_id=1, source_target_pairs={{0,16},{4,20},{8,24},{12,28},{16,0},{20,4},{24,8},{28,12},{1,17},{... | collective-permute-start | bytes 196616 | tf_op jit(solution)/shard_map/ppermute | solution.py:461
  53.4 0.8 %collective-permute-done.10.refs_1_ = bf16[32,1024]{1,0:T(8,128)(2,1)S(1)} collective-permute-done((bf16[32,1024]{1,0:T(8,128)(2,1)S(1)}, bf16[32,1024]{1,0:T(8,128)(2,1)S(1)}, u32[]{:S(2)}, u32[]{:S(2)}) %collective-permute-start.10) | collective-permute-done | bytes 65568 | tf_op jit(solution)/shard_map/ppermute | solution.py:461
  54.1 1.5 %collective-permute-done.11.refs_2_ = bf16[32,1024]{1,0:T(8,128)(2,1)S(1)} collective-permute-done((bf16[32,1024]{1,0:T(8,128)(2,1)S(1)}, bf16[32,1024]{1,0:T(8,128)(2,1)S(1)}, u32[]{:S(2)}, u32[]{:S(2)}) %collective-permute-start.11) | collective-permute-done | bytes 65568 | tf_op jit(solution)/shard_map/ppermute | solution.py:461
  55.6 2.4 %collective-permute-done.12.refs_3_ = bf16[32,1024]{1,0:T(8,128)(2,1)S(1)} collective-permute-done((bf16[32,1024]{1,0:T(8,128)(2,1)S(1)}, bf16[32,1024]{1,0:T(8,128)(2,1)S(1)}, u32[]{:S(2)}, u32[]{:S(2)}) %collective-permute-start.12) | collective-permute-done | bytes 65568 | tf_op jit(solution)/shard_map/ppermute | solution.py:461
  58.0 0.8 %widen.1 = f32[24,4,1024]{2,1,0:T(4,128)} custom-call(s32[1]{0:T(128)} %bitcast.mine_ref, bf16[32,1024]{1,0:T(8,128)(2,1)S(1)} %get-tuple-element.87.refs_0_, bf16[32,1024]{1,0:T(8,128)(2,1)S(1)} %collective-permute-done.10.refs_1_, bf16[32,1024]{1,0:T(8,128)(2,1)S(1)} %collective-permute-done.11.refs_2_, bf16[32,1024]{1,0:T(8,128)(2,1)S(1)} %collective-permute-done.12.refs_3_), custom_call_target="tpu_custom_call" | custom-call | tf_op jit(solution)/shard_map/widen/pallas_call | solution.py:410
  (26 shorter events, 3.0 us)
Async XLA Ops:
  0.0 23.4 %copy-start = (f32[2,128]{1,0:T(2,128)S(1)}, f32[2,128]{1,0:T(2,128)}, u32[]{:S(2)}) copy-start(f32[2,128]{1,0:T(2,128)} %constant.36.clone.refs_5_) | copy-start | bytes 3076
  1.8 0.7 %copy-start.1 = (s32[1,1,18,2]{2,3,1,0:T(2,128)S(1)}, s32[1,1,18,2]{2,3,1,0:T(2,128)}, u32[]{:S(2)}) copy-start(s32[1,1,18,2]{2,3,1,0:T(2,128)} %param.8) | copy-start | bytes 436
  3.1 9.7 %collective-permute-start = (bf16[32,2176]{1,0:T(8,128)(2,1)S(1)}, bf16[32,2176]{1,0:T(8,128)(2,1)S(1)}, u32[]{:S(2)}, u32[]{:S(2)}) collective-permute-start(bf16[32,2176]{1,0:T(8,128)(2,1)S(1)} %get-tuple-element.48), channel_id=1, source_target_pairs={{0,3},{1,2},{2,1},{3,0},{4,7},{5,6},{6,5},{7,4},{8,11},{9,10},{10,... | collective-permute-start | bytes 417800 | tf_op jit(solution)/shard_map/ppermute | solution.py:431
  8.2 7.7 %collective-permute-start.1 = (bf16[32,2176]{1,0:T(8,128)(2,1)S(1)}, bf16[32,2176]{1,0:T(8,128)(2,1)S(1)}, u32[]{:S(2)}, u32[]{:S(2)}) collective-permute-start(bf16[32,2176]{1,0:T(8,128)(2,1)S(1)} %get-tuple-element.49), channel_id=1, source_target_pairs={{0,1},{1,0},{2,3},{3,2},{4,5},{5,4},{6,7},{7,6},{8,9},{9,8},{10,11... | collective-permute-start | bytes 417800 | tf_op jit(solution)/shard_map/ppermute | solution.py:431
  8.2 15.1 %collective-permute-start.5 = (bf16[32,2176]{1,0:T(8,128)(2,1)S(1)}, bf16[32,2176]{1,0:T(8,128)(2,1)S(1)}, u32[]{:S(2)}, u32[]{:S(2)}) collective-permute-start(bf16[32,2176]{1,0:T(8,128)(2,1)S(1)} %get-tuple-element.60), channel_id=1, source_target_pairs={{0,2},{1,3},{2,0},{3,1},{4,6},{5,7},{6,4},{7,5},{8,10},{9,11},{10,... | collective-permute-start | bytes 417800 | tf_op jit(solution)/shard_map/ppermute | solution.py:431
  16.0 11.9 %collective-permute-start.2 = (bf16[32,2048]{1,0:T(8,128)(2,1)S(1)}, bf16[32,2048]{1,0:T(8,128)(2,1)S(1)}, u32[]{:S(2)}, u32[]{:S(2)}) collective-permute-start(bf16[32,2048]{1,0:T(8,128)(2,1)S(1)} %get-tuple-element.54), channel_id=1, source_target_pairs={{0,3},{1,2},{2,1},{3,0},{4,7},{5,6},{6,5},{7,4},{8,11},{9,10},{10,... | collective-permute-start | bytes 393224 | tf_op jit(solution)/shard_map/ppermute | solution.py:431
  17.8 10.2 %collective-permute-start.3 = (bf16[32,2048]{1,0:T(8,128)(2,1)S(1)}, bf16[32,2048]{1,0:T(8,128)(2,1)S(1)}, u32[]{:S(2)}, u32[]{:S(2)}) collective-permute-start(bf16[32,2048]{1,0:T(8,128)(2,1)S(1)} %get-tuple-element.55), channel_id=1, source_target_pairs={{0,1},{1,0},{2,3},{3,2},{4,5},{5,4},{6,7},{7,6},{8,9},{9,8},{10,11... | collective-permute-start | bytes 393224 | tf_op jit(solution)/shard_map/ppermute | solution.py:431
  17.8 13.5 %collective-permute-start.4 = (bf16[32,2048]{1,0:T(8,128)(2,1)S(1)}, bf16[32,2048]{1,0:T(8,128)(2,1)S(1)}, u32[]{:S(2)}, u32[]{:S(2)}) collective-permute-start(bf16[32,2048]{1,0:T(8,128)(2,1)S(1)} %get-tuple-element.56), channel_id=1, source_target_pairs={{0,2},{1,3},{2,0},{3,1},{4,6},{5,7},{6,4},{7,5},{8,10},{9,11},{10,... | collective-permute-start | bytes 393224 | tf_op jit(solution)/shard_map/ppermute | solution.py:431
  32.9 14.9 %copy-start.2 = (s32[1,1,18,1]{2,3,1,0:T(1,128)S(1)}, s32[1,1,18,1]{2,3,1,0:T(1,128)}, u32[]{:S(2)}) copy-start(s32[1,1,18,1]{2,3,1,0:T(1,128)} %param.9) | copy-start | bytes 220
  35.5 12.3 %collective-permute-start.7 = (bf16[72,1024]{1,0:T(8,128)(2,1)S(1)}, bf16[72,1024]{1,0:T(8,128)(2,1)S(1)}, u32[]{:S(2)}, u32[]{:S(2)}) collective-permute-start(bf16[72,1024]{1,0:T(8,128)(2,1)S(1)} %get-tuple-element.82), channel_id=1, source_target_pairs={{0,2},{1,3},{2,0},{3,1},{4,6},{5,7},{6,4},{7,5},{8,10},{9,11},{10,... | collective-permute-start | bytes 442376 | tf_op jit(solution)/shard_map/ppermute | solution.py:431
  35.6 12.2 %collective-permute-start.8 = (bf16[72,1024]{1,0:T(8,128)(2,1)S(1)}, bf16[72,1024]{1,0:T(8,128)(2,1)S(1)}, u32[]{:S(2)}, u32[]{:S(2)}) collective-permute-start(bf16[72,1024]{1,0:T(8,128)(2,1)S(1)} %get-tuple-element.83), channel_id=1, source_target_pairs={{0,1},{1,0},{2,3},{3,2},{4,5},{5,4},{6,7},{7,6},{8,9},{9,8},{10,11... | collective-permute-start | bytes 442376 | tf_op jit(solution)/shard_map/ppermute | solution.py:431
  38.6 9.2 %collective-permute-start.6 = (bf16[72,1024]{1,0:T(8,128)(2,1)S(1)}, bf16[72,1024]{1,0:T(8,128)(2,1)S(1)}, u32[]{:S(2)}, u32[]{:S(2)}) collective-permute-start(bf16[72,1024]{1,0:T(8,128)(2,1)S(1)} %correlate.6), channel_id=1, source_target_pairs={{0,3},{1,2},{2,1},{3,0},{4,7},{5,6},{6,5},{7,4},{8,11},{9,10},{10,... | collective-permute-start | bytes 442376 | tf_op jit(solution)/shard_map/ppermute | solution.py:431
  48.4 1.4 %collective-permute-start.9 = (bf16[64,1024]{1,0:T(8,128)(2,1)S(1)}, bf16[64,1024]{1,0:T(8,128)(2,1)S(1)}, u32[]{:S(2)}, u32[]{:S(2)}) collective-permute-start(bf16[64,1024]{1,0:T(8,128)(2,1)S(1)} %get-tuple-element.86), channel_id=1, source_target_pairs={{0,4},{4,0},{8,12},{12,8},{16,20},{20,16},{24,28},{28,24},{1,5},{5... | collective-permute-start | bytes 393224 | tf_op jit(solution)/shard_map/ppermute | solution.py:461
  49.8 4.3 %collective-permute-start.10 = (bf16[32,1024]{1,0:T(8,128)(2,1)S(1)}, bf16[32,1024]{1,0:T(8,128)(2,1)S(1)}, u32[]{:S(2)}, u32[]{:S(2)}) collective-permute-start(bf16[32,1024]{1,0:T(8,128)(2,1)S(1)} %get-tuple-element.88), channel_id=1, source_target_pairs={{0,8},{4,12},{8,0},{12,4},{16,24},{20,28},{24,16},{28,20},{1,9},{5... | collective-permute-start | bytes 196616 | tf_op jit(solution)/shard_map/ppermute | solution.py:461
  51.4 4.3 %collective-permute-start.11 = (bf16[32,1024]{1,0:T(8,128)(2,1)S(1)}, bf16[32,1024]{1,0:T(8,128)(2,1)S(1)}, u32[]{:S(2)}, u32[]{:S(2)}) collective-permute-start(bf16[32,1024]{1,0:T(8,128)(2,1)S(1)} %get-tuple-element.89), channel_id=1, source_target_pairs={{0,16},{4,20},{8,24},{12,28},{16,0},{20,4},{24,8},{28,12},{1,17},{... | collective-permute-start | bytes 196616 | tf_op jit(solution)/shard_map/ppermute | solution.py:461
  52.9 5.2 %collective-permute-start.12 = (bf16[32,1024]{1,0:T(8,128)(2,1)S(1)}, bf16[32,1024]{1,0:T(8,128)(2,1)S(1)}, u32[]{:S(2)}, u32[]{:S(2)}) collective-permute-start(bf16[32,1024]{1,0:T(8,128)(2,1)S(1)} %get-tuple-element.90), channel_id=1, source_target_pairs={{0,24},{4,28},{8,16},{12,20},{16,8},{20,12},{24,0},{28,4},{1,25},{... | collective-permute-start | bytes 196616 | tf_op jit(solution)/shard_map/ppermute | solution.py:461

commit v10 on v8

--- a/solution.py
+++ b/solution.py
@@ -279,7 +279,7 @@
 
 def correlate(panels, table, place, parts, wanted, wave, before):
     chunks = table.shape[0] // LANES
-    per_step = min(4, chunks // LATE)
+    per_step = min(8, chunks // LATE)
     span = per_step * 2 * LANES
     rows = panels[0].shape[0]
     late = chunks // LATE // per_step

time: 57.8 us -> 57.2 us (0.990)
  Pallas kernels: 12 us -> 9.36 us
  waiting for transfers between devices: 23.7 us -> 25.8 us
    pallas_call x4, Pallas kernels: 8.76 us -> 6.1 us  [correlate(): pl.pallas_call(functools.partial(corr_kernel, per_step, parts, lists, wav...]
    ppermute x9, waiting for transfers between devices: 17.6 us -> 19.8 us  [swap(): return lax.ppermute(array, 'chan', [(i, i ^ d) for i in range(parts)])]
  transfers between devices with their start and end apart: 13 -> 13, of which waited for: 9 -> 9; matrix products, arithmetic and copies ran while one was open for 1% -> 1% of each run, Pallas kernels for 13% -> 10%
where the time goes in v10:
time: 57.2 us; the launch traced here: 56.6 us
  waiting for transfers between devices  25.8 us (45%)
  starting transfers between devices  18.3 us (32%)
  Pallas kernels  9.36 us (16%)
  local copies, waits for them, and re-layouts  2.51 us (4%)
    ppermute x9, waiting for transfers between devices, swap(): return lax.ppermute(array, 'chan', [(i, i ^ d) for i in range(parts)])  19.8 us
    ppermute x9, starting transfers between devices, swap(): return lax.ppermute(array, 'chan', [(i, i ^ d) for i in range(parts)])  14.7 us
    pallas_call x4, Pallas kernels, correlate(): pl.pallas_call(functools.partial(corr_kernel, per_step, parts, lists, wav...  6.1 us
    ppermute x4, waiting for transfers between devices, trade(): return lax.ppermute(array, 'grp', [(i, i ^ m) for i in range(groups)])  6.02 us
    ppermute x4, starting transfers between devices, trade(): return lax.ppermute(array, 'grp', [(i, i ^ m) for i in range(groups)])  3.62 us
    reshape x1, local copies, waits for them, and re-layouts, whiten(): planes = jnp.transpose(spectra.reshape(rows, 2, F), (1, 0, 2))  1.82 us
    pallas_call x1, Pallas kernels, tables(): pl.pallas_call(table_kernel, grid_spec=pltpu.PrefetchScalarGridSpec(num_s...  1.33 us
  transfers between devices with their start and end apart: 13, of which 9 were waited for; matrix products, arithmetic and copies ran while one was open for 1% of the time, Pallas kernels for 10%

profile of v10, /device:TPU:0, one launch (start us, length us, event | category | flops | bytes accessed | tf_op | source)
XLA Modules:
  0.0 56.6 jit_solution(5694407989925753122)
XLA Ops:
  0.0 1.8 %copy.11 = bf16[32,2,8192]{2,0,1:T(8,128)(2,1)S(1)} copy(bf16[32,2,8192]{2,1,0:T(2,128)(2,1)} %bitcast.14) | data formatting | bytes 2097152 | tf_op jit(solution)/shard_map/reshape | solution.py:65
  1.8 0.7 %copy-done.1 = s32[1,1,18,2]{2,3,1,0:T(2,128)S(1)} copy-done((s32[1,1,18,2]{2,3,1,0:T(2,128)S(1)}, s32[1,1,18,2]{2,3,1,0:T(2,128)}, u32[]{:S(2)}) %copy-start.1) | copy-done | bytes 168
  3.1 5.1 %collective-permute-start = (bf16[32,2176]{1,0:T(8,128)(2,1)S(1)}, bf16[32,2176]{1,0:T(8,128)(2,1)S(1)}, u32[]{:S(2)}, u32[]{:S(2)}) collective-permute-start(bf16[32,2176]{1,0:T(8,128)(2,1)S(1)} %get-tuple-element.44), channel_id=1, source_target_pairs={{0,3},{1,2},{2,1},{3,0},{4,7},{5,6},{6,5},{7,4},{8,11},{9,10},{10,... | collective-permute-start | bytes 417800 | tf_op jit(solution)/shard_map/ppermute | solution.py:431
  9.4 3.4 %collective-permute-done.refs_0_.refs_6_ = bf16[32,2176]{1,0:T(8,128)(2,1)S(1)} collective-permute-done((bf16[32,2176]{1,0:T(8,128)(2,1)S(1)}, bf16[32,2176]{1,0:T(8,128)(2,1)S(1)}, u32[]{:S(2)}, u32[]{:S(2)}) %collective-permute-start) | collective-permute-done | bytes 139296 | tf_op jit(solution)/shard_map/ppermute | solution.py:431
  12.8 3.2 %collective-permute-done.1.refs_1_.refs_7_ = bf16[32,2176]{1,0:T(8,128)(2,1)S(1)} collective-permute-done((bf16[32,2176]{1,0:T(8,128)(2,1)S(1)}, bf16[32,2176]{1,0:T(8,128)(2,1)S(1)}, u32[]{:S(2)}, u32[]{:S(2)}) %collective-permute-start.1) | collective-permute-done | bytes 139296 | tf_op jit(solution)/shard_map/ppermute | solution.py:431
  16.0 1.8 %collective-permute-start.2 = (bf16[32,2048]{1,0:T(8,128)(2,1)S(1)}, bf16[32,2048]{1,0:T(8,128)(2,1)S(1)}, u32[]{:S(2)}, u32[]{:S(2)}) collective-permute-start(bf16[32,2048]{1,0:T(8,128)(2,1)S(1)} %get-tuple-element.50), channel_id=1, source_target_pairs={{0,3},{1,2},{2,1},{3,0},{4,7},{5,6},{6,5},{7,4},{8,11},{9,10},{10,... | collective-permute-start | bytes 393224 | tf_op jit(solution)/shard_map/ppermute | solution.py:431
  17.8 2.6 %collective-permute-start.4 = (bf16[32,2048]{1,0:T(8,128)(2,1)S(1)}, bf16[32,2048]{1,0:T(8,128)(2,1)S(1)}, u32[]{:S(2)}, u32[]{:S(2)}) collective-permute-start(bf16[32,2048]{1,0:T(8,128)(2,1)S(1)} %get-tuple-element.52), channel_id=1, source_target_pairs={{0,2},{1,3},{2,0},{3,1},{4,6},{5,7},{6,4},{7,5},{8,10},{9,11},{10,... | collective-permute-start | bytes 393224 | tf_op jit(solution)/shard_map/ppermute | solution.py:431
  20.4 1.3 %tables.1.refs_4_ = bf16[2048,1024]{1,0:T(8,128)(2,1)S(1)} custom-call(s32[1]{0:T(128)} %bitcast.2.place_ref.first_ref.place, f32[16,512]{1,0:T(8,128)S(1)} %get-tuple-element.89.hi_cos_ref, f32[16,512]{1,0:T(8,128)S(1)} %get-tuple-element.84.hi_sin_ref, f32[16,512]{1,0:T(8,128)S(1)} %get-tuple-element.90.mid_cos_ref, ...), custom_call_target="tpu_custom_call" | custom-call | flops 8388608 | bytes 4194304 | tf_op jit(solution)/shard_map/tables/pallas_call | solution.py:131
  21.8 1.6 %collective-permute-done.5.refs_2_.refs_6_ = bf16[32,2176]{1,0:T(8,128)(2,1)S(1)} collective-permute-done((bf16[32,2176]{1,0:T(8,128)(2,1)S(1)}, bf16[32,2176]{1,0:T(8,128)(2,1)S(1)}, u32[]{:S(2)}, u32[]{:S(2)}) %collective-permute-start.5) | collective-permute-done | bytes 139296 | tf_op jit(solution)/shard_map/ppermute | solution.py:431
  23.4 1.1 %correlate.4 = (f32[96,1024]{1,0:T(8,128)S(1)}, f32[96,128]{1,0:T(8,128)S(1)}, bf16[192,128]{1,0:T(8,128)(2,1)S(1)}) custom-call(s32[1]{0:T(128)} %bitcast.2.place_ref.first_ref.place, bf16[32,2176]{1,0:T(8,128)(2,1)S(1)} %collective-permute-done.refs_0_.refs_6_, bf16[32,2176]{1,0:T(8,128)(2,1)S(1)} %collective-permute-done.1.refs_1_.refs_7_, ...), custom_call_target="tpu_custom_call" | custom-call | flops 201326592 | bytes 2097152 | tf_op jit(solution)/shard_map/correlate/pallas_call | solution.py:309
  24.5 1.7 %correlate.5 = (f32[224,1024]{1,0:T(8,128)S(1)}, f32[224,128]{1,0:T(8,128)S(1)}, bf16[448,128]{1,0:T(8,128)(2,1)S(1)}) custom-call(s32[1]{0:T(128)} %bitcast.2.place_ref.first_ref.place, bf16[32,2176]{1,0:T(8,128)(2,1)S(1)} %collective-permute-done.refs_0_.refs_6_, bf16[32,2176]{1,0:T(8,128)(2,1)S(1)} %collective-permute-done.1.refs_1_.refs_7_, ...), custom_call_target="tpu_custom_call" | custom-call | flops 469762048 | bytes 2097152 | tf_op jit(solution)/shard_map/correlate/pallas_call | solution.py:309
  26.2 5.0 %collective-permute-done.4.refs_2_ = bf16[32,2048]{1,0:T(8,128)(2,1)S(1)} collective-permute-done((bf16[32,2048]{1,0:T(8,128)(2,1)S(1)}, bf16[32,2048]{1,0:T(8,128)(2,1)S(1)}, u32[]{:S(2)}, u32[]{:S(2)}) %collective-permute-start.4) | collective-permute-done | bytes 131104 | tf_op jit(solution)/shard_map/ppermute | solution.py:431
  31.3 2.0 %correlate.7 = (bf16[72,1024]{1,0:T(8,128)(2,1)S(1)}, bf16[72,1024]{1,0:T(8,128)(2,1)S(1)}, bf16[72,1024]{1,0:T(8,128)(2,1)S(1)}) custom-call(s32[1]{0:T(128)} %bitcast.2.place_ref.first_ref.place, bf16[32,2048]{1,0:T(8,128)(2,1)S(1)} %collective-permute-done.2.refs_0_, bf16[32,2048]{1,0:T(8,128)(2,1)S(1)} %collective-permute-done.3.refs_1_, ...), custom_call_target="tpu_custom_call" | custom-call | flops 469762048 | bytes 2097152 | tf_op jit(solution)/shard_map/correlate/pallas_call | solution.py:309
  33.4 3.0 %collective-permute-start.8 = (bf16[72,1024]{1,0:T(8,128)(2,1)S(1)}, bf16[72,1024]{1,0:T(8,128)(2,1)S(1)}, u32[]{:S(2)}, u32[]{:S(2)}) collective-permute-start(bf16[72,1024]{1,0:T(8,128)(2,1)S(1)} %get-tuple-element.75), channel_id=1, source_target_pairs={{0,1},{1,0},{2,3},{3,2},{4,5},{5,4},{6,7},{7,6},{8,9},{9,8},{10,11... | collective-permute-start | bytes 442376 | tf_op jit(solution)/shard_map/ppermute | solution.py:431
  36.4 1.3 %correlate.6 = bf16[72,1024]{1,0:T(8,128)(2,1)S(1)} custom-call(s32[1]{0:T(128)} %bitcast.2.place_ref.first_ref.place, bf16[32,2048]{1,0:T(8,128)(2,1)S(1)} %collective-permute-done.2.refs_0_, bf16[32,2048]{1,0:T(8,128)(2,1)S(1)} %collective-permute-done.3.refs_1_, bf16[32,2048]{1,0:T(8,128)(2,1)S(1)} %collective-permute-done.4.refs_2_, ...), custom_call_target="tpu_custom_call" | custom-call | flops 201326592 | bytes 2097152 | tf_op jit(solution)/shard_map/correlate/pallas_call | solution.py:309
  37.7 1.4 %collective-permute-start.6 = (bf16[72,1024]{1,0:T(8,128)(2,1)S(1)}, bf16[72,1024]{1,0:T(8,128)(2,1)S(1)}, u32[]{:S(2)}, u32[]{:S(2)}) collective-permute-start(bf16[72,1024]{1,0:T(8,128)(2,1)S(1)} %correlate.6), channel_id=1, source_target_pairs={{0,3},{1,2},{2,1},{3,0},{4,7},{5,6},{6,5},{7,4},{8,11},{9,10},{10,... | collective-permute-start | bytes 442376 | tf_op jit(solution)/shard_map/ppermute | solution.py:431
  39.1 6.5 %collective-permute-done.7.refs_1_ = bf16[72,1024]{1,0:T(8,128)(2,1)S(1)} collective-permute-done((bf16[72,1024]{1,0:T(8,128)(2,1)S(1)}, bf16[72,1024]{1,0:T(8,128)(2,1)S(1)}, u32[]{:S(2)}, u32[]{:S(2)}) %collective-permute-start.7) | collective-permute-done | bytes 147488 | tf_op jit(solution)/shard_map/ppermute | solution.py:431
  46.2 1.3 %collective-permute-done.9.brought_ref = bf16[64,1024]{1,0:T(8,128)(2,1)S(1)} collective-permute-done((bf16[64,1024]{1,0:T(8,128)(2,1)S(1)}, bf16[64,1024]{1,0:T(8,128)(2,1)S(1)}, u32[]{:S(2)}, u32[]{:S(2)}) %collective-permute-start.9) | collective-permute-done | bytes 131104 | tf_op jit(solution)/shard_map/ppermute | solution.py:459
  47.6 1.6 %collective-permute-start.10 = (bf16[32,1024]{1,0:T(8,128)(2,1)S(1)}, bf16[32,1024]{1,0:T(8,128)(2,1)S(1)}, u32[]{:S(2)}, u32[]{:S(2)}) collective-permute-start(bf16[32,1024]{1,0:T(8,128)(2,1)S(1)} %get-tuple-element.80), channel_id=1, source_target_pairs={{0,8},{4,12},{8,0},{12,4},{16,24},{20,28},{24,16},{28,20},{1,9},{5... | collective-permute-start | bytes 196616 | tf_op jit(solution)/shard_map/ppermute | solution.py:459
  49.1 1.5 %collective-permute-start.11 = (bf16[32,1024]{1,0:T(8,128)(2,1)S(1)}, bf16[32,1024]{1,0:T(8,128)(2,1)S(1)}, u32[]{:S(2)}, u32[]{:S(2)}) collective-permute-start(bf16[32,1024]{1,0:T(8,128)(2,1)S(1)} %get-tuple-element.81), channel_id=1, source_target_pairs={{0,16},{4,20},{8,24},{12,28},{16,0},{20,4},{24,8},{28,12},{1,17},{... | collective-permute-start | bytes 196616 | tf_op jit(solution)/shard_map/ppermute | solution.py:459
  51.1 0.8 %collective-permute-done.10.refs_1_ = bf16[32,1024]{1,0:T(8,128)(2,1)S(1)} collective-permute-done((bf16[32,1024]{1,0:T(8,128)(2,1)S(1)}, bf16[32,1024]{1,0:T(8,128)(2,1)S(1)}, u32[]{:S(2)}, u32[]{:S(2)}) %collective-permute-start.10) | collective-permute-done | bytes 65568 | tf_op jit(solution)/shard_map/ppermute | solution.py:459
  51.9 1.5 %collective-permute-done.11.refs_2_ = bf16[32,1024]{1,0:T(8,128)(2,1)S(1)} collective-permute-done((bf16[32,1024]{1,0:T(8,128)(2,1)S(1)}, bf16[32,1024]{1,0:T(8,128)(2,1)S(1)}, u32[]{:S(2)}, u32[]{:S(2)}) %collective-permute-start.11) | collective-permute-done | bytes 65568 | tf_op jit(solution)/shard_map/ppermute | solution.py:459
  53.4 2.4 %collective-permute-done.12.refs_3_ = bf16[32,1024]{1,0:T(8,128)(2,1)S(1)} collective-permute-done((bf16[32,1024]{1,0:T(8,128)(2,1)S(1)}, bf16[32,1024]{1,0:T(8,128)(2,1)S(1)}, u32[]{:S(2)}, u32[]{:S(2)}) %collective-permute-start.12) | collective-permute-done | bytes 65568 | tf_op jit(solution)/shard_map/ppermute | solution.py:459
  55.8 0.8 %widen.1 = f32[24,4,1024]{2,1,0:T(4,128)} custom-call(s32[1]{0:T(128)} %bitcast.mine_ref, bf16[32,1024]{1,0:T(8,128)(2,1)S(1)} %get-tuple-element.79.refs_0_, bf16[32,1024]{1,0:T(8,128)(2,1)S(1)} %collective-permute-done.10.refs_1_, bf16[32,1024]{1,0:T(8,128)(2,1)S(1)} %collective-permute-done.11.refs_2_, bf16[32,1024]{1,0:T(8,128)(2,1)S(1)} %collective-permute-done.12.refs_3_), custom_call_target="tpu_custom_call" | custom-call | tf_op jit(solution)/shard_map/widen/pallas_call | solution.py:410
  (26 shorter events, 3.0 us)
Async XLA Ops:
  0.0 23.4 %copy-start = (f32[2,128]{1,0:T(2,128)S(1)}, f32[2,128]{1,0:T(2,128)}, u32[]{:S(2)}) copy-start(f32[2,128]{1,0:T(2,128)} %constant.36.clone.refs_5_) | copy-start | bytes 3076
  1.8 0.7 %copy-start.1 = (s32[1,1,18,2]{2,3,1,0:T(2,128)S(1)}, s32[1,1,18,2]{2,3,1,0:T(2,128)}, u32[]{:S(2)}) copy-start(s32[1,1,18,2]{2,3,1,0:T(2,128)} %param.8) | copy-start | bytes 436
  3.1 9.7 %collective-permute-start = (bf16[32,2176]{1,0:T(8,128)(2,1)S(1)}, bf16[32,2176]{1,0:T(8,128)(2,1)S(1)}, u32[]{:S(2)}, u32[]{:S(2)}) collective-permute-start(bf16[32,2176]{1,0:T(8,128)(2,1)S(1)} %get-tuple-element.44), channel_id=1, source_target_pairs={{0,3},{1,2},{2,1},{3,0},{4,7},{5,6},{6,5},{7,4},{8,11},{9,10},{10,... | collective-permute-start | bytes 417800 | tf_op jit(solution)/shard_map/ppermute | solution.py:431
  8.2 7.7 %collective-permute-start.1 = (bf16[32,2176]{1,0:T(8,128)(2,1)S(1)}, bf16[32,2176]{1,0:T(8,128)(2,1)S(1)}, u32[]{:S(2)}, u32[]{:S(2)}) collective-permute-start(bf16[32,2176]{1,0:T(8,128)(2,1)S(1)} %get-tuple-element.45), channel_id=1, source_target_pairs={{0,1},{1,0},{2,3},{3,2},{4,5},{5,4},{6,7},{7,6},{8,9},{9,8},{10,11... | collective-permute-start | bytes 417800 | tf_op jit(solution)/shard_map/ppermute | solution.py:431
  8.2 15.1 %collective-permute-start.5 = (bf16[32,2176]{1,0:T(8,128)(2,1)S(1)}, bf16[32,2176]{1,0:T(8,128)(2,1)S(1)}, u32[]{:S(2)}, u32[]{:S(2)}) collective-permute-start(bf16[32,2176]{1,0:T(8,128)(2,1)S(1)} %get-tuple-element.56), channel_id=1, source_target_pairs={{0,2},{1,3},{2,0},{3,1},{4,6},{5,7},{6,4},{7,5},{8,10},{9,11},{10,... | collective-permute-start | bytes 417800 | tf_op jit(solution)/shard_map/ppermute | solution.py:431
  16.0 10.2 %collective-permute-start.2 = (bf16[32,2048]{1,0:T(8,128)(2,1)S(1)}, bf16[32,2048]{1,0:T(8,128)(2,1)S(1)}, u32[]{:S(2)}, u32[]{:S(2)}) collective-permute-start(bf16[32,2048]{1,0:T(8,128)(2,1)S(1)} %get-tuple-element.50), channel_id=1, source_target_pairs={{0,3},{1,2},{2,1},{3,0},{4,7},{5,6},{6,5},{7,4},{8,11},{9,10},{10,... | collective-permute-start | bytes 393224 | tf_op jit(solution)/shard_map/ppermute | solution.py:431
  17.8 8.4 %collective-permute-start.3 = (bf16[32,2048]{1,0:T(8,128)(2,1)S(1)}, bf16[32,2048]{1,0:T(8,128)(2,1)S(1)}, u32[]{:S(2)}, u32[]{:S(2)}) collective-permute-start(bf16[32,2048]{1,0:T(8,128)(2,1)S(1)} %get-tuple-element.51), channel_id=1, source_target_pairs={{0,1},{1,0},{2,3},{3,2},{4,5},{5,4},{6,7},{7,6},{8,9},{9,8},{10,11... | collective-permute-start | bytes 393224 | tf_op jit(solution)/shard_map/ppermute | solution.py:431
  17.8 13.5 %collective-permute-start.4 = (bf16[32,2048]{1,0:T(8,128)(2,1)S(1)}, bf16[32,2048]{1,0:T(8,128)(2,1)S(1)}, u32[]{:S(2)}, u32[]{:S(2)}) collective-permute-start(bf16[32,2048]{1,0:T(8,128)(2,1)S(1)} %get-tuple-element.52), channel_id=1, source_target_pairs={{0,2},{1,3},{2,0},{3,1},{4,6},{5,7},{6,4},{7,5},{8,10},{9,11},{10,... | collective-permute-start | bytes 393224 | tf_op jit(solution)/shard_map/ppermute | solution.py:431
  31.3 14.3 %copy-start.2 = (s32[1,1,18,1]{2,3,1,0:T(1,128)S(1)}, s32[1,1,18,1]{2,3,1,0:T(1,128)}, u32[]{:S(2)}) copy-start(s32[1,1,18,1]{2,3,1,0:T(1,128)} %param.9) | copy-start | bytes 220
  33.3 12.3 %collective-permute-start.7 = (bf16[72,1024]{1,0:T(8,128)(2,1)S(1)}, bf16[72,1024]{1,0:T(8,128)(2,1)S(1)}, u32[]{:S(2)}, u32[]{:S(2)}) collective-permute-start(bf16[72,1024]{1,0:T(8,128)(2,1)S(1)} %get-tuple-element.74), channel_id=1, source_target_pairs={{0,2},{1,3},{2,0},{3,1},{4,6},{5,7},{6,4},{7,5},{8,10},{9,11},{10,... | collective-permute-start | bytes 442376 | tf_op jit(solution)/shard_map/ppermute | solution.py:431
  33.4 12.2 %collective-permute-start.8 = (bf16[72,1024]{1,0:T(8,128)(2,1)S(1)}, bf16[72,1024]{1,0:T(8,128)(2,1)S(1)}, u32[]{:S(2)}, u32[]{:S(2)}) collective-permute-start(bf16[72,1024]{1,0:T(8,128)(2,1)S(1)} %get-tuple-element.75), channel_id=1, source_target_pairs={{0,1},{1,0},{2,3},{3,2},{4,5},{5,4},{6,7},{7,6},{8,9},{9,8},{10,11... | collective-permute-start | bytes 442376 | tf_op jit(solution)/shard_map/ppermute | solution.py:431
  37.7 7.9 %collective-permute-start.6 = (bf16[72,1024]{1,0:T(8,128)(2,1)S(1)}, bf16[72,1024]{1,0:T(8,128)(2,1)S(1)}, u32[]{:S(2)}, u32[]{:S(2)}) collective-permute-start(bf16[72,1024]{1,0:T(8,128)(2,1)S(1)} %correlate.6), channel_id=1, source_target_pairs={{0,3},{1,2},{2,1},{3,0},{4,7},{5,6},{6,5},{7,4},{8,11},{9,10},{10,... | collective-permute-start | bytes 442376 | tf_op jit(solution)/shard_map/ppermute | solution.py:431
  46.1 1.4 %collective-permute-start.9 = (bf16[64,1024]{1,0:T(8,128)(2,1)S(1)}, bf16[64,1024]{1,0:T(8,128)(2,1)S(1)}, u32[]{:S(2)}, u32[]{:S(2)}) collective-permute-start(bf16[64,1024]{1,0:T(8,128)(2,1)S(1)} %get-tuple-element.78), channel_id=1, source_target_pairs={{0,4},{4,0},{8,12},{12,8},{16,20},{20,16},{24,28},{28,24},{1,5},{5... | collective-permute-start | bytes 393224 | tf_op jit(solution)/shard_map/ppermute | solution.py:459
  47.6 4.3 %collective-permute-start.10 = (bf16[32,1024]{1,0:T(8,128)(2,1)S(1)}, bf16[32,1024]{1,0:T(8,128)(2,1)S(1)}, u32[]{:S(2)}, u32[]{:S(2)}) collective-permute-start(bf16[32,1024]{1,0:T(8,128)(2,1)S(1)} %get-tuple-element.80), channel_id=1, source_target_pairs={{0,8},{4,12},{8,0},{12,4},{16,24},{20,28},{24,16},{28,20},{1,9},{5... | collective-permute-start | bytes 196616 | tf_op jit(solution)/shard_map/ppermute | solution.py:459
  49.1 4.3 %collective-permute-start.11 = (bf16[32,1024]{1,0:T(8,128)(2,1)S(1)}, bf16[32,1024]{1,0:T(8,128)(2,1)S(1)}, u32[]{:S(2)}, u32[]{:S(2)}) collective-permute-start(bf16[32,1024]{1,0:T(8,128)(2,1)S(1)} %get-tuple-element.81), channel_id=1, source_target_pairs={{0,16},{4,20},{8,24},{12,28},{16,0},{20,4},{24,8},{28,12},{1,17},{... | collective-permute-start | bytes 196616 | tf_op jit(solution)/shard_map/ppermute | solution.py:459
  50.6 5.2 %collective-permute-start.12 = (bf16[32,1024]{1,0:T(8,128)(2,1)S(1)}, bf16[32,1024]{1,0:T(8,128)(2,1)S(1)}, u32[]{:S(2)}, u32[]{:S(2)}) collective-permute-start(bf16[32,1024]{1,0:T(8,128)(2,1)S(1)} %get-tuple-element.82), channel_id=1, source_target_pairs={{0,24},{4,28},{8,16},{12,20},{16,8},{20,12},{24,0},{28,4},{1,25},{... | collective-permute-start | bytes 196616 | tf_op jit(solution)/shard_map/ppermute | solution.py:459

commit v11 on v10

--- a/solution.py
+++ b/solution.py
@@ -437,7 +437,7 @@
     first, second = whiten(spectra, pair_blocks[0, 0].T, place, parts)
     first = exchange(first)
     table = tables(place, chunks)
-    gates = [d for d in sequence(parts)[:2] if d]
+    gates = sequence(parts)[:1]
     here, second = lax.optimization_barrier(([first[d] for d in gates], second))
     for d, panel in zip(gates, here):
         first[d] = panel

time: 57.2 us -> 57.2 us (level)
  starting transfers between devices: 18.3 us -> 19 us
  waiting for transfers between devices: 25.8 us -> 25.1 us
    ppermute x9, starting transfers between devices: 14.7 us -> 15.4 us  [swap(): return lax.ppermute(array, 'chan', [(i, i ^ d) for i in range(parts)])]
    ppermute x9, waiting for transfers between devices: 19.8 us -> 19.1 us  [swap(): return lax.ppermute(array, 'chan', [(i, i ^ d) for i in range(parts)])]
  transfers between devices with their start and end apart: 13 -> 13, of which waited for: 9 -> 8; matrix products, arithmetic and copies ran while one was open for 1% -> 1% of each run, Pallas kernels for 10% -> 10%
where the time goes in v11:
time: 57.2 us; the launch traced here: 56.6 us
  waiting for transfers between devices  25.1 us (44%)
  starting transfers between devices  19 us (33%)
  Pallas kernels  9.36 us (16%)
  local copies, waits for them, and re-layouts  2.51 us (4%)
    ppermute x9, waiting for transfers between devices, swap(): return lax.ppermute(array, 'chan', [(i, i ^ d) for i in range(parts)])  19.1 us
    ppermute x9, starting transfers between devices, swap(): return lax.ppermute(array, 'chan', [(i, i ^ d) for i in range(parts)])  15.4 us
    pallas_call x4, Pallas kernels, correlate(): pl.pallas_call(functools.partial(corr_kernel, per_step, parts, lists, wav...  6.1 us
    ppermute x4, waiting for transfers between devices, trade(): return lax.ppermute(array, 'grp', [(i, i ^ m) for i in range(groups)])  6.03 us
    ppermute x4, starting transfers between devices, trade(): return lax.ppermute(array, 'grp', [(i, i ^ m) for i in range(groups)])  3.62 us
    reshape x1, local copies, waits for them, and re-layouts, whiten(): planes = jnp.transpose(spectra.reshape(rows, 2, F), (1, 0, 2))  1.82 us
    pallas_call x1, Pallas kernels, tables(): pl.pallas_call(table_kernel, grid_spec=pltpu.PrefetchScalarGridSpec(num_s...  1.33 us
  transfers between devices with their start and end apart: 13, of which 8 were waited for; matrix products, arithmetic and copies ran while one was open for 1% of the time, Pallas kernels for 10%

profile of v11, /device:TPU:0, one launch (start us, length us, event | category | flops | bytes accessed | tf_op | source)
XLA Modules:
  0.0 56.6 jit_solution(1985063117879741758)
XLA Ops:
  0.0 1.8 %copy.11 = bf16[32,2,8192]{2,0,1:T(8,128)(2,1)S(1)} copy(bf16[32,2,8192]{2,1,0:T(2,128)(2,1)} %bitcast.14) | data formatting | bytes 2097152 | tf_op jit(solution)/shard_map/reshape | solution.py:65
  1.8 0.7 %copy-done.1 = s32[1,1,18,2]{2,3,1,0:T(2,128)S(1)} copy-done((s32[1,1,18,2]{2,3,1,0:T(2,128)S(1)}, s32[1,1,18,2]{2,3,1,0:T(2,128)}, u32[]{:S(2)}) %copy-start.1) | copy-done | bytes 168
  3.1 5.1 %collective-permute-start = (bf16[32,2176]{1,0:T(8,128)(2,1)S(1)}, bf16[32,2176]{1,0:T(8,128)(2,1)S(1)}, u32[]{:S(2)}, u32[]{:S(2)}) collective-permute-start(bf16[32,2176]{1,0:T(8,128)(2,1)S(1)} %get-tuple-element.43), channel_id=1, source_target_pairs={{0,3},{1,2},{2,1},{3,0},{4,7},{5,6},{6,5},{7,4},{8,11},{9,10},{10,... | collective-permute-start | bytes 417800 | tf_op jit(solution)/shard_map/ppermute | solution.py:431
  8.2 0.6 %collective-permute-start.5 = (bf16[32,2176]{1,0:T(8,128)(2,1)S(1)}, bf16[32,2176]{1,0:T(8,128)(2,1)S(1)}, u32[]{:S(2)}, u32[]{:S(2)}) collective-permute-start(bf16[32,2176]{1,0:T(8,128)(2,1)S(1)} %get-tuple-element.54), channel_id=1, source_target_pairs={{0,2},{1,3},{2,0},{3,1},{4,6},{5,7},{6,4},{7,5},{8,10},{9,11},{10,... | collective-permute-start | bytes 417800 | tf_op jit(solution)/shard_map/ppermute | solution.py:431
  9.4 3.4 %collective-permute-done.refs_0_.refs_6_ = bf16[32,2176]{1,0:T(8,128)(2,1)S(1)} collective-permute-done((bf16[32,2176]{1,0:T(8,128)(2,1)S(1)}, bf16[32,2176]{1,0:T(8,128)(2,1)S(1)}, u32[]{:S(2)}, u32[]{:S(2)}) %collective-permute-start) | collective-permute-done | bytes 139296 | tf_op jit(solution)/shard_map/ppermute | solution.py:431
  12.8 3.8 %collective-permute-start.1 = (bf16[32,2048]{1,0:T(8,128)(2,1)S(1)}, bf16[32,2048]{1,0:T(8,128)(2,1)S(1)}, u32[]{:S(2)}, u32[]{:S(2)}) collective-permute-start(bf16[32,2048]{1,0:T(8,128)(2,1)S(1)} %get-tuple-element.48), channel_id=1, source_target_pairs={{0,3},{1,2},{2,1},{3,0},{4,7},{5,6},{6,5},{7,4},{8,11},{9,10},{10,... | collective-permute-start | bytes 393224 | tf_op jit(solution)/shard_map/ppermute | solution.py:431
  16.6 0.7 %collective-permute-start.2 = (bf16[32,2048]{1,0:T(8,128)(2,1)S(1)}, bf16[32,2048]{1,0:T(8,128)(2,1)S(1)}, u32[]{:S(2)}, u32[]{:S(2)}) collective-permute-start(bf16[32,2048]{1,0:T(8,128)(2,1)S(1)} %get-tuple-element.49), channel_id=1, source_target_pairs={{0,1},{1,0},{2,3},{3,2},{4,5},{5,4},{6,7},{7,6},{8,9},{9,8},{10,11... | collective-permute-start | bytes 393224 | tf_op jit(solution)/shard_map/ppermute | solution.py:431
  17.9 1.3 %tables.1.refs_4_ = bf16[2048,1024]{1,0:T(8,128)(2,1)S(1)} custom-call(s32[1]{0:T(128)} %bitcast.2.place_ref.first_ref.place, f32[16,512]{1,0:T(8,128)S(1)} %get-tuple-element.87.hi_cos_ref, f32[16,512]{1,0:T(8,128)S(1)} %get-tuple-element.82.hi_sin_ref, f32[16,512]{1,0:T(8,128)S(1)} %get-tuple-element.88.mid_cos_ref, ...), custom_call_target="tpu_custom_call" | custom-call | flops 8388608 | bytes 4194304 | tf_op jit(solution)/shard_map/tables/pallas_call | solution.py:131
  19.3 7.4 %collective-permute-done.5.refs_2_.refs_6_ = bf16[32,2176]{1,0:T(8,128)(2,1)S(1)} collective-permute-done((bf16[32,2176]{1,0:T(8,128)(2,1)S(1)}, bf16[32,2176]{1,0:T(8,128)(2,1)S(1)}, u32[]{:S(2)}, u32[]{:S(2)}) %collective-permute-start.5) | collective-permute-done | bytes 139296 | tf_op jit(solution)/shard_map/ppermute | solution.py:431
  26.6 1.1 %correlate.4 = (f32[96,1024]{1,0:T(8,128)S(1)}, f32[96,128]{1,0:T(8,128)S(1)}, bf16[192,128]{1,0:T(8,128)(2,1)S(1)}) custom-call(s32[1]{0:T(128)} %bitcast.2.place_ref.first_ref.place, bf16[32,2176]{1,0:T(8,128)(2,1)S(1)} %collective-permute-done.refs_0_.refs_6_, bf16[32,2176]{1,0:T(8,128)(2,1)S(1)} %collective-permute-done.4.refs_1_.refs_7_, ...), custom_call_target="tpu_custom_call" | custom-call | flops 201326592 | bytes 2097152 | tf_op jit(solution)/shard_map/correlate/pallas_call | solution.py:309
  27.7 1.7 %correlate.5 = (f32[224,1024]{1,0:T(8,128)S(1)}, f32[224,128]{1,0:T(8,128)S(1)}, bf16[448,128]{1,0:T(8,128)(2,1)S(1)}) custom-call(s32[1]{0:T(128)} %bitcast.2.place_ref.first_ref.place, bf16[32,2176]{1,0:T(8,128)(2,1)S(1)} %collective-permute-done.refs_0_.refs_6_, bf16[32,2176]{1,0:T(8,128)(2,1)S(1)} %collective-permute-done.4.refs_1_.refs_7_, ...), custom_call_target="tpu_custom_call" | custom-call | flops 469762048 | bytes 2097152 | tf_op jit(solution)/shard_map/correlate/pallas_call | solution.py:309
  29.5 1.8 %collective-permute-done.3.refs_2_ = bf16[32,2048]{1,0:T(8,128)(2,1)S(1)} collective-permute-done((bf16[32,2048]{1,0:T(8,128)(2,1)S(1)}, bf16[32,2048]{1,0:T(8,128)(2,1)S(1)}, u32[]{:S(2)}, u32[]{:S(2)}) %collective-permute-start.3) | collective-permute-done | bytes 131104 | tf_op jit(solution)/shard_map/ppermute | solution.py:431
  31.3 2.0 %correlate.7 = (bf16[72,1024]{1,0:T(8,128)(2,1)S(1)}, bf16[72,1024]{1,0:T(8,128)(2,1)S(1)}, bf16[72,1024]{1,0:T(8,128)(2,1)S(1)}) custom-call(s32[1]{0:T(128)} %bitcast.2.place_ref.first_ref.place, bf16[32,2048]{1,0:T(8,128)(2,1)S(1)} %collective-permute-done.1.refs_0_, bf16[32,2048]{1,0:T(8,128)(2,1)S(1)} %collective-permute-done.2.refs_1_, ...), custom_call_target="tpu_custom_call" | custom-call | flops 469762048 | bytes 2097152 | tf_op jit(solution)/shard_map/correlate/pallas_call | solution.py:309
  33.4 3.0 %collective-permute-start.8 = (bf16[72,1024]{1,0:T(8,128)(2,1)S(1)}, bf16[72,1024]{1,0:T(8,128)(2,1)S(1)}, u32[]{:S(2)}, u32[]{:S(2)}) collective-permute-start(bf16[72,1024]{1,0:T(8,128)(2,1)S(1)} %get-tuple-element.73), channel_id=1, source_target_pairs={{0,1},{1,0},{2,3},{3,2},{4,5},{5,4},{6,7},{7,6},{8,9},{9,8},{10,11... | collective-permute-start | bytes 442376 | tf_op jit(solution)/shard_map/ppermute | solution.py:431
  36.4 1.3 %correlate.6 = bf16[72,1024]{1,0:T(8,128)(2,1)S(1)} custom-call(s32[1]{0:T(128)} %bitcast.2.place_ref.first_ref.place, bf16[32,2048]{1,0:T(8,128)(2,1)S(1)} %collective-permute-done.1.refs_0_, bf16[32,2048]{1,0:T(8,128)(2,1)S(1)} %collective-permute-done.2.refs_1_, bf16[32,2048]{1,0:T(8,128)(2,1)S(1)} %collective-permute-done.3.refs_2_, ...), custom_call_target="tpu_custom_call" | custom-call | flops 201326592 | bytes 2097152 | tf_op jit(solution)/shard_map/correlate/pallas_call | solution.py:309
  37.7 1.5 %collective-permute-start.6 = (bf16[72,1024]{1,0:T(8,128)(2,1)S(1)}, bf16[72,1024]{1,0:T(8,128)(2,1)S(1)}, u32[]{:S(2)}, u32[]{:S(2)}) collective-permute-start(bf16[72,1024]{1,0:T(8,128)(2,1)S(1)} %correlate.6), channel_id=1, source_target_pairs={{0,3},{1,2},{2,1},{3,0},{4,7},{5,6},{6,5},{7,4},{8,11},{9,10},{10,... | collective-permute-start | bytes 442376 | tf_op jit(solution)/shard_map/ppermute | solution.py:431
  39.1 6.5 %collective-permute-done.7.refs_1_ = bf16[72,1024]{1,0:T(8,128)(2,1)S(1)} collective-permute-done((bf16[72,1024]{1,0:T(8,128)(2,1)S(1)}, bf16[72,1024]{1,0:T(8,128)(2,1)S(1)}, u32[]{:S(2)}, u32[]{:S(2)}) %collective-permute-start.7) | collective-permute-done | bytes 147488 | tf_op jit(solution)/shard_map/ppermute | solution.py:431
  46.2 1.3 %collective-permute-done.9.brought_ref = bf16[64,1024]{1,0:T(8,128)(2,1)S(1)} collective-permute-done((bf16[64,1024]{1,0:T(8,128)(2,1)S(1)}, bf16[64,1024]{1,0:T(8,128)(2,1)S(1)}, u32[]{:S(2)}, u32[]{:S(2)}) %collective-permute-start.9) | collective-permute-done | bytes 131104 | tf_op jit(solution)/shard_map/ppermute | solution.py:459
  47.6 1.6 %collective-permute-start.10 = (bf16[32,1024]{1,0:T(8,128)(2,1)S(1)}, bf16[32,1024]{1,0:T(8,128)(2,1)S(1)}, u32[]{:S(2)}, u32[]{:S(2)}) collective-permute-start(bf16[32,1024]{1,0:T(8,128)(2,1)S(1)} %get-tuple-element.78), channel_id=1, source_target_pairs={{0,8},{4,12},{8,0},{12,4},{16,24},{20,28},{24,16},{28,20},{1,9},{5... | collective-permute-start | bytes 196616 | tf_op jit(solution)/shard_map/ppermute | solution.py:459
  49.1 1.5 %collective-permute-start.11 = (bf16[32,1024]{1,0:T(8,128)(2,1)S(1)}, bf16[32,1024]{1,0:T(8,128)(2,1)S(1)}, u32[]{:S(2)}, u32[]{:S(2)}) collective-permute-start(bf16[32,1024]{1,0:T(8,128)(2,1)S(1)} %get-tuple-element.79), channel_id=1, source_target_pairs={{0,16},{4,20},{8,24},{12,28},{16,0},{20,4},{24,8},{28,12},{1,17},{... | collective-permute-start | bytes 196616 | tf_op jit(solution)/shard_map/ppermute | solution.py:459
  51.1 0.8 %collective-permute-done.10.refs_1_ = bf16[32,1024]{1,0:T(8,128)(2,1)S(1)} collective-permute-done((bf16[32,1024]{1,0:T(8,128)(2,1)S(1)}, bf16[32,1024]{1,0:T(8,128)(2,1)S(1)}, u32[]{:S(2)}, u32[]{:S(2)}) %collective-permute-start.10) | collective-permute-done | bytes 65568 | tf_op jit(solution)/shard_map/ppermute | solution.py:459
  51.9 1.5 %collective-permute-done.11.refs_2_ = bf16[32,1024]{1,0:T(8,128)(2,1)S(1)} collective-permute-done((bf16[32,1024]{1,0:T(8,128)(2,1)S(1)}, bf16[32,1024]{1,0:T(8,128)(2,1)S(1)}, u32[]{:S(2)}, u32[]{:S(2)}) %collective-permute-start.11) | collective-permute-done | bytes 65568 | tf_op jit(solution)/shard_map/ppermute | solution.py:459
  53.4 2.4 %collective-permute-done.12.refs_3_ = bf16[32,1024]{1,0:T(8,128)(2,1)S(1)} collective-permute-done((bf16[32,1024]{1,0:T(8,128)(2,1)S(1)}, bf16[32,1024]{1,0:T(8,128)(2,1)S(1)}, u32[]{:S(2)}, u32[]{:S(2)}) %collective-permute-start.12) | collective-permute-done | bytes 65568 | tf_op jit(solution)/shard_map/ppermute | solution.py:459
  55.8 0.8 %widen.1 = f32[24,4,1024]{2,1,0:T(4,128)} custom-call(s32[1]{0:T(128)} %bitcast.mine_ref, bf16[32,1024]{1,0:T(8,128)(2,1)S(1)} %get-tuple-element.77.refs_0_, bf16[32,1024]{1,0:T(8,128)(2,1)S(1)} %collective-permute-done.10.refs_1_, bf16[32,1024]{1,0:T(8,128)(2,1)S(1)} %collective-permute-done.11.refs_2_, bf16[32,1024]{1,0:T(8,128)(2,1)S(1)} %collective-permute-done.12.refs_3_), custom_call_target="tpu_custom_call" | custom-call | tf_op jit(solution)/shard_map/widen/pallas_call | solution.py:410
  (26 shorter events, 2.9 us)
Async XLA Ops:
  0.0 26.6 %copy-start = (f32[2,128]{1,0:T(2,128)S(1)}, f32[2,128]{1,0:T(2,128)}, u32[]{:S(2)}) copy-start(f32[2,128]{1,0:T(2,128)} %constant.36.clone.refs_5_) | copy-start | bytes 3076
  1.8 0.7 %copy-start.1 = (s32[1,1,18,2]{2,3,1,0:T(2,128)S(1)}, s32[1,1,18,2]{2,3,1,0:T(2,128)}, u32[]{:S(2)}) copy-start(s32[1,1,18,2]{2,3,1,0:T(2,128)} %param.8) | copy-start | bytes 436
  3.1 9.7 %collective-permute-start = (bf16[32,2176]{1,0:T(8,128)(2,1)S(1)}, bf16[32,2176]{1,0:T(8,128)(2,1)S(1)}, u32[]{:S(2)}, u32[]{:S(2)}) collective-permute-start(bf16[32,2176]{1,0:T(8,128)(2,1)S(1)} %get-tuple-element.43), channel_id=1, source_target_pairs={{0,3},{1,2},{2,1},{3,0},{4,7},{5,6},{6,5},{7,4},{8,11},{9,10},{10,... | collective-permute-start | bytes 417800 | tf_op jit(solution)/shard_map/ppermute | solution.py:431
  8.2 11.0 %collective-permute-start.4 = (bf16[32,2176]{1,0:T(8,128)(2,1)S(1)}, bf16[32,2176]{1,0:T(8,128)(2,1)S(1)}, u32[]{:S(2)}, u32[]{:S(2)}) collective-permute-start(bf16[32,2176]{1,0:T(8,128)(2,1)S(1)} %get-tuple-element.53), channel_id=1, source_target_pairs={{0,1},{1,0},{2,3},{3,2},{4,5},{5,4},{6,7},{7,6},{8,9},{9,8},{10,11... | collective-permute-start | bytes 417800 | tf_op jit(solution)/shard_map/ppermute | solution.py:431
  8.2 18.4 %collective-permute-start.5 = (bf16[32,2176]{1,0:T(8,128)(2,1)S(1)}, bf16[32,2176]{1,0:T(8,128)(2,1)S(1)}, u32[]{:S(2)}, u32[]{:S(2)}) collective-permute-start(bf16[32,2176]{1,0:T(8,128)(2,1)S(1)} %get-tuple-element.54), channel_id=1, source_target_pairs={{0,2},{1,3},{2,0},{3,1},{4,6},{5,7},{6,4},{7,5},{8,10},{9,11},{10,... | collective-permute-start | bytes 417800 | tf_op jit(solution)/shard_map/ppermute | solution.py:431
  12.8 16.7 %collective-permute-start.1 = (bf16[32,2048]{1,0:T(8,128)(2,1)S(1)}, bf16[32,2048]{1,0:T(8,128)(2,1)S(1)}, u32[]{:S(2)}, u32[]{:S(2)}) collective-permute-start(bf16[32,2048]{1,0:T(8,128)(2,1)S(1)} %get-tuple-element.48), channel_id=1, source_target_pairs={{0,3},{1,2},{2,1},{3,0},{4,7},{5,6},{6,5},{7,4},{8,11},{9,10},{10,... | collective-permute-start | bytes 393224 | tf_op jit(solution)/shard_map/ppermute | solution.py:431
  16.6 12.9 %collective-permute-start.2 = (bf16[32,2048]{1,0:T(8,128)(2,1)S(1)}, bf16[32,2048]{1,0:T(8,128)(2,1)S(1)}, u32[]{:S(2)}, u32[]{:S(2)}) collective-permute-start(bf16[32,2048]{1,0:T(8,128)(2,1)S(1)} %get-tuple-element.49), channel_id=1, source_target_pairs={{0,1},{1,0},{2,3},{3,2},{4,5},{5,4},{6,7},{7,6},{8,9},{9,8},{10,11... | collective-permute-start | bytes 393224 | tf_op jit(solution)/shard_map/ppermute | solution.py:431
  17.3 14.0 %collective-permute-start.3 = (bf16[32,2048]{1,0:T(8,128)(2,1)S(1)}, bf16[32,2048]{1,0:T(8,128)(2,1)S(1)}, u32[]{:S(2)}, u32[]{:S(2)}) collective-permute-start(bf16[32,2048]{1,0:T(8,128)(2,1)S(1)} %get-tuple-element.50), channel_id=1, source_target_pairs={{0,2},{1,3},{2,0},{3,1},{4,6},{5,7},{6,4},{7,5},{8,10},{9,11},{10,... | collective-permute-start | bytes 393224 | tf_op jit(solution)/shard_map/ppermute | solution.py:431
  31.3 14.3 %copy-start.2 = (s32[1,1,18,1]{2,3,1,0:T(1,128)S(1)}, s32[1,1,18,1]{2,3,1,0:T(1,128)}, u32[]{:S(2)}) copy-start(s32[1,1,18,1]{2,3,1,0:T(1,128)} %param.9) | copy-start | bytes 220
  33.3 12.3 %collective-permute-start.7 = (bf16[72,1024]{1,0:T(8,128)(2,1)S(1)}, bf16[72,1024]{1,0:T(8,128)(2,1)S(1)}, u32[]{:S(2)}, u32[]{:S(2)}) collective-permute-start(bf16[72,1024]{1,0:T(8,128)(2,1)S(1)} %get-tuple-element.72), channel_id=1, source_target_pairs={{0,2},{1,3},{2,0},{3,1},{4,6},{5,7},{6,4},{7,5},{8,10},{9,11},{10,... | collective-permute-start | bytes 442376 | tf_op jit(solution)/shard_map/ppermute | solution.py:431
  33.4 12.2 %collective-permute-start.8 = (bf16[72,1024]{1,0:T(8,128)(2,1)S(1)}, bf16[72,1024]{1,0:T(8,128)(2,1)S(1)}, u32[]{:S(2)}, u32[]{:S(2)}) collective-permute-start(bf16[72,1024]{1,0:T(8,128)(2,1)S(1)} %get-tuple-element.73), channel_id=1, source_target_pairs={{0,1},{1,0},{2,3},{3,2},{4,5},{5,4},{6,7},{7,6},{8,9},{9,8},{10,11... | collective-permute-start | bytes 442376 | tf_op jit(solution)/shard_map/ppermute | solution.py:431
  37.7 7.9 %collective-permute-start.6 = (bf16[72,1024]{1,0:T(8,128)(2,1)S(1)}, bf16[72,1024]{1,0:T(8,128)(2,1)S(1)}, u32[]{:S(2)}, u32[]{:S(2)}) collective-permute-start(bf16[72,1024]{1,0:T(8,128)(2,1)S(1)} %correlate.6), channel_id=1, source_target_pairs={{0,3},{1,2},{2,1},{3,0},{4,7},{5,6},{6,5},{7,4},{8,11},{9,10},{10,... | collective-permute-start | bytes 442376 | tf_op jit(solution)/shard_map/ppermute | solution.py:431
  46.1 1.4 %collective-permute-start.9 = (bf16[64,1024]{1,0:T(8,128)(2,1)S(1)}, bf16[64,1024]{1,0:T(8,128)(2,1)S(1)}, u32[]{:S(2)}, u32[]{:S(2)}) collective-permute-start(bf16[64,1024]{1,0:T(8,128)(2,1)S(1)} %get-tuple-element.76), channel_id=1, source_target_pairs={{0,4},{4,0},{8,12},{12,8},{16,20},{20,16},{24,28},{28,24},{1,5},{5... | collective-permute-start | bytes 393224 | tf_op jit(solution)/shard_map/ppermute | solution.py:459
  47.6 4.3 %collective-permute-start.10 = (bf16[32,1024]{1,0:T(8,128)(2,1)S(1)}, bf16[32,1024]{1,0:T(8,128)(2,1)S(1)}, u32[]{:S(2)}, u32[]{:S(2)}) collective-permute-start(bf16[32,1024]{1,0:T(8,128)(2,1)S(1)} %get-tuple-element.78), channel_id=1, source_target_pairs={{0,8},{4,12},{8,0},{12,4},{16,24},{20,28},{24,16},{28,20},{1,9},{5... | collective-permute-start | bytes 196616 | tf_op jit(solution)/shard_map/ppermute | solution.py:459
  49.1 4.3 %collective-permute-start.11 = (bf16[32,1024]{1,0:T(8,128)(2,1)S(1)}, bf16[32,1024]{1,0:T(8,128)(2,1)S(1)}, u32[]{:S(2)}, u32[]{:S(2)}) collective-permute-start(bf16[32,1024]{1,0:T(8,128)(2,1)S(1)} %get-tuple-element.79), channel_id=1, source_target_pairs={{0,16},{4,20},{8,24},{12,28},{16,0},{20,4},{24,8},{28,12},{1,17},{... | collective-permute-start | bytes 196616 | tf_op jit(solution)/shard_map/ppermute | solution.py:459
  50.7 5.2 %collective-permute-start.12 = (bf16[32,1024]{1,0:T(8,128)(2,1)S(1)}, bf16[32,1024]{1,0:T(8,128)(2,1)S(1)}, u32[]{:S(2)}, u32[]{:S(2)}) collective-permute-start(bf16[32,1024]{1,0:T(8,128)(2,1)S(1)} %get-tuple-element.80), channel_id=1, source_target_pairs={{0,24},{4,28},{8,16},{12,20},{16,8},{20,12},{24,0},{28,4},{1,25},{... | collective-permute-start | bytes 196616 | tf_op jit(solution)/shard_map/ppermute | solution.py:459
